TPU v7x, 256 devices: a whole 4x4x8 slice. The times are simulated.
256 devices in a mesh: ctx: 64 (over x, z, core), ch: 4 (over y).
Axes of the slice: x: 4, y: 4, z: 8, core: 2. Of those that a mesh axis runs over, the one named last changes fastest.
Arguments:
- query_proj: bfloat16 [16384, 8192], P('ctx', 'ch'), may hold values from -6 to 6
- key_proj: bfloat16 [16384, 8192], P('ctx', 'ch'), may hold values from -6 to 6
- value_proj: bfloat16 [16384, 8192], P('ctx', 'ch'), may hold values from -6 to 6
- short_filter: float32 [3, 3, 8192], P(None, None, 'ch'), may hold values from -3 to 3
- decay_rate: float32 [16, 8192], P(None, 'ch'), may hold values from 6.1035156e-05 to 0.05
- residue: float32 [16, 8192], P(None, 'ch'), may hold values from -5 to 5
- skip_gain: float32 [8192], P('ch'), may hold values from -4 to 4
- norm_gain: float32 [8192], P('ch'), may hold values from 0.5 to 1.5
- residual: bfloat16 [16384, 8192], P('ctx', 'ch'), may hold values from -6 to 6
- lengths: int32 [4], replicated, may hold values from 1 to 8192, as said below
Outputs:
- stream: float32 [16384, 8192], P('ctx', 'ch')
- normed: float32 [16384, 8192], P('ctx', 'ch')
Inputs may be any that keep to these rules, and one draw needn't show every extreme that they name: 4 segment lengths summing to 16384; the second segment is the longest, exactly 8192, and starts after position 2048 and at or before 16384 // 4.
All inputs are finite; a program needn't handle non-finite values.
Results may differ from a plain program's by a relative error of at most 0.0003.
Values may be sent and summed in bfloat16 or wider, within the bound.
No kernel may reach another device: no remote copies, remote signals or barrier semaphores. Data moves between devices by JAX's collectives and lax.ppermute only.
A program may use at most 128 MiB of HBM per device.

v0:
```python
import jax
import jax.numpy as jnp
from jax import lax
from jax.sharding import PartitionSpec as P


def passed_along(block, axis, distance):
    devices = range(lax.axis_size(axis))
    route = [(i - distance, i) for i in devices if i - distance in devices]
    return lax.ppermute(block, axis, route)


def carried_in(value, axis, join, neutral):
    count, mine = (lax.axis_size(axis), lax.axis_index(axis))
    pieces = jax.tree.map(lambda part: lax.all_gather(part, axis), value)
    running = jax.tree.map(
        lambda part, zero: jnp.full_like(part, 0) + jnp.asarray(zero, part.dtype), value, neutral
    )

    def step(position, running):
        longer = join(running, jax.tree.map(lambda part: part[position], pieces))
        return jax.tree.map(lambda new, old: jnp.where(position < mine, new, old), longer, running)

    return lax.fori_loop(0, count - 1, step, running)


def combine_pair(earlier, later):
    return (earlier[0] * later[0], earlier[1] * later[0] + later[1])


def short_pass(signal, before, taps, same_one, same_two):
    extended = jnp.concatenate([before, signal], axis=0).astype(jnp.float32)
    return (
        taps[0] * extended[2:]
        + taps[1] * extended[1:-1] * same_one[:, None]
        + taps[2] * extended[:-2] * same_two[:, None]
    )


def on_device(
    query_proj,
    key_proj,
    value_proj,
    short_filter,
    decay_rate,
    residue,
    skip_gain,
    norm_gain,
    residual,
    lengths,
):
    rows_here, width_here = query_proj.shape
    pole_count = decay_rate.shape[0]
    device_rank = lax.axis_index("ctx")
    starts_at = jnp.cumsum(lengths) - lengths
    positions = device_rank * rows_here + jnp.arange(rows_here + 2, dtype=jnp.int32) - 2
    segment_of = jnp.sum((positions[:, None] >= starts_at[None, :]).astype(jnp.int32), axis=1) - 1
    resets = jnp.any(positions[2:, None] == starts_at[None, :], axis=1)
    keep_mask = 1.0 - resets.astype(jnp.float32)
    same_one = (segment_of[2:] == segment_of[1:-1]).astype(jnp.float32)
    same_two = (segment_of[2:] == segment_of[:-2]).astype(jnp.float32)
    rims = jnp.stack([query_proj[-2:], key_proj[-2:], value_proj[-2:]])
    prev_rims = passed_along(rims, "ctx", 1)
    query_short = short_pass(query_proj, prev_rims[0], short_filter[0], same_one, same_two)
    key_short = short_pass(key_proj, prev_rims[1], short_filter[1], same_one, same_two)
    value_short = short_pass(value_proj, prev_rims[2], short_filter[2], same_one, same_two)
    gated = key_short * value_short
    decay = jnp.exp(-decay_rate)
    pole_gain = residue * jnp.sqrt(-jnp.expm1(-2.0 * decay_rate))
    blocks = rows_here // 16
    inputs = gated.reshape(blocks, 16, width_here)
    keeps = keep_mask.reshape(blocks, 16)
    alive = jnp.cumprod(keeps, axis=1)
    states = jnp.zeros((blocks, pole_count, width_here), jnp.float32)
    partial_out = []
    for offset in range(16):
        states = (
            keeps[:, offset][:, None, None] * decay[None] * states + inputs[:, offset][:, None, :]
        )
        partial_out.append(jnp.sum(pole_gain[None] * states, axis=1))
    block_decay = alive[:, 15][:, None, None] * jnp.exp(-16.0 * decay_rate)[None]
    through_decay, through_state = lax.associative_scan(combine_pair, (block_decay, states), axis=0)
    end_decay = through_decay[-1]
    end_state = through_state[-1]
    identity = (jnp.ones_like(end_decay), jnp.zeros_like(end_state))
    incoming = carried_in((end_decay, end_state), "ctx", combine_pair, identity)[1]
    zero_block = jnp.zeros((1, pole_count, width_here), jnp.float32)
    unit_block = jnp.ones((1, pole_count, width_here), jnp.float32)
    entry_state = jnp.concatenate([zero_block, through_state[:-1]], axis=0)
    entry_state = (
        entry_state + jnp.concatenate([unit_block, through_decay[:-1]], axis=0) * incoming[None]
    )
    long_rows = []
    for offset in range(16):
        weights = pole_gain * jnp.exp(-(offset + 1.0) * decay_rate)
        carried = jnp.sum(weights[None] * entry_state, axis=1)
        long_rows.append(partial_out[offset] + alive[:, offset][:, None] * carried)
    long_out = jnp.stack(long_rows, axis=1).reshape(rows_here, width_here)
    stream = residual.astype(jnp.float32) + query_short * (long_out + skip_gain * gated)
    power = lax.psum(jnp.sum(stream * stream, axis=1), "ch")
    total_width = width_here * lax.axis_size("ch")
    scale = lax.rsqrt(power / total_width + 1e-06)
    normed = stream * scale[:, None] * norm_gain
    return (stream, normed)


def solution(mesh):
    placed = (
        P("ctx", "ch"),
        P("ctx", "ch"),
        P("ctx", "ch"),
        P(None, None, "ch"),
        P(None, "ch"),
        P(None, "ch"),
        P("ch"),
        P("ch"),
        P("ctx", "ch"),
        P(),
    )
    return jax.shard_map(
        on_device,
        mesh=mesh,
        in_specs=placed,
        out_specs=(P("ctx", "ch"), P("ctx", "ch")),
        check_vma=False,
    )
```

profile of v0, /device:TPU:1, one launch (start us, length us, event | category | flops | bytes accessed | tf_op | source)
XLA Modules:
  0.0 371.1 jit_solution(10427337333996154706)
XLA Ops:
  8.8 4.9 %collective-permute-start = (bf16[3,2,2048]{2,1,0:T(2,128)(2,1)S(1)}, bf16[3,2,2048]{2,1,0:T(2,128)(2,1)S(1)}, u32[]{:S(2)}, u32[]{:S(2)}) collective-permute-start(bf16[3,2,2048]{2,1,0:T(2,128)(2,1)S(1)} %pad_maximum_fusion.6), channel_id=1, source_target_pairs={{0,4},{4,8},{8,12},{12,16},{16,20},{20,24},{24,28},{28,32},{32,36}... | collective-permute-start | bytes 73736 | tf_op jit(solution)/shard_map/ppermute | solution.py:10
  18.9 2.3 exponential_multiply_fusion.13
  29.5 8.5 %multiply_reduce_fusion.4 = (f32[16,2048]{1,0:T(8,128)}, f32[16,2048]{1,0:T(8,128)}, f32[16,2048]{1,0:T(8,128)}, f32[16,2048]{1,0:T(8,128)}, f32[16,2048]{1,0:T(...) fusion(f32[16,2048]{1,0:T(8,128)S(1)} %bitcast.117, f32[16]{0:T(128)S(1)} %get-tuple-element.180, ...), kind=kLoop, calls=%fused_computation.33 | loop fusion | flops 29687808 | bytes 5112768 | tf_op jit(solution)/shard_map/reduce_sum | solution.py:80
  38.1 7.5 %multiply_reduce_fusion.18 = (f32[16,2048]{1,0:T(8,128)}, f32[16,2048]{1,0:T(8,128)}, f32[16,2048]{1,0:T(8,128)}, f32[16,2048]{1,0:T(8,128)}, f32[16,2048]{1,0:T...) fusion(f32[16,2048]{1,0:T(8,128)S(1)} %get-tuple-element.197, ...), kind=kLoop, calls=%fused_computation.47 | loop fusion | flops 24870912 | bytes 6947456 | tf_op jit(solution)/shard_map/reduce_sum | solution.py:80
  50.2 2.4 pad.54
  52.6 2.5 pad.55
  57.1 4.1 %pad.57 = f32[8,16,2048]{2,1,0:T(8,128)} pad(f32[4,16,2048]{2,1,0:T(8,128)} %add.543, f32[]{:T(128)} %constant.31.clone.1), padding=1_0_1x0_0_0x0_0_0 | pad | bytes 1572868 | tf_op jit(solution)/shard_map/pad | solution.py:82
  62.8 2.4 pad.62
  65.3 2.5 pad.63
  67.7 2.3 fusion.17
  70.1 2.4 pad.56
  74.1 4.0 %pad.141 = f32[15,16,2048]{2,1,0:T(8,128)} pad(f32[8,16,2048]{2,1,0:T(8,128)S(1)} %add.545, f32[]{:T(128)} %constant.31.clone.1), padding=0_0_1x0_0_0x0_0_0 | pad | bytes 3014660
  79.7 2.0 add.549
  82.7 4.4 %pad.65 = f32[8,16,2048]{2,1,0:T(8,128)} pad(f32[4,16,2048]{2,1,0:T(8,128)} %add.549, f32[]{:T(128)} %constant.31.clone.1), padding=1_0_1x0_0_0x0_0_0 | pad | bytes 1572868 | tf_op jit(solution)/shard_map/pad | solution.py:82
  88.9 4.1 %pad.64 = f32[8,16,2048]{2,1,0:T(8,128)} pad(f32[4,16,2048]{2,1,0:T(8,128)} %pad_maximum_fusion.3, f32[]{:T(128)} %constant.31.clone.1), padding=0_1_1x0_0_0x0_0_0 | pad | bytes 1572868 | tf_op jit(solution)/shard_map/pad | solution.py:82
  93.0 2.8 add.550
  95.8 6.4 %pad.139 = f32[15,16,2048]{2,1,0:T(8,128)} pad(f32[8,16,2048]{2,1,0:T(8,128)} %add.550, f32[]{:T(128)} %constant.31.clone.1), padding=0_0_1x0_0_0x0_0_0 | pad | bytes 3014660
  104.5 4.0 %pad.59 = f32[16,16,2048]{2,1,0:T(8,128)} pad(f32[8,16,2048]{2,1,0:T(8,128)S(1)} %add.545, f32[]{:T(128)} %constant.31.clone.1), padding=1_0_1x0_0_0x0_0_0 | pad | bytes 3145732 | tf_op jit(solution)/shard_map/pad | solution.py:82
  108.5 6.5 %pad.67 = f32[16,16,2048]{2,1,0:T(8,128)} pad(f32[8,16,2048]{2,1,0:T(8,128)} %add.550, f32[]{:T(128)} %constant.31.clone.1), padding=1_0_1x0_0_0x0_0_0 | pad | bytes 3145732 | tf_op jit(solution)/shard_map/pad | solution.py:82
  114.9 3.5 fusion.16
  118.5 4.0 %pad.58 = f32[16,16,2048]{2,1,0:T(8,128)} pad(f32[8,16,2048]{2,1,0:T(8,128)S(1)} %pad_maximum_fusion, f32[]{:T(128)} %constant.31.clone.1), padding=0_1_1x0_0_0x0_0_0 | pad | bytes 3145732 | tf_op jit(solution)/shard_map/pad | solution.py:82
  122.6 4.0 %pad.66 = f32[16,16,2048]{2,1,0:T(8,128)} pad(f32[8,16,2048]{2,1,0:T(8,128)S(1)} %pad_maximum_fusion.1, f32[]{:T(128)} %constant.31.clone.1), padding=0_1_1x0_0_0x0_0_0 | pad | bytes 3145732 | tf_op jit(solution)/shard_map/pad | solution.py:82
  128.6 3.2 slice_add_fusion.1
  133.7 3.4 multiply_reduce_fusion.16
  137.1 27.7 %all-gather.5.cloned.1.call-done = f32[64,16,2048]{2,1,0:T(8,128)} async-done(((f32[1,16,2048]{2,1,0:T(8,128)}), f32[64,16,2048]{2,1,0:T(8,128)}) %all-gather.5.cloned.1.call-update) | async-done | bytes 8388624 | tf_op jit(solution)/shard_map/all_gather | solution.py:15
  164.8 83.1 %all-gather.3.cloned.1.call-done = f32[64,16,2048]{2,1,0:T(8,128)} async-done(((f32[1,16,2048]{2,1,0:T(8,128)}), f32[64,16,2048]{2,1,0:T(8,128)}) %all-gather.3.cloned.1.call-update) | async-done | bytes 8388624 | tf_op jit(solution)/shard_map/all_gather | solution.py:15
  247.9 68.7 %while.14 = (s32[]{:T(128)}, f32[16,2048]{1,0:T(8,128)S(1)}, s32[]{:T(128)}, f32[64,16,2048]{2,1,0:T(8,128)}, f32[64,16,2048]{2,1,0:T(8,128)}, /*index=5*/s32[]{:T(128)}, s32[]{:T(128)}) while((s32[]{:T(128)}, f32[16,2048]{1,0:T(8,128)S(1)}, s32[]{:T(128)}, f32[64,16,2048]{2,1,0:T(8,128)}, f32[64,16,2048]{2,1,0:T(8,128)}, ...), condition=%wide.region_6.7_spmd.clone, body=%wide.region_5.6_spmd.clone.sunk | while | flops 131076 | bytes 524389 | solution.py:24
  316.8 10.4 %multiply_reduce_fusion.1 = (f32[16,2048]{1,0:T(8,128)S(1)}, f32[16,2048]{1,0:T(8,128)S(1)}, f32[16,2048]{1,0:T(8,128)S(1)}, f32[16,2048]{1,0:T(8,128)S(1)}, f32...) fusion(f32[16,2048]{1,0:T(8,128)S(1)} %copy-done.31, ...), kind=kLoop, calls=%fused_computation.30 | loop fusion | flops 17301504 | bytes 8257536 | tf_op jit(solution)/shard_map/reduce_sum | solution.py:96
  339.9 7.8 %stack.14 = f32[16,16,2048]{2,1,0:T(8,128)} concatenate(f32[16,1,2048]{2,1,0:T(1,128)} %multiply_add_fusion.32, f32[16,1,2048]{2,1,0:T(1,128)} %multiply_add_fusion.31, f32[16,1,2048]{2,1,0:T(1,128)} %multiply_add_fusion.30, f32[16,1,2048]{2,1,0:T(1,128)} %multiply_add_fusion.29, f32[16,1,2048]{2,1,0:T(1,128)} %multiply_add_fusion.28, f32[16,1,2048]{2,1,0:T(1,128)} %multiply_add_fusion.27, ...), dimensions={1} | concatenate | bytes 4194304 | tf_op jit(solution)/shard_map/stack | solution.py:98
  347.8 4.9 %multiply_reduce_fusion = (f32[256]{0:T(256)S(1)}, f32[256,2048]{1,0:T(8,128)}) fusion(f32[256,2048]{1,0:T(8,128)} %copy-done, f32[2048]{0:T(1024)S(1)} %copy-done.59, f32[16,16,2048]{2,1,0:T(8,128)} %stack.14, f32[256]{0:T(256)S(1)} %copy-done.58, f32[258,2048]{1,0:T(8,128)S(1)} %maximum_convert_fusion, f32[2048]{0:T(1024)S(1)} %bitcast.126, ...), kind=kLoop, calls=%fused_computation.29 | loop fusion | flops 7339776 | bytes 13667328 | tf_op jit(solution)/shard_map/reduce_sum | solution.py:100
  352.7 8.4 %psum.7 = f32[256]{0:T(256)S(1)} all-reduce(f32[256]{0:T(256)S(1)} %get-tuple-element.192), channel_id=1, replica_groups=mesh['ctx'=64,'ch'=4] {'ch'}, use_global_device_ids=true, to_apply=%region_39.40 | all-reduce | flops 256 | bytes 2048 | tf_op jit(solution)/shard_map/psum | solution.py:100
  361.1 3.2 multiply_multiply_fusion
  (342 shorter events, 114.8 us)
Async XLA Ops:
  7.2 157.7 %all-gather.5.cloned.1.call-start = ((), (), s32[]{:S(2)}) async-start(), calls=%async_computation.1 | async-start | bytes 8519680 | tf_op jit(solution)/shard_map/all_gather | solution.py:15
  8.8 14.6 %collective-permute-start = (bf16[3,2,2048]{2,1,0:T(2,128)(2,1)S(1)}, bf16[3,2,2048]{2,1,0:T(2,128)(2,1)S(1)}, u32[]{:S(2)}, u32[]{:S(2)}) collective-permute-start(bf16[3,2,2048]{2,1,0:T(2,128)(2,1)S(1)} %pad_maximum_fusion.6), channel_id=1, source_target_pairs={{0,4},{4,8},{8,12},{12,16},{16,20},{20,24},{24,28},{28,32},{32,36}... | collective-permute-start | bytes 73736 | tf_op jit(solution)/shard_map/ppermute | solution.py:10
  22.8 22.8 %copy-start.1 = (f32[16,16,2048]{2,1,0:T(8,128)}, f32[16,16,2048]{2,1,0:T(8,128)S(1)}, u32[]{:S(2)}) copy-start(f32[16,16,2048]{2,1,0:T(8,128)S(1)} %broadcast_multiply_fusion) | copy-start | bytes 6291460
  23.3 14.6 %copy-start.61 = (f32[16]{0:T(128)}, f32[16]{0:T(128)S(1)}, u32[]{:S(2)}) copy-start(f32[16]{0:T(128)S(1)} %get-tuple-element.167) | copy-start | bytes 196
  23.3 14.6 %copy-start.63 = (f32[16]{0:T(128)}, f32[16]{0:T(128)S(1)}, u32[]{:S(2)}) copy-start(f32[16]{0:T(128)S(1)} %get-tuple-element.168) | copy-start | bytes 196
  23.3 14.6 %copy-start.65 = (f32[16]{0:T(128)}, f32[16]{0:T(128)S(1)}, u32[]{:S(2)}) copy-start(f32[16]{0:T(128)S(1)} %get-tuple-element.169) | copy-start | bytes 196
  23.4 14.6 %copy-start.67 = (f32[16]{0:T(128)}, f32[16]{0:T(128)S(1)}, u32[]{:S(2)}) copy-start(f32[16]{0:T(128)S(1)} %get-tuple-element.170) | copy-start | bytes 196
  23.4 14.6 %copy-start.69 = (f32[16]{0:T(128)}, f32[16]{0:T(128)S(1)}, u32[]{:S(2)}) copy-start(f32[16]{0:T(128)S(1)} %get-tuple-element.171) | copy-start | bytes 196
  23.4 14.6 %copy-start.71 = (f32[16]{0:T(128)}, f32[16]{0:T(128)S(1)}, u32[]{:S(2)}) copy-start(f32[16]{0:T(128)S(1)} %get-tuple-element.172) | copy-start | bytes 196
  23.4 14.6 %copy-start.73 = (f32[16]{0:T(128)}, f32[16]{0:T(128)S(1)}, u32[]{:S(2)}) copy-start(f32[16]{0:T(128)S(1)} %get-tuple-element.173) | copy-start | bytes 196
  23.4 14.6 %copy-start.75 = (f32[16]{0:T(128)}, f32[16]{0:T(128)S(1)}, u32[]{:S(2)}) copy-start(f32[16]{0:T(128)S(1)} %get-tuple-element.181) | copy-start | bytes 196
  28.6 9.4 %copy-start.9 = (f32[16,1,2048]{2,0,1:T(8,128)}, f32[16,1,2048]{2,0,1:T(8,128)S(1)}, u32[]{:S(2)}) copy-start(f32[16,1,2048]{2,0,1:T(8,128)S(1)} %copy.85) | copy-start | bytes 393220
  28.7 9.3 %copy-start.11 = (f32[16,1,2048]{2,0,1:T(8,128)}, f32[16,1,2048]{2,0,1:T(8,128)S(1)}, u32[]{:S(2)}) copy-start(f32[16,1,2048]{2,0,1:T(8,128)S(1)} %copy.86) | copy-start | bytes 393220
  46.0 21.7 %copy-start.6 = (f32[8,16,2048]{2,1,0:T(8,128)}, f32[8,16,2048]{2,1,0:T(8,128)S(1)}, u32[]{:S(2)}) copy-start(f32[8,16,2048]{2,1,0:T(8,128)S(1)} %get-tuple-element.201) | copy-start | bytes 3145732
  79.7 168.2 %all-gather.3.cloned.1.call-start = ((), (), s32[]{:S(2)}) async-start(), calls=%async_computation | async-start | bytes 8519680 | tf_op jit(solution)/shard_map/all_gather | solution.py:15
  137.1 179.6 %copy-start.30 = (f32[16,2048]{1,0:T(8,128)S(1)}, f32[16,2048]{1,0:T(8,128)}, u32[]{:S(2)}) copy-start(f32[16,2048]{1,0:T(8,128)} %get-tuple-element.228) | copy-start | bytes 393220
  137.1 179.6 %copy-start.31 = (f32[16,2048]{1,0:T(8,128)S(1)}, f32[16,2048]{1,0:T(8,128)}, u32[]{:S(2)}) copy-start(f32[16,2048]{1,0:T(8,128)} %get-tuple-element.229) | copy-start | bytes 393220
  137.1 179.6 %copy-start.32 = (f32[16,2048]{1,0:T(8,128)S(1)}, f32[16,2048]{1,0:T(8,128)}, u32[]{:S(2)}) copy-start(f32[16,2048]{1,0:T(8,128)} %get-tuple-element.230) | copy-start | bytes 393220
  137.1 179.6 %copy-start.33 = (f32[16,2048]{1,0:T(8,128)S(1)}, f32[16,2048]{1,0:T(8,128)}, u32[]{:S(2)}) copy-start(f32[16,2048]{1,0:T(8,128)} %get-tuple-element.231) | copy-start | bytes 393220
  316.7 10.6 %copy-start.48 = (f32[16,2048]{1,0:T(8,128)S(1)}, f32[16,2048]{1,0:T(8,128)}, u32[]{:S(2)}) copy-start(f32[16,2048]{1,0:T(8,128)} %get-tuple-element.149) | copy-start | bytes 393220
  316.7 10.6 %copy-start.78 = (f32[16]{0:T(128)S(1)}, f32[16]{0:T(128)}, u32[]{:S(2)}) copy-start(f32[16]{0:T(128)} %copy-done.77) | copy-start | bytes 196
  316.7 10.8 %copy-start.47 = (f32[16,2048]{1,0:T(8,128)S(1)}, f32[16,2048]{1,0:T(8,128)}, u32[]{:S(2)}) copy-start(f32[16,2048]{1,0:T(8,128)} %get-tuple-element.118) | copy-start | bytes 393220
  316.7 10.8 %copy-start.95 = (f32[16]{0:T(128)S(1)}, f32[16]{0:T(128)}, u32[]{:S(2)}) copy-start(f32[16]{0:T(128)} %get-tuple-element.150) | copy-start | bytes 196
  316.7 11.0 %copy-start.46 = (f32[16,2048]{1,0:T(8,128)S(1)}, f32[16,2048]{1,0:T(8,128)}, u32[]{:S(2)}) copy-start(f32[16,2048]{1,0:T(8,128)} %get-tuple-element.119) | copy-start | bytes 393220
  316.7 11.0 %copy-start.94 = (f32[16]{0:T(128)S(1)}, f32[16]{0:T(128)}, u32[]{:S(2)}) copy-start(f32[16]{0:T(128)} %get-tuple-element.151) | copy-start | bytes 196
  316.7 11.9 %copy-start.45 = (f32[16,2048]{1,0:T(8,128)S(1)}, f32[16,2048]{1,0:T(8,128)}, u32[]{:S(2)}) copy-start(f32[16,2048]{1,0:T(8,128)} %get-tuple-element.148) | copy-start | bytes 393220
  316.8 11.9 %copy-start.93 = (f32[16]{0:T(128)S(1)}, f32[16]{0:T(128)}, u32[]{:S(2)}) copy-start(f32[16]{0:T(128)} %get-tuple-element.152) | copy-start | bytes 196
  316.8 12.7 %copy-start.43 = (f32[16,2048]{1,0:T(8,128)S(1)}, f32[16,2048]{1,0:T(8,128)}, u32[]{:S(2)}) copy-start(f32[16,2048]{1,0:T(8,128)} %get-tuple-element.147) | copy-start | bytes 393220
  316.8 12.7 %copy-start.92 = (f32[16]{0:T(128)S(1)}, f32[16]{0:T(128)}, u32[]{:S(2)}) copy-start(f32[16]{0:T(128)} %get-tuple-element.153) | copy-start | bytes 196
  316.8 13.6 %copy-start.41 = (f32[16,2048]{1,0:T(8,128)S(1)}, f32[16,2048]{1,0:T(8,128)}, u32[]{:S(2)}) copy-start(f32[16,2048]{1,0:T(8,128)} %get-tuple-element.146) | copy-start | bytes 393220
  316.8 13.6 %copy-start.91 = (f32[16]{0:T(128)S(1)}, f32[16]{0:T(128)}, u32[]{:S(2)}) copy-start(f32[16]{0:T(128)} %get-tuple-element.154) | copy-start | bytes 196
  347.8 13.4 %copy-start.60 = (f32[2048]{0:T(1024)S(1)}, f32[2048]{0:T(1024)}, u32[]{:S(2)}) copy-start(f32[2048]{0:T(1024)} %param.19) | copy-start | bytes 24580
  (68 other events, 354.1 us)
Sparse Core Ops, SparseCore 0:
  79.8 84.9 all-gather.4
  167.6 80.2 all-gather.2
where the time goes:
time: 375 us; the launch traced here: 371 us
  other arithmetic  155 us (41%)
  waiting for transfers between devices  111 us (30%)
  local copies, waits for them, and re-layouts  75.4 us (20%)
  between operations  15.3 us (4%)
  blocking collectives  8.42 us (2%)
  starting transfers between devices  5.01 us (1%)
    all_gather x2, waiting for transfers between devices, carried_in(): pieces = jax.tree.map(lambda part: lax.all_gather(part, axis), value)  111 us
    select_n x63, other arithmetic, step(): jnp.where(position < mine, new, old)  67.4 us
    pad x12, local copies, waits for them, and re-layouts, on_device(): lax.associative_scan(combine_pair, (block_decay, states), axis=0)  43.2 us
    reduce_sum x3, other arithmetic, on_device(): partial_out.append(jnp.sum(pole_gain[None] * states, axis=1))  19.4 us
    add x8, other arithmetic, on_device(): lax.associative_scan(combine_pair, (block_decay, states), axis=0)  15 us
    add x16, other arithmetic, on_device(): long_rows.append(partial_out[offset] + alive[:, offset][:, None] * carried)  12.4 us
    unnamed x210, local copies, waits for them, and re-layouts  12.2 us
    reduce_sum x1, other arithmetic, on_device(): carried = jnp.sum(weights[None] * entry_state, axis=1)  10.4 us
  transfers between devices with their start and end apart: 3, of which 2 were waited for; matrix products, arithmetic and copies ran while one was open for 18% of the time, Pallas kernels for 0%

commit v1 on v0

v1 whole, which is shorter than its diff:
```python
import functools

import jax
import jax.numpy as jnp
from jax import lax
from jax.experimental import pallas as pl
from jax.experimental.pallas import tpu as pltpu
from jax.sharding import PartitionSpec as P

LANES = 128
CHUNKS = 8
GROUP = 512
STEPS = 8
F32 = jnp.float32
BF16 = jnp.bfloat16


def starts_of(lengths_ref):
    first = lengths_ref[0]
    second = first + lengths_ref[1]
    third = second + lengths_ref[2]
    return (first, second, third)


def spread(row):
    return jnp.broadcast_to(row, (CHUNKS, LANES))


def no_start(starts, where):
    kept = jnp.ones(where.shape, jnp.bool_)
    for start in starts:
        kept = kept & (where != start)
    return kept.astype(F32)


def any_in(starts, low, high):
    found = jnp.bool_(False)
    for start in starts:
        found = found | ((start >= low) & (start < high))
    return found


def block_has_start(starts, base, rows, block):
    found = jnp.bool_(False)
    for start in starts:
        inside = start - base
        place = lax.rem(jnp.maximum(inside, 0), rows // CHUNKS)
        found = found | (
            (inside >= 0) & (inside < rows) & (place >= block * STEPS) & (place < (block + 1) * STEPS)
        )
    return found


def lanes_at(part):
    return pl.ds(pl.multiple_of(part * LANES, LANES), LANES)


def chunk_of(place):
    return pl.ds(pl.multiple_of(place * CHUNKS, CHUNKS), CHUNKS)


def lay_out(source, lanes, target, span, offset):
    for piece in range(CHUNKS):
        low = offset + piece * (span + 1)
        target[low : low + span, :] = source[piece * span : (piece + 1) * span, lanes].astype(F32)


def column_copies(sources, targets, sems, group):
    lanes = pl.ds(pl.multiple_of(group * GROUP, GROUP), GROUP)
    return [
        pltpu.make_async_copy(source.at[:, lanes], target.at[:, lanes], sems.at[i, group])
        for i, (source, target) in enumerate(zip(sources, targets))
    ]


def rim_kernel(q_hbm, k_hbm, v_hbm, out_ref, buffer, sems):
    tail = buffer.shape[1]
    copies = [
        pltpu.make_async_copy(source.at[pl.ds(source.shape[0] - tail, tail), :], buffer.at[i], sems.at[i])
        for i, source in enumerate((q_hbm, k_hbm, v_hbm))
    ]
    for copy in copies:
        copy.start()
    for i, copy in enumerate(copies):
        copy.wait()
        out_ref[i] = buffer[i, tail - 2 :, :]


def walk(span, starts, base, rows, run, carry):
    def one_block(block, carry):
        flag = block_has_start(starts, base, rows, block)
        return lax.cond(
            flag, functools.partial(run, block, True), functools.partial(run, block, False), carry
        )

    return lax.fori_loop(0, span // STEPS, one_block, carry)


def end_kernel(rows, poles, lengths_ref, k_hbm, v_hbm, rim_ref, taps_hbm, rate_hbm, gated_a, gated_hbm, local_hbm, end_ref, rim_hbm, k_ref, v_ref, gated_b, local_ref, taps_ref, rate_ref, kx, vx, decay_ref, sems, out_sems, local_sems, small_sems):
    span = rows // CHUNKS
    starts = starts_of(lengths_ref)
    base = lax.axis_index("ctx") * rows
    chunk = lax.broadcasted_iota(jnp.int32, (CHUNKS, LANES), 0)
    chunk_row = base + chunk * span
    small = [
        pltpu.make_async_copy(taps_hbm, taps_ref, small_sems.at[0]),
        pltpu.make_async_copy(rate_hbm, rate_ref, small_sems.at[1]),
    ]
    pass_on = pltpu.make_async_copy(rim_ref.at[0], rim_hbm, small_sems.at[2])
    groups = k_ref.shape[1] // GROUP
    for group in range(groups):
        for copy in column_copies((k_hbm, v_hbm), (k_ref, v_ref), sems, group):
            copy.start()
        if group == 0:
            for copy in small:
                copy.start()
    pass_on.start()
    for copy in small:
        copy.wait()
    far = no_start(starts, chunk_row - 1)
    alive = jnp.ones((CHUNKS, LANES), jnp.bool_)
    for start in starts:
        alive = alive & ((start < chunk_row) | (start >= chunk_row + span))
    joined = (alive & (chunk > 0)).astype(F32)

    inner = GROUP // LANES

    def store(here):
        return pltpu.make_async_copy(gated_b.at[here], gated_hbm.at[here], out_sems.at[here])

    def store_local(part):
        return pltpu.make_async_copy(local_ref.at[part], local_hbm.at[part], local_sems.at[part])

    def one_group(group, first, gated_ref):
        for copy in column_copies((k_hbm, v_hbm), (k_ref, v_ref), sems, group):
            copy.wait()

        @pl.loop(group * inner, (group + 1) * inner)
        def _(part):
            lanes = lanes_at(part)
            here = part - first * inner
            for i, source, target in ((1, k_ref, kx), (2, v_ref, vx)):
                target[5:7, :] = rim_ref[i, :, lanes].astype(F32)
                lay_out(source, lanes, target, span, 8)
            decay_ref[...] = jnp.exp(-rate_ref[:, lanes])
            taps = [[spread(taps_ref[i, j : j + 1, lanes]) for j in range(3)] for i in (1, 2)]
            decay = [spread(decay_ref[m : m + 1, :]) for m in range(poles)]
            carry = (
                kx[pl.ds(6, CHUNKS, stride=span + 1), :],
                kx[pl.ds(5, CHUNKS, stride=span + 1), :] * far,
                vx[pl.ds(6, CHUNKS, stride=span + 1), :],
                vx[pl.ds(5, CHUNKS, stride=span + 1), :] * far,
            ) + tuple(jnp.zeros((CHUNKS, LANES), F32) for _ in range(poles))

            def run(block, masked, carry):
                carry = list(carry)
                for step in range(STEPS):
                    place = block * STEPS + step
                    if masked:
                        keep = no_start(starts, chunk_row + place)
                        carry = [held * keep for held in carry]
                    row = pl.ds(8 + place, CHUNKS, stride=span + 1)
                    key = kx[row, :]
                    value = vx[row, :]
                    key_short = taps[0][0] * key + taps[0][1] * carry[0] + taps[0][2] * carry[1]
                    value_short = taps[1][0] * value + taps[1][1] * carry[2] + taps[1][2] * carry[3]
                    gated = key_short * value_short
                    gated_ref[here, chunk_of(place), :] = gated
                    states = [decay[m] * carry[4 + m] + gated for m in range(poles)]
                    carry = [key, carry[0], value, carry[2]] + states
                return tuple(carry)

            carry = walk(span, starts, base, rows, run, carry)
            for m in range(poles):
                rate = spread(rate_ref[m : m + 1, lanes])
                reach = jnp.exp(-float(span) * rate) * joined
                state = carry[4 + m]
                for hop in (1, 2, 4):
                    state = state + reach * pltpu.roll(state, hop, 0)
                    if hop < 4:
                        reach = reach * pltpu.roll(reach, hop, 0)
                end_ref[part, m : m + 1, :] = state[CHUNKS - 1 :, :]
                local_ref[part, m * CHUNKS : (m + 1) * CHUNKS, :] = jnp.where(
                    chunk > 0, pltpu.roll(state, 1, 0), 0.0
                )
            store_local(part).start()
            if first:
                store(here).start()

    middle = gated_a.shape[0] // inner
    pl.loop(0, middle)(lambda group: one_group(group, 0, gated_a))
    pl.loop(middle, groups)(lambda group: one_group(group, middle, gated_b))
    pass_on.wait()
    for here in range(gated_b.shape[0]):
        store(here).wait()
    for part in range(local_ref.shape[0]):
        store_local(part).wait()


def scan_kernel(rows, poles, lengths_ref, rate_ref, pieces_ref, out_ref):
    starts = starts_of(lengths_ref)
    ranks, held = pieces_ref.shape[:2]
    shares = poles // held
    mine = lax.axis_index("ctx")
    lanes = lanes_at(lax.div(mine, shares))
    rate = rate_ref[:held, lanes]
    for share in range(1, shares):
        theirs = rate_ref[share * held : (share + 1) * held, lanes]
        rate = jnp.where(lax.rem(mine, shares) == share, theirs, rate)
    whole = jnp.exp(-float(rows) * rate)
    running = jnp.zeros((held, LANES), F32)
    for rank in range(ranks):
        out_ref[rank] = running
        alive = jnp.where(any_in(starts, rank * rows, (rank + 1) * rows), 0.0, 1.0)
        running = (alive * whole) * running + pieces_ref[rank]


def near_kernel(rows, poles, first, lengths_ref, q_hbm, res_hbm, rim_hbm, taps_hbm, rate_hbm, gain_ref, skip_ref, gated_in, local_hbm, near_ref, query_out, q_ref, r_ref, local_ref, rim_ref, taps_ref, rate_ref, qx, rx, decay_ref, sems, local_sems, small_sems, *moved):
    span = rows // CHUNKS
    starts = starts_of(lengths_ref)
    base = lax.axis_index("ctx") * rows
    chunk = lax.broadcasted_iota(jnp.int32, (CHUNKS, LANES), 0)
    chunk_row = base + chunk * span
    small = [
        pltpu.make_async_copy(taps_hbm, taps_ref, small_sems.at[0]),
        pltpu.make_async_copy(rate_hbm, rate_ref, small_sems.at[1]),
        pltpu.make_async_copy(rim_hbm, rim_ref, small_sems.at[2]),
    ]
    for copy in small:
        copy.start()
    inner = GROUP // LANES
    gated_ref, query_ref, gated_sems, query_sems = moved or (gated_in, query_out, None, None)

    def fetch_local(here):
        source = local_hbm.at[here + first * inner]
        return pltpu.make_async_copy(source, local_ref.at[here], local_sems.at[here])

    def fetch(here):
        return pltpu.make_async_copy(gated_in.at[here], gated_ref.at[here], gated_sems.at[here])

    def store(here):
        return pltpu.make_async_copy(query_ref.at[here], query_out.at[here], query_sems.at[here])

    count = near_ref.shape[0] // inner
    for group in range(first, first + count):
        for copy in column_copies((q_hbm, res_hbm), (q_ref, r_ref), sems, group):
            copy.start()
        for here in range((group - first) * inner, (group - first + 1) * inner):
            fetch_local(here).start()
            if moved:
                fetch(here).start()
    for copy in small:
        copy.wait()
    far = no_start(starts, chunk_row - 1)

    @pl.loop(first, first + count)
    def _(group):
        for copy in column_copies((q_hbm, res_hbm), (q_ref, r_ref), sems, group):
            copy.wait()

        @pl.loop(group * inner, (group + 1) * inner)
        def _(part):
            lanes = lanes_at(part)
            here = part - first * inner
            fetch_local(here).wait()
            if moved:
                fetch(here).wait()
            qx[5:7, :] = rim_ref[:, lanes].astype(F32)
            lay_out(q_ref, lanes, qx, span, 8)
            lay_out(r_ref, lanes, rx, span, 0)
            decay_ref[...] = jnp.exp(-rate_ref[:, lanes])
            taps = [spread(taps_ref[0, j : j + 1, lanes]) for j in range(3)]
            skip = spread(skip_ref[:, lanes])
            decay = [spread(decay_ref[m : m + 1, :]) for m in range(poles)]
            gain = [spread(gain_ref[m : m + 1, lanes]) for m in range(poles)]
            carry = [
                qx[pl.ds(6, CHUNKS, stride=span + 1), :],
                qx[pl.ds(5, CHUNKS, stride=span + 1), :] * far,
            ] + [local_ref[here, m * CHUNKS : (m + 1) * CHUNKS, :] for m in range(poles)]

            def run(block, masked, carry):
                carry = list(carry)
                for step in range(STEPS):
                    place = block * STEPS + step
                    if masked:
                        keep = no_start(starts, chunk_row + place)
                        carry = [held * keep for held in carry]
                    query = qx[pl.ds(8 + place, CHUNKS, stride=span + 1), :]
                    query_short = taps[0] * query + taps[1] * carry[0] + taps[2] * carry[1]
                    gated = gated_ref[here, chunk_of(place), :]
                    states = [decay[m] * carry[2 + m] + gated for m in range(poles)]
                    total = skip * gated
                    for m in range(poles):
                        total = total + gain[m] * states[m]
                    query_ref[here, chunk_of(place), :] = query_short
                    near_ref[here, chunk_of(place), :] = (
                        rx[pl.ds(place, CHUNKS, stride=span + 1), :] + query_short * total
                    )
                    carry = [query, carry[0]] + states
                return tuple(carry)

            walk(span, starts, base, rows, run, tuple(carry))
            if moved:
                store(here).start()

    if moved:
        for here in range(near_ref.shape[0]):
            store(here).wait()


def stream_kernel(rows, poles, lengths_ref, rate_ref, gain_ref, incoming_ref, near_a, query_a, near_b, query_hbm, out_hbm, stream_ref, power_ref, query_b, sx, px, decay_ref, sems, query_sems):
    span = rows // CHUNKS
    starts = starts_of(lengths_ref)
    base = lax.axis_index("ctx") * rows
    chunk = lax.broadcasted_iota(jnp.int32, (CHUNKS, LANES), 0)
    chunk_row = base + chunk * span
    ahead = base + rows
    for start in starts:
        ahead = jnp.where((start >= base) & (start < ahead), start, ahead)
    px[...] = jnp.zeros_like(px)
    half = near_a.shape[0]
    inner = GROUP // LANES

    def fetch(here):
        return pltpu.make_async_copy(query_hbm.at[here], query_b.at[here], query_sems.at[here])

    for here in range(half):
        fetch(here).start()
    before = (chunk * span).astype(F32)

    def copy_out(group):
        lanes = pl.ds(pl.multiple_of(group * GROUP, GROUP), GROUP)
        return pltpu.make_async_copy(stream_ref.at[:, lanes], out_hbm.at[:, lanes], sems.at[group])

    def one_part(part, near_ref, query_ref, place_of):
        lanes = lanes_at(part)
        decay_ref[...] = jnp.exp(-rate_ref[:, lanes])
        decay = [spread(decay_ref[m : m + 1, :]) for m in range(poles)]
        carry = []
        for m in range(poles):
            entering = incoming_ref[part, m : m + 1, :] * gain_ref[m : m + 1, lanes]
            carry.append(jnp.exp(-before * spread(rate_ref[m : m + 1, lanes])) * spread(entering))
        for place in range(span):
            carry = [decay[m] * carry[m] for m in range(poles)]
            terms = list(carry)
            while len(terms) > 1:
                terms = [
                    terms[i] + terms[i + 1] if i + 1 < len(terms) else terms[i]
                    for i in range(0, len(terms), 2)
                ]
            carried = jnp.where(chunk_row + place < ahead, terms[0], 0.0)
            here = chunk_of(place)
            sx[pl.ds(place, CHUNKS, stride=span + 1), :] = (
                near_ref[place_of, here, :] + query_ref[place_of, here, :] * carried
            )
        for piece in range(CHUNKS):
            low = piece * (span + 1)
            stream = sx[low : low + span, :]
            native = slice(piece * span, (piece + 1) * span)
            stream_ref[native, lanes] = stream
            px[native, :] += stream * stream

    groups = stream_ref.shape[1] // GROUP
    for side, (near_ref, query_ref) in enumerate(((near_a, query_a), (near_b, query_b))):

        @pl.loop(0, half // inner)
        def _(group):
            @pl.loop(group * inner, (group + 1) * inner)
            def _(part):
                if side:
                    fetch(part).wait()
                one_part(part + side * half, near_ref, query_ref, part)

            copy_out(group + side * (half // inner)).start()

    for piece in range(rows // LANES):
        turned = px[piece * LANES : (piece + 1) * LANES, :].T
        power_ref[piece : piece + 1, :] = jnp.sum(turned, axis=0, keepdims=True)
    for group in range(groups):
        copy_out(group).wait()


def norm_kernel(width, power_ref, gain_ref, stream_ref, out_hbm, scale_ref, buffer, sems):
    scale = lax.rsqrt(jnp.sum(power_ref[...], axis=0) / width + 1e-06)
    for piece in range(scale.shape[0]):
        wide = jnp.broadcast_to(scale[piece : piece + 1, :], (LANES, LANES))
        scale_ref[piece * LANES : (piece + 1) * LANES, :] = wide.T
    rows = stream_ref.shape[0]
    count = sems.shape[0]
    tall = rows // count

    def copy_out(group):
        here = pl.ds(pl.multiple_of(group * tall, tall), tall)
        return pltpu.make_async_copy(buffer.at[here, :], out_hbm.at[here, :], sems.at[group])

    @pl.loop(0, count)
    def _(group):
        here = pl.ds(pl.multiple_of(group * tall, tall), tall)
        factor = scale_ref[here, :]
        for part in range(stream_ref.shape[1] // LANES):
            lanes = slice(part * LANES, (part + 1) * LANES)
            buffer[here, lanes] = stream_ref[here, lanes] * factor * gain_ref[:, lanes]
        copy_out(group).start()

    for group in range(count):
        copy_out(group).wait()


def shifted(block, axis, distance, wrap):
    count = lax.axis_size(axis)
    route = [(i, (i + distance) % count) for i in range(count) if wrap or i + distance < count]
    return lax.ppermute(block, axis, route)


def on_device(query_proj, key_proj, value_proj, short_filter, decay_rate, residue, skip_gain, norm_gain, residual, lengths):
    rows, width = query_proj.shape
    poles = decay_rate.shape[0]
    ranks = lax.axis_size("ctx")
    parts = width // LANES
    span = rows // CHUNKS
    groups = width // GROUP
    numbers = pl.BlockSpec(memory_space=pltpu.SMEM)
    near_by = pl.BlockSpec(memory_space=pltpu.VMEM)
    outside = pl.BlockSpec(memory_space=pltpu.HBM)
    limit = pltpu.CompilerParams(vmem_limit_bytes=12 * 1024 * 1024)
    shape = lambda *dims: jax.ShapeDtypeStruct(dims, F32)
    kept_near = lambda *dims: pltpu.VMEM(dims, F32)
    far_off = lambda array: pltpu.with_memory_space_constraint(array, pltpu.HBM)
    close_by = lambda array: pltpu.with_memory_space_constraint(array, pltpu.VMEM)
    query_proj, key_proj, value_proj, residual, short_filter = map(
        far_off, (query_proj, key_proj, value_proj, residual, short_filter)
    )

    rims = pl.pallas_call(
        rim_kernel,
        in_specs=[outside] * 3,
        out_specs=near_by,
        out_shape=jax.ShapeDtypeStruct((3, 2, width), query_proj.dtype),
        scratch_shapes=[pltpu.VMEM((3, 16, width), BF16), pltpu.SemaphoreType.DMA((3,))],
        name="rims",
    )(query_proj, key_proj, value_proj)
    rims = shifted(rims, "ctx", 1, False)
    pole_gain = residue * jnp.sqrt(-jnp.expm1(-2.0 * decay_rate))
    skip = skip_gain.reshape(1, width)

    half = parts // 2
    gated_a, gated_b, local, end, query_rim = pl.pallas_call(
        functools.partial(end_kernel, rows, poles),
        in_specs=[numbers, outside, outside, near_by, outside, outside],
        out_specs=[near_by, outside, outside, near_by, outside],
        out_shape=[
            kept_near(half, rows, LANES),
            pltpu.HBM((half, rows, LANES), F32),
            pltpu.HBM((parts, poles * CHUNKS, LANES), F32),
            shape(parts, poles, LANES),
            pltpu.HBM((2, width), BF16),
        ],
        scratch_shapes=[
            pltpu.VMEM((rows, width), BF16),
            pltpu.VMEM((rows, width), BF16),
            pltpu.VMEM((half, rows, LANES), F32),
            pltpu.VMEM((parts, poles * CHUNKS, LANES), F32),
            pltpu.VMEM((3, 3, width), F32),
            pltpu.VMEM((poles, width), F32),
            pltpu.VMEM((rows + 16, LANES), F32),
            pltpu.VMEM((rows + 16, LANES), F32),
            pltpu.VMEM((poles, LANES), F32),
            pltpu.SemaphoreType.DMA((2, groups)),
            pltpu.SemaphoreType.DMA((half,)),
            pltpu.SemaphoreType.DMA((parts,)),
            pltpu.SemaphoreType.DMA((3,)),
        ],
        compiler_params=limit,
        name="end_state",
    )(lengths, key_proj, value_proj, rims, short_filter, decay_rate)

    held = parts * poles // ranks
    pieces = lax.all_to_all(end.reshape(ranks, held, LANES), "ctx", 0, 0, tiled=True)

    def near_side(first, count, gated, moved):
        block = (count * (GROUP // LANES), rows, LANES)
        return pl.pallas_call(
            functools.partial(near_kernel, rows, poles, first),
            in_specs=[numbers] + [outside] * 5 + [near_by, near_by, outside if moved else near_by, outside],
            out_specs=[near_by, outside if moved else near_by],
            out_shape=[kept_near(*block), pltpu.HBM(block, F32) if moved else kept_near(*block)],
            scratch_shapes=[
                pltpu.VMEM((rows, width), BF16),
                pltpu.VMEM((rows, width), BF16),
                pltpu.VMEM((block[0], poles * CHUNKS, LANES), F32),
                pltpu.VMEM((2, width), BF16),
                pltpu.VMEM((3, 3, width), F32),
                pltpu.VMEM((poles, width), F32),
                pltpu.VMEM((rows + 16, LANES), F32),
                pltpu.VMEM((rows + 16, LANES), F32),
                pltpu.VMEM((poles, LANES), F32),
                pltpu.SemaphoreType.DMA((2, groups)),
                pltpu.SemaphoreType.DMA((block[0],)),
                pltpu.SemaphoreType.DMA((3,)),
            ]
            + (
                [
                    pltpu.VMEM(block, F32),
                    pltpu.VMEM(block, F32),
                    pltpu.SemaphoreType.DMA((block[0],)),
                    pltpu.SemaphoreType.DMA((block[0],)),
                ]
                if moved
                else []
            ),
            compiler_params=limit,
            cost_estimate=pl.CostEstimate(flops=4000000, bytes_accessed=8000000, transcendentals=0),
            name="near",
        )(
            lengths,
            query_proj,
            residual,
            far_off(query_rim),
            short_filter,
            decay_rate,
            pole_gain,
            skip,
            far_off(gated) if moved else close_by(gated),
            far_off(local),
        )

    near_a, query_a = near_side(0, groups // 2, gated_a, False)
    near_b, query_b = near_side(groups // 2, groups - groups // 2, gated_b, True)
    pieces, near_a = lax.optimization_barrier((pieces, near_a))
    scanned = pl.pallas_call(
        functools.partial(scan_kernel, rows, poles),
        in_specs=[numbers, near_by, near_by],
        out_specs=near_by,
        out_shape=pltpu.HBM((ranks, held, LANES), F32),
        compiler_params=limit,
        name="rank_scan",
    )(lengths, decay_rate, pieces)
    incoming = lax.all_to_all(scanned, "ctx", 0, 0, tiled=True).reshape(parts, poles, LANES)

    stream, kept, power = pl.pallas_call(
        functools.partial(stream_kernel, rows, poles),
        in_specs=[numbers] + [near_by] * 6 + [outside],
        out_specs=[outside, near_by, near_by],
        out_shape=[pltpu.HBM((rows, width), F32), kept_near(rows, width), kept_near(rows // LANES, LANES)],
        scratch_shapes=[
            pltpu.VMEM((half, rows, LANES), F32),
            pltpu.VMEM((rows + 8, LANES), F32),
            pltpu.VMEM((rows, LANES), F32),
            pltpu.VMEM((poles, LANES), F32),
            pltpu.SemaphoreType.DMA((groups,)),
            pltpu.SemaphoreType.DMA((half,)),
        ],
        compiler_params=limit,
        name="stream",
    )(lengths, decay_rate, pole_gain, incoming, *map(close_by, (near_a, query_a, near_b)), far_off(query_b))
    shares = lax.axis_size("ch")
    powers = jnp.stack([power] + [shifted(power, "ch", i, True) for i in range(1, shares)])
    normed = pl.pallas_call(
        functools.partial(norm_kernel, float(width * shares)),
        in_specs=[near_by, near_by, near_by],
        out_specs=outside,
        out_shape=shape(rows, width),
        scratch_shapes=[
            pltpu.VMEM((rows, LANES), F32),
            pltpu.VMEM((rows, width), F32),
            pltpu.SemaphoreType.DMA((8,)),
        ],
        compiler_params=limit,
        name="norm",
    )(powers, norm_gain.reshape(1, width), close_by(kept))
    return (stream, normed)


def solution(mesh):
    placed = (
        P("ctx", "ch"),
        P("ctx", "ch"),
        P("ctx", "ch"),
        P(None, None, "ch"),
        P(None, "ch"),
        P(None, "ch"),
        P("ch"),
        P("ch"),
        P("ctx", "ch"),
        P(),
    )
    return jax.shard_map(
        on_device,
        mesh=mesh,
        in_specs=placed,
        out_specs=(P("ctx", "ch"), P("ctx", "ch")),
        check_vma=False,
    )
```

time: 375 us -> 73.3 us (0.20)
  other arithmetic: 155 us -> 0.1 us
  waiting for transfers between devices: 111 us -> 11.1 us
  local copies, waits for them, and re-layouts: 75.4 us -> 0.02 us
  Pallas kernels: 0 us -> 32.2 us
  starting transfers between devices: 5.01 us -> 28.7 us
  between operations: 15.3 us -> 0.76 us
  blocking collectives: 8.42 us -> 0 us
    all_gather x2 -> x0, waiting for transfers between devices: 111 us -> none  [carried_in(): pieces = jax.tree.map(lambda part: lax.all_gather(part, axis), value)]
    select_n x63 -> x0, other arithmetic: 67.4 us -> none  [step(): jnp.where(position < mine, new, old)]
    pad x12 -> x0, local copies, waits for them, and re-layouts: 43.2 us -> none  [on_device(): lax.associative_scan(combine_pair, (block_decay, states), axis=0)]
    reduce_sum x6 -> x0, other arithmetic: 34.8 us -> none  [the longest x3 19.4 us: on_device(): partial_out.append(jnp.sum(pole_gain[None] * states, axis=1))]
    add x30 -> x0, other arithmetic: 33.8 us -> none  [the longest x8 15 us: on_device(): lax.associative_scan(combine_pair, (block_decay, states), axis=0)]
    pallas_call x0 -> x7, Pallas kernels: none -> 32.2 us  [the longest x2 13.6 us: near_side(): pl.pallas_call(functools.partial(near_kernel, rows, poles, first), in_spe...]
    all_to_all x0 -> x2, starting transfers between devices: none -> 19.8 us  [the longest x1 13.5 us: on_device(): lax.all_to_all(end.reshape(ranks, held, LANES), 'ctx', 0, 0, tiled=True)]
    unnamed x210 -> x10, local copies, waits for them, and re-layouts: 12.2 us -> 0.02 us
  transfers between devices with their start and end apart: 3 -> 6, of which waited for: 2 -> 5; matrix products, arithmetic and copies ran while one was open for 18% -> 0% of each run, Pallas kernels for 0% -> 19%
where the time goes in v1:
time: 73.3 us; the launch traced here: 72.9 us
  Pallas kernels  32.2 us (44%)
  starting transfers between devices  28.7 us (39%)
  waiting for transfers between devices  11.1 us (15%)
  between operations  0.76 us (1%)
    pallas_call x2, Pallas kernels, near_side(): pl.pallas_call(functools.partial(near_kernel, rows, poles, first), in_spe...  13.6 us
    all_to_all x1, starting transfers between devices, on_device(): lax.all_to_all(end.reshape(ranks, held, LANES), 'ctx', 0, 0, tiled=True)  13.5 us
    pallas_call x1, Pallas kernels, on_device(): pl.pallas_call(functools.partial(end_kernel, rows, poles), in_specs=[numb...  9.46 us
    ppermute x4, starting transfers between devices, shifted(): return lax.ppermute(block, axis, route)  8.92 us
    all_to_all x1, starting transfers between devices, on_device(): lax.all_to_all(scanned, 'ctx', 0, 0, tiled=True)  6.31 us
    pallas_call x1, Pallas kernels, on_device(): pl.pallas_call(functools.partial(stream_kernel, rows, poles), in_specs=[n...  4.65 us
    ppermute x4, waiting for transfers between devices, shifted(): return lax.ppermute(block, axis, route)  4.07 us
    all_to_all x1, waiting for transfers between devices, on_device(): lax.all_to_all(end.reshape(ranks, held, LANES), 'ctx', 0, 0, tiled=True)  4.03 us
  transfers between devices with their start and end apart: 6, of which 5 were waited for; matrix products, arithmetic and copies ran while one was open for 0% of the time, Pallas kernels for 19%

profile of v1, /device:TPU:1, one launch (start us, length us, event | category | flops | bytes accessed | tf_op | source)
XLA Modules:
  0.0 72.9 jit_solution(7077958261983947105)
XLA Ops:
  0.6 0.0 copy-start
  0.6 0.0 copy-start.2
  0.6 1.6 %rims.1 = bf16[3,2,2048]{2,1,0:T(2,128)(2,1)} custom-call(bf16[256,2048]{1,0:T(8,128)(2,1)} %q_hbm.5, bf16[256,2048]{1,0:T(8,128)(2,1)} %k_hbm.3, bf16[256,2048]{1,0:T(8,128)(2,1)} %v_hbm.3), custom_call_target="tpu_custom_call" | custom-call | tf_op jit(solution)/shard_map/rims/pallas_call | solution.py:434
  2.2 0.0 copy-start.4
  2.2 0.0 copy-start.1
  2.3 5.1 %collective-permute-start = (bf16[3,2,2048]{2,1,0:T(2,128)(2,1)}, bf16[3,2,2048]{2,1,0:T(2,128)(2,1)S(1)}, u32[]{:S(2)}, u32[]{:S(2)}) collective-permute-start(bf16[3,2,2048]{2,1,0:T(2,128)(2,1)} %rims.1), channel_id=1, source_target_pairs={{0,4},{4,8},{8,12},{12,16},{16,20},{20,24},{24,28},{28,32},{32,36}... | collective-permute-start | bytes 73736 | tf_op jit(solution)/shard_map/ppermute | solution.py:412
  7.3 1.1 %collective-permute-done.rim_ref = bf16[3,2,2048]{2,1,0:T(2,128)(2,1)S(1)} collective-permute-done((bf16[3,2,2048]{2,1,0:T(2,128)(2,1)}, bf16[3,2,2048]{2,1,0:T(2,128)(2,1)S(1)}, u32[]{:S(2)}, u32[]{:S(2)}) %collective-permute-start) | collective-permute-done | bytes 24608 | tf_op jit(solution)/shard_map/ppermute | solution.py:412
  8.5 0.0 copy-done
  8.5 0.0 copy-done.2
  8.5 9.5 %end_state.1 = (f32[8,256,128]{2,1,0:T(8,128)S(1)}, f32[8,256,128]{2,1,0:T(8,128)}, f32[16,128,128]{2,1,0:T(8,128)}, f32[16,16,128]{2,1,0:T(8,128)}, bf16[2,2048]{1,0:T(2,128)(2,1)}) custom-call(s32[4]{0:T(128)S(1)} %copy-done.2, bf16[256,2048]{1,0:T(8,128)(2,1)} %k_hbm.3, bf16[256,2048]{1,0:T(8,128)(2,1)} %v_hbm.3, ...), custom_call_target="tpu_custom_call" | custom-call | tf_op jit(solution)/shard_map/end_state/pallas_call | solution.py:447
  17.9 13.5 %all-to-all-start = ((f32[64,4,128]{2,1,0:T(4,128)}), f32[64,4,128]{2,1,0:T(4,128)S(1)}, u32[]{:S(2)}, u32[]{:S(2)}) async-start(f32[64,4,128]{2,1,0:T(4,128)} %bitcast), calls=%async_computation | async-start | bytes 262144 | tf_op jit(solution)/shard_map/all_to_all | solution.py:478
  31.4 0.0 copy-done.4
  31.5 0.1 sqrt_multiply_fusion.gain_ref
  31.5 0.0 copy-done.1
  31.6 6.2 %near.2 = (f32[8,256,128]{2,1,0:T(8,128)S(1)}, f32[8,256,128]{2,1,0:T(8,128)S(1)}) custom-call(s32[4]{0:T(128)S(1)} %copy-done.2, bf16[256,2048]{1,0:T(8,128)(2,1)} %q_hbm.5, bf16[256,2048]{1,0:T(8,128)(2,1)} %res_hbm.3, bf16[2,2048]{1,0:T(2,128)(2,1)} %get-tuple-element.17.rim_hbm, f32[3,3,2048]{2,1,0:T(4,128)} %taps_hbm.5, f32[16,2048]{1,0:T(8,128)S(1)} %copy-done, ...), custom_call_target="tpu_custom_call" | custom-call | flops 4000000 | bytes 8000000 | tf_op jit(solution)/shard_map/near/pallas_call | solution.py:482
  37.8 4.0 %all-to-all-done.pieces_ref = f32[64,4,128]{2,1,0:T(4,128)S(1)} async-done(((f32[64,4,128]{2,1,0:T(4,128)}), f32[64,4,128]{2,1,0:T(4,128)S(1)}, u32[]{:S(2)}, u32[]{:S(2)}) %all-to-all-start) | async-done | bytes 131104 | tf_op jit(solution)/shard_map/all_to_all | solution.py:478
  41.8 1.5 %rank_scan.1 = f32[64,4,128]{2,1,0:T(4,128)} custom-call(s32[4]{0:T(128)S(1)} %copy-done.2, f32[16,2048]{1,0:T(8,128)S(1)} %copy-done, f32[64,4,128]{2,1,0:T(4,128)S(1)} %all-to-all-done.pieces_ref), custom_call_target="tpu_custom_call" | custom-call | tf_op jit(solution)/shard_map/rank_scan/pallas_call | solution.py:530
  43.3 6.3 %all-to-all-start.1 = ((f32[64,4,128]{2,1,0:T(4,128)}), f32[64,4,128]{2,1,0:T(4,128)S(1)}, u32[]{:S(2)}, u32[]{:S(2)}) async-start(f32[64,4,128]{2,1,0:T(4,128)} %rank_scan.1), calls=%async_computation.1 | async-start | bytes 262144 | tf_op jit(solution)/shard_map/all_to_all | solution.py:538
  49.6 7.3 %near.3 = (f32[8,256,128]{2,1,0:T(8,128)S(1)}, f32[8,256,128]{2,1,0:T(8,128)}) custom-call(s32[4]{0:T(128)S(1)} %copy-done.2, bf16[256,2048]{1,0:T(8,128)(2,1)} %q_hbm.5, bf16[256,2048]{1,0:T(8,128)(2,1)} %res_hbm.3, bf16[2,2048]{1,0:T(2,128)(2,1)} %get-tuple-element.17.rim_hbm, f32[3,3,2048]{2,1,0:T(4,128)} %taps_hbm.5, f32[16,2048]{1,0:T(8,128)S(1)} %copy-done, ...), custom_call_target="tpu_custom_call" | custom-call | flops 4000000 | bytes 8000000 | tf_op jit(solution)/shard_map/near/pallas_call | solution.py:482
  57.0 3.0 %all-to-all-done.1 = f32[64,4,128]{2,1,0:T(4,128)S(1)} async-done(((f32[64,4,128]{2,1,0:T(4,128)}), f32[64,4,128]{2,1,0:T(4,128)S(1)}, u32[]{:S(2)}, u32[]{:S(2)}) %all-to-all-start.1) | async-done | bytes 131104 | tf_op jit(solution)/shard_map/all_to_all | solution.py:538
  60.0 0.0 copy-start.3
  60.0 4.6 %stream.1 = (f32[256,2048]{1,0:T(8,128)}, f32[256,2048]{1,0:T(8,128)S(1)}, f32[2,128]{1,0:T(2,128)S(1)}) custom-call(s32[4]{0:T(128)S(1)} %copy-done.2, f32[16,2048]{1,0:T(8,128)S(1)} %copy-done, f32[16,2048]{1,0:T(8,128)S(1)} %sqrt_multiply_fusion.gain_ref, f32[16,16,128]{2,1,0:T(8,128)S(1)} %bitcast.8, f32[8,256,128]{2,1,0:T(8,128)S(1)} %get-tuple-element.22.near_a, ...), custom_call_target="tpu_custom_call" | custom-call | tf_op jit(solution)/shard_map/stream/pallas_call | solution.py:540
  64.6 2.8 %collective-permute-start.3 = (f32[2,128]{1,0:T(2,128)S(1)}, f32[2,128]{1,0:T(2,128)S(1)}, u32[]{:S(2)}, u32[]{:S(2)}) collective-permute-start(f32[2,128]{1,0:T(2,128)S(1)} %get-tuple-element.28), channel_id=1, source_target_pairs={{0,3},{1,0},{2,1},{3,2},{4,7},{5,4},{6,5},{7,6},{8,11},{9,8},{10,9... | collective-permute-start | bytes 3080 | tf_op jit(solution)/shard_map/ppermute | solution.py:412
  67.4 0.3 collective-permute-start.2
  67.8 0.7 collective-permute-start.1
  68.5 0.0 collective-permute-done.3
  68.5 2.9 %collective-permute-done.2 = f32[2,128]{1,0:T(2,128)S(1)} collective-permute-done((f32[2,128]{1,0:T(2,128)S(1)}, f32[2,128]{1,0:T(2,128)S(1)}, u32[]{:S(2)}, u32[]{:S(2)}) %collective-permute-start.2) | collective-permute-done | bytes 1056 | tf_op jit(solution)/shard_map/ppermute | solution.py:412
  71.4 0.1 collective-permute-done.1
  71.4 0.0 copy-done.3
  71.4 1.5 %norm.1 = f32[256,2048]{1,0:T(8,128)} custom-call(f32[4,2,128]{2,1,0:T(2,128)S(1)} %pad_maximum_fusion.power_ref, f32[1,2048]{1,0:T(1,128)S(1)} %bitcast.11, f32[256,2048]{1,0:T(8,128)S(1)} %get-tuple-element.29.stream_ref), custom_call_target="tpu_custom_call" | custom-call | tf_op jit(solution)/shard_map/norm/pallas_call | solution.py:558
  (1 shorter events, 0.0 us)
Async XLA Ops:
  0.6 7.8 %copy-start = (f32[16,2048]{1,0:T(8,128)S(1)}, f32[16,2048]{1,0:T(8,128)}, u32[]{:S(2)}) copy-start(f32[16,2048]{1,0:T(8,128)} %rate_ref.3) | copy-start | bytes 393220
  0.6 7.8 %copy-start.2 = (s32[4]{0:T(128)S(1)}, s32[4]{0:T(128)}, u32[]{:S(2)}) copy-start(s32[4]{0:T(128)} %lengths_ref.9) | copy-start | bytes 52
  2.2 29.2 %copy-start.4 = (f32[16,2048]{1,0:T(8,128)S(1)}, f32[16,2048]{1,0:T(8,128)}, u32[]{:S(2)}) copy-start(f32[16,2048]{1,0:T(8,128)} %param.15) | copy-start | bytes 393220
  2.2 29.3 %copy-start.1 = (f32[2048]{0:T(1024)S(1)}, f32[2048]{0:T(1024)}, u32[]{:S(2)}) copy-start(f32[2048]{0:T(1024)} %param.16) | copy-start | bytes 24580
  2.3 6.2 %collective-permute-start = (bf16[3,2,2048]{2,1,0:T(2,128)(2,1)}, bf16[3,2,2048]{2,1,0:T(2,128)(2,1)S(1)}, u32[]{:S(2)}, u32[]{:S(2)}) collective-permute-start(bf16[3,2,2048]{2,1,0:T(2,128)(2,1)} %rims.1), channel_id=1, source_target_pairs={{0,4},{4,8},{8,12},{12,16},{16,20},{20,24},{24,28},{28,32},{32,36}... | collective-permute-start | bytes 73736 | tf_op jit(solution)/shard_map/ppermute | solution.py:412
  17.9 23.9 %all-to-all-start = ((f32[64,4,128]{2,1,0:T(4,128)}), f32[64,4,128]{2,1,0:T(4,128)S(1)}, u32[]{:S(2)}, u32[]{:S(2)}) async-start(f32[64,4,128]{2,1,0:T(4,128)} %bitcast), calls=%async_computation | async-start | bytes 262144 | tf_op jit(solution)/shard_map/all_to_all | solution.py:478
  43.3 16.7 %all-to-all-start.1 = ((f32[64,4,128]{2,1,0:T(4,128)}), f32[64,4,128]{2,1,0:T(4,128)S(1)}, u32[]{:S(2)}, u32[]{:S(2)}) async-start(f32[64,4,128]{2,1,0:T(4,128)} %rank_scan.1), calls=%async_computation.1 | async-start | bytes 262144 | tf_op jit(solution)/shard_map/all_to_all | solution.py:538
  60.0 11.5 %copy-start.3 = (f32[2048]{0:T(1024)S(1)}, f32[2048]{0:T(1024)}, u32[]{:S(2)}) copy-start(f32[2048]{0:T(1024)} %param.17) | copy-start | bytes 24580
  64.6 3.9 %collective-permute-start.3 = (f32[2,128]{1,0:T(2,128)S(1)}, f32[2,128]{1,0:T(2,128)S(1)}, u32[]{:S(2)}, u32[]{:S(2)}) collective-permute-start(f32[2,128]{1,0:T(2,128)S(1)} %get-tuple-element.28), channel_id=1, source_target_pairs={{0,3},{1,0},{2,1},{3,2},{4,7},{5,4},{6,5},{7,6},{8,11},{9,8},{10,9... | collective-permute-start | bytes 3080 | tf_op jit(solution)/shard_map/ppermute | solution.py:412
  67.4 3.9 %collective-permute-start.2 = (f32[2,128]{1,0:T(2,128)S(1)}, f32[2,128]{1,0:T(2,128)S(1)}, u32[]{:S(2)}, u32[]{:S(2)}) collective-permute-start(f32[2,128]{1,0:T(2,128)S(1)} %get-tuple-element.28), channel_id=1, source_target_pairs={{0,2},{1,3},{2,0},{3,1},{4,6},{5,7},{6,4},{7,5},{8,10},{9,11},{10,... | collective-permute-start | bytes 3080 | tf_op jit(solution)/shard_map/ppermute | solution.py:412
  67.8 3.6 %collective-permute-start.1 = (f32[2,128]{1,0:T(2,128)S(1)}, f32[2,128]{1,0:T(2,128)S(1)}, u32[]{:S(2)}, u32[]{:S(2)}) collective-permute-start(f32[2,128]{1,0:T(2,128)S(1)} %get-tuple-element.28), channel_id=1, source_target_pairs={{0,1},{1,2},{2,3},{3,0},{4,5},{5,6},{6,7},{7,4},{8,9},{9,10},{10,1... | collective-permute-start | bytes 3080 | tf_op jit(solution)/shard_map/ppermute | solution.py:412

commit v2 on v1

v2 whole, which is shorter than its diff:
```python
import functools

import jax
import jax.numpy as jnp
from jax import lax
from jax.experimental import pallas as pl
from jax.experimental.pallas import tpu as pltpu
from jax.sharding import PartitionSpec as P

LANES = 128
CHUNKS = 8
GROUP = 256
FIRST_SHARE = 4
HEAD = 2
READY = 6
STEPS = 16
F32 = jnp.float32
BF16 = jnp.bfloat16


def starts_of(lengths_ref):
    first = lengths_ref[0]
    second = first + lengths_ref[1]
    third = second + lengths_ref[2]
    return (first, second, third)


def spread(row):
    return jnp.broadcast_to(row, (CHUNKS, LANES))


def no_start(starts, where):
    kept = jnp.ones(where.shape, jnp.bool_)
    for start in starts:
        kept = kept & (where != start)
    return kept.astype(F32)


def any_in(starts, low, high):
    found = jnp.bool_(False)
    for start in starts:
        found = found | ((start >= low) & (start < high))
    return found


def block_has_start(starts, base, rows, block):
    found = jnp.bool_(False)
    for start in starts:
        inside = start - base
        place = lax.rem(jnp.maximum(inside, 0), rows // CHUNKS)
        found = found | (
            (inside >= 0) & (inside < rows) & (place >= block * STEPS) & (place < (block + 1) * STEPS)
        )
    return found


def lanes_at(part):
    return pl.ds(pl.multiple_of(part * LANES, LANES), LANES)


def chunk_of(place):
    return pl.ds(pl.multiple_of(place * CHUNKS, CHUNKS), CHUNKS)


def lay_out(source, lanes, target, span, offset):
    for piece in range(CHUNKS):
        low = offset + piece * (span + 1)
        target[low : low + span, :] = source[piece * span : (piece + 1) * span, lanes].astype(F32)


def column_copies(sources, targets, sems, group):
    lanes = pl.ds(pl.multiple_of(group * GROUP, GROUP), GROUP)
    return [
        pltpu.make_async_copy(source.at[:, lanes], target.at[:, lanes], sems.at[i, group])
        for i, (source, target) in enumerate(zip(sources, targets))
    ]


def rim_kernel(q_hbm, k_hbm, v_hbm, out_ref, buffer, sems):
    tail = buffer.shape[1]
    copies = [
        pltpu.make_async_copy(source.at[pl.ds(source.shape[0] - tail, tail), :], buffer.at[i], sems.at[i])
        for i, source in enumerate((q_hbm, k_hbm, v_hbm))
    ]
    for copy in copies:
        copy.start()
    for i, copy in enumerate(copies):
        copy.wait()
        out_ref[i] = buffer[i, tail - 2 :, :]


def walk(span, flags, run, carry):
    for block in range(span // STEPS):
        carry = lax.cond(
            flags[block], functools.partial(run, block, True), functools.partial(run, block, False), carry
        )
    return carry


FAR, JOINED, REACHED, AHEAD, FLAGS, BEGUN, INSIDE = (slice(i * CHUNKS, (i + 1) * CHUNKS) for i in (0, 1, 2, 3, 4, 5, 8))
SECTIONS = 11 * CHUNKS


def describe(starts, base, rows, info_ref):
    span = rows // CHUNKS
    chunk = lax.broadcasted_iota(jnp.int32, (CHUNKS, LANES), 0)
    chunk_row = base + chunk * span
    alive = jnp.ones((CHUNKS, LANES), jnp.bool_)
    reached = jnp.ones((CHUNKS, LANES), jnp.bool_)
    ahead = jnp.full((CHUNKS, LANES), span, jnp.int32)
    for start in starts:
        inside = start - chunk_row
        alive = alive & ((inside < 0) | (inside >= span))
        reached = reached & ((start < base) | (inside >= 0))
        ahead = jnp.where((inside >= 0) & (inside < ahead), inside, ahead)
    info_ref[FAR, :] = no_start(starts, chunk_row - 1)
    info_ref[JOINED, :] = (alive & (chunk > 0)).astype(F32)
    info_ref[REACHED, :] = reached.astype(F32)
    info_ref[AHEAD, :] = ahead.astype(F32)
    for block in range(span // STEPS):
        flag = jnp.where(block_has_start(starts, base, rows, block), 1.0, 0.0)
        info_ref[FLAGS.start + block : FLAGS.start + block + 1, :] = jnp.full((1, LANES), flag, F32)
    for i, start in enumerate(starts):
        rank = lax.div(start, rows).astype(F32)
        low = BEGUN.start + i * CHUNKS
        info_ref[low : low + CHUNKS, :] = jnp.full((CHUNKS, LANES), rank, F32)
        low = INSIDE.start + i * CHUNKS
        info_ref[low : low + CHUNKS, :] = (start - chunk_row).astype(F32)


def pitched(row, span):
    return row + lax.div(row, span)


def end_kernel(rows, poles, lengths_hbm, k_hbm, v_hbm, q_hbm, res_hbm, rim_ref, taps_hbm, rate_hbm, gated_a, gated_hbm, end_hbm, q_next, r_next, rim_next, taps_next, info_ref, lengths_ref, k_ref, v_ref, gated_b, end_ref, taps_ref, rate_ref, kx, vx, gx, decay_ref, sems, out_sems, end_sems, small_sems):
    span = rows // CHUNKS
    base = lax.axis_index("ctx") * rows
    phase = lax.broadcasted_iota(jnp.int32, (CHUNKS, LANES), 0)
    small = [
        pltpu.make_async_copy(source, target, small_sems.at[i])
        for i, (source, target) in enumerate(((lengths_hbm, lengths_ref), (taps_hbm, taps_ref), (rate_hbm, rate_ref)))
    ]
    columns = pl.ds(0, q_next.shape[1])
    ahead_of_time = [
        pltpu.make_async_copy(source.at[:, columns], target, small_sems.at[len(small) + i])
        for i, (source, target) in enumerate(((q_hbm, q_next), (res_hbm, r_next)))
    ]
    groups = k_ref.shape[1] // GROUP
    for copy in small:
        copy.start()
    for group in range(groups):
        for copy in column_copies((k_hbm, v_hbm), (k_ref, v_ref), sems, group):
            copy.start()
    for copy in ahead_of_time:
        copy.start()
    rim_next[...] = rim_ref[0]
    for copy in small:
        copy.wait()
    taps_next[...] = taps_ref[0]
    starts = starts_of(lengths_ref)
    touched = any_in(starts, base - 1, base + rows)
    last = jnp.int32(0)
    for start in starts:
        last = jnp.where((start >= base) & (start < base + rows), start - base, last)
    describe(starts, base, rows, info_ref)
    inner = GROUP // LANES

    def store(here):
        return pltpu.make_async_copy(gated_b.at[here], gated_hbm.at[here], out_sems.at[here])

    def send(group):
        here = pl.ds(group * inner, inner)
        return pltpu.make_async_copy(end_ref.at[here], end_hbm.at[here], end_sems.at[group])

    def one_group(group, first, gated_ref):
        for copy in column_copies((k_hbm, v_hbm), (k_ref, v_ref), sems, group):
            copy.wait()

        @pl.loop(group * inner, (group + 1) * inner)
        def _(part):
            lanes = lanes_at(part)
            here = part - first * inner
            for i, source, target in ((1, k_ref, kx), (2, v_ref, vx)):
                target[6:8, :] = rim_ref[i, :, lanes].astype(F32)
                target[8:, :] = source[:, lanes].astype(F32)
            decay_ref[...] = jnp.exp(-float(CHUNKS) * rate_ref[:, lanes])
            lines = [[taps_ref[i, j : j + 1, lanes] for j in range(3)] for i in (1, 2)]
            taps = [[spread(line) for line in three] for three in lines]
            for block in range(rows // CHUNKS):
                low = block * CHUNKS
                shorts = []
                for three, source in zip(taps, (kx, vx)):
                    short = three[0] * source[low + 8 : low + 16, :]
                    for back in (1, 2):
                        short = short + three[back] * source[low + 8 - back : low + 16 - back, :]
                    shorts.append(short)
                gated = shorts[0] * shorts[1]
                gx[low : low + CHUNKS, :] = gated
                to = low + low // span
                gated_ref[here, to : to + CHUNKS, :] = gated

            @pl.when(touched)
            def _():
                for start in starts:
                    inside = start - base

                    def mend(row, reach):
                        shorts = []
                        for three, source in zip(lines, (kx, vx)):
                            short = three[0] * source[pl.ds(row + 8, 1), :]
                            if reach:
                                short = short + three[1] * source[pl.ds(row + 7, 1), :]
                            shorts.append(short)
                        gated = shorts[0] * shorts[1]
                        gx[pl.ds(row, 1), :] = gated
                        gated_ref[here, pl.ds(pitched(row, span), 1), :] = gated

                    @pl.when((inside >= 0) & (inside < rows))
                    def _():
                        mend(inside, False)

                    @pl.when((inside >= -1) & (inside < rows - 1))
                    def _():
                        mend(inside + 1, True)

                for block in range(rows // CHUNKS):
                    low = block * CHUNKS
                    gx[low : low + CHUNKS, :] = jnp.where(
                        phase + low >= last, gx[low : low + CHUNKS, :], 0.0
                    )

            decay = [spread(decay_ref[m : m + 1, :]) for m in range(poles)]
            sums = [gx[:CHUNKS, :] for _ in range(poles)]
            for block in range(1, rows // CHUNKS):
                gated = gx[block * CHUNKS : (block + 1) * CHUNKS, :]
                sums = [decay[m] * sums[m] + gated for m in range(poles)]
            after = (phase - (CHUNKS - 1)).astype(F32)
            for m in range(poles):
                weight = jnp.exp(after * spread(rate_ref[m : m + 1, lanes]))
                end_ref[part, m : m + 1, :] = jnp.sum(weight * sums[m], axis=0, keepdims=True)
            if first:
                store(here).start()

        send(group).start()

    middle = gated_a.shape[0] // inner
    pl.loop(0, middle)(lambda group: one_group(group, 0, gated_a))
    pl.loop(middle, groups)(lambda group: one_group(group, middle, gated_b))
    for copy in ahead_of_time:
        copy.wait()
    for here in range(gated_b.shape[0]):
        store(here).wait()
    for group in range(groups):
        send(group).wait()


def rank_factors(info_ref, rows, poles, rate_ref, out_ref):
    ranks, held = out_ref.shape[:2]
    shares = poles // held
    mine = lax.axis_index("ctx")
    lanes = lanes_at(lax.div(mine, shares))
    rate = rate_ref[:held, lanes]
    for share in range(1, shares):
        theirs = rate_ref[share * held : (share + 1) * held, lanes]
        rate = jnp.where(lax.rem(mine, shares) == share, theirs, rate)
    whole = jnp.exp(-float(rows) * rate)
    begun = [info_ref[BEGUN.start + i * CHUNKS : BEGUN.start + i * CHUNKS + held, :] for i in range(3)]
    for rank in range(ranks):
        kept = whole
        for begin in begun:
            kept = jnp.where(begin == float(rank), 0.0, kept)
        out_ref[rank] = kept


def scan_kernel(factor_ref, pieces_ref, out_ref):
    running = jnp.zeros(pieces_ref.shape[1:], F32)
    for rank in range(pieces_ref.shape[0]):
        out_ref[rank] = running
        running = factor_ref[rank] * running + pieces_ref[rank]


def near_kernel(rows, poles, first, early, info_ref, rim_ref, taps_ref, rate_ref, gain_ref, skip_ref, gated_in, q_in, r_in, q_hbm, res_hbm, gated_hbm, *others):
    if early:
        outs, (factor_ref, gated_next, q_next, r_next, *others) = others[:3], others[3:]
        near_ref, query_ref, local_ref, q_ref, r_ref, qx, rx, decay_ref, own_sems, far_sems, next_sems = others
        gated_ref = gated_in
        count = near_ref.shape[0]
    else:
        heads, tails, others = others[:3], others[3:6], others[6:]
        gated_ref, near_ref, query_ref, local_ref, q_ref, r_ref, qx, rx, decay_ref, own_sems, far_sems = others
        count = near_ref.shape[0]

    def fetch(here):
        pairs = [(q_hbm.at[:, lanes_at(first + here)], q_ref.at[:, lanes_at(here)])]
        pairs.append((res_hbm.at[:, lanes_at(first + here)], r_ref.at[:, lanes_at(here)]))
        if not early:
            pairs.append((gated_hbm.at[here], gated_ref.at[here]))
        return [
            pltpu.make_async_copy(source, target, own_sems.at[i, here])
            for i, (source, target) in enumerate(pairs)
        ]

    for here in range(HEAD, count):
        for copy in fetch(here):
            copy.start()
    for i, (source, target) in enumerate(((q_in, q_ref), (r_in, r_ref))):
        target[:, : HEAD * LANES] = source[...]
    if early:
        columns = pl.ds((first + count) * LANES, HEAD * LANES)
        pairs = (
            (gated_hbm.at[pl.ds(0, HEAD)], gated_next),
            (q_hbm.at[:, columns], q_next),
            (res_hbm.at[:, columns], r_next),
        )
        ahead_of_time = [
            pltpu.make_async_copy(source, target, next_sems.at[i]) for i, (source, target) in enumerate(pairs)
        ]
        for copy in ahead_of_time:
            copy.start()
        rank_factors(info_ref, rows, poles, rate_ref, factor_ref)
    else:
        gated_ref[:HEAD] = gated_in[...]
    span = rows // CHUNKS
    chunk = lax.broadcasted_iota(jnp.int32, (CHUNKS, LANES), 0)
    flags = [
        jnp.max(info_ref[FLAGS.start + block : FLAGS.start + block + 1, :]) > 0.0
        for block in range(span // STEPS)
    ]

    made = (near_ref, query_ref, local_ref)

    def store(here, targets, low):
        return [
            pltpu.make_async_copy(source.at[here], target.at[here - low], far_sems.at[i, here])
            for i, (source, target) in enumerate(zip(made, targets))
        ]

    @pl.loop(0, count)
    def _(here):
        own = lanes_at(here)
        lanes = lanes_at(here + first)
        far = info_ref[FAR, :]
        joined = info_ref[JOINED, :]

        @pl.when(here >= HEAD)
        def _():
            for copy in fetch(here):
                copy.wait()

        qx[5:7, :] = rim_ref[:, lanes].astype(F32)
        lay_out(q_ref, own, qx, span, 8)
        lay_out(r_ref, own, rx, span, 0)
        decay_ref[...] = jnp.exp(-rate_ref[:, lanes])
        taps = [spread(taps_ref[j : j + 1, lanes]) for j in range(3)]
        skip = spread(skip_ref[:, lanes])
        decay = [spread(decay_ref[m : m + 1, :]) for m in range(poles)]
        gain = [spread(gain_ref[m : m + 1, lanes]) for m in range(poles)]
        carry = [
            qx[pl.ds(6, CHUNKS, stride=span + 1), :],
            qx[pl.ds(5, CHUNKS, stride=span + 1), :] * far,
        ] + [jnp.zeros((CHUNKS, LANES), F32)] * poles

        def run(block, masked, carry):
            carry = list(carry)
            for step in range(STEPS):
                place = block * STEPS + step
                if masked:
                    keep = jnp.ones((CHUNKS, LANES), F32)
                    for i in range(3):
                        low = INSIDE.start + i * CHUNKS
                        keep = jnp.where(info_ref[low : low + CHUNKS, :] == float(place), 0.0, keep)
                    carry = [held * keep for held in carry]
                query = qx[pl.ds(8 + place, CHUNKS, stride=span + 1), :]
                query_short = taps[0] * query + taps[1] * carry[0] + taps[2] * carry[1]
                gated = gated_ref[here, pl.ds(place, CHUNKS, stride=span + 1), :]
                states = [decay[m] * carry[2 + m] + gated for m in range(poles)]
                total = skip * gated
                for m in range(poles):
                    total = total + gain[m] * states[m]
                query_ref[here, chunk_of(place), :] = query_short
                near_ref[here, chunk_of(place), :] = (
                    rx[pl.ds(place, CHUNKS, stride=span + 1), :] + query_short * total
                )
                carry = [query, carry[0]] + states
            return tuple(carry)

        carry = walk(span, flags, run, tuple(carry))
        for m in range(poles):
            reach = jnp.exp(-float(span) * spread(rate_ref[m : m + 1, lanes])) * joined
            state = carry[2 + m]
            for hop in (1, 2, 4):
                state = state + reach * pltpu.roll(state, hop, 0)
                if hop < 4:
                    reach = reach * pltpu.roll(reach, hop, 0)
            local_ref[here, m * CHUNKS : (m + 1) * CHUNKS, :] = jnp.where(
                chunk > 0, pltpu.roll(state, 1, 0), 0.0
            )
        if early:
            for copy in store(here, outs, 0):
                copy.start()
        else:

            @pl.when(here < READY)
            def _():
                for source, target in zip(made, heads):
                    target[here] = source[here]

            @pl.when(here >= READY)
            def _():
                for copy in store(here, tails, READY):
                    copy.start()

    if early:
        for copy in ahead_of_time:
            copy.wait()
    for here in range(0 if early else READY, count):
        for copy in store(here, outs, 0) if early else store(here, tails, READY):
            copy.wait()


def stream_kernel(rows, poles, info_ref, rate_ref, gain_ref, incoming_ref, near_hbm, query_hbm, local_hbm, near_head, query_head, local_head, near_rest, query_rest, local_rest, out_hbm, stream_ref, power_ref, near_a, query_a, local_a, near_b, query_b, local_b, sx, px, decay_ref, sems, far_sems, rest_sems):
    span = rows // CHUNKS
    chunk = lax.broadcasted_iota(jnp.int32, (CHUNKS, LANES), 0)
    px[...] = jnp.zeros_like(px)
    inner = GROUP // LANES
    early = near_a.shape[0]

    def fetch(group):
        here = pl.ds(group * inner, inner)
        pairs = ((near_hbm, near_a), (query_hbm, query_a), (local_hbm, local_a))
        return [
            pltpu.make_async_copy(source.at[here], target.at[here], far_sems.at[i, group])
            for i, (source, target) in enumerate(pairs)
        ]

    pairs = ((near_rest, near_b), (query_rest, query_b), (local_rest, local_b))
    rest = [pltpu.make_async_copy(source, target, rest_sems.at[i]) for i, (source, target) in enumerate(pairs)]
    for group in range(early // inner):
        for copy in fetch(group):
            copy.start()
    for copy in rest:
        copy.start()
    before = (chunk * span).astype(F32)

    def copy_out(group):
        lanes = pl.ds(pl.multiple_of(group * GROUP, GROUP), GROUP)
        return pltpu.make_async_copy(stream_ref.at[:, lanes], out_hbm.at[:, lanes], sems.at[group])

    def one_part(part, near_ref, query_ref, local_ref, place_of):
        lanes = lanes_at(part)
        decay_ref[...] = jnp.exp(-rate_ref[:, lanes])
        decay = [spread(decay_ref[m : m + 1, :]) for m in range(poles)]
        reached = info_ref[REACHED, :]
        ahead = info_ref[AHEAD, :]
        carry = []
        for m in range(poles):
            entering = reached * jnp.exp(-before * spread(rate_ref[m : m + 1, lanes]))
            entering = entering * spread(incoming_ref[part, m : m + 1, :])
            entering = entering + local_ref[place_of, m * CHUNKS : (m + 1) * CHUNKS, :]
            carry.append(spread(gain_ref[m : m + 1, lanes]) * entering)
        for place in range(span):
            carry = [decay[m] * carry[m] for m in range(poles)]
            terms = list(carry)
            while len(terms) > 1:
                terms = [
                    terms[i] + terms[i + 1] if i + 1 < len(terms) else terms[i]
                    for i in range(0, len(terms), 2)
                ]
            carried = jnp.where(ahead > float(place), terms[0], 0.0)
            here = chunk_of(place)
            sx[pl.ds(place, CHUNKS, stride=span + 1), :] = (
                near_ref[place_of, here, :] + query_ref[place_of, here, :] * carried
            )
        for piece in range(CHUNKS):
            low = piece * (span + 1)
            stream = sx[low : low + span, :]
            native = slice(piece * span, (piece + 1) * span)
            stream_ref[native, lanes] = stream
            px[native, :] += stream * stream

    groups = stream_ref.shape[1] // GROUP
    sides = (
        (early, near_head, query_head, local_head),
        (0, near_a, query_a, local_a),
        (early + READY, near_b, query_b, local_b),
    )
    for first, near_ref, query_ref, local_ref in sides:

        @pl.loop(0, near_ref.shape[0] // inner)
        def _(group):
            if near_ref is near_a:
                for copy in fetch(group):
                    copy.wait()
            if near_ref is near_b:
                for copy in rest:
                    copy.wait()

            @pl.loop(group * inner, (group + 1) * inner)
            def _(part):
                one_part(part + first, near_ref, query_ref, local_ref, part)

            copy_out(group + first // inner).start()

    for piece in range(rows // LANES):
        turned = px[piece * LANES : (piece + 1) * LANES, :].T
        power_ref[piece : piece + 1, :] = jnp.sum(turned, axis=0, keepdims=True)
    for group in range(groups):
        copy_out(group).wait()


def norm_kernel(width, power_ref, gain_ref, stream_ref, out_hbm, scale_ref, buffer, sems):
    scale = lax.rsqrt(jnp.sum(power_ref[...], axis=0) / width + 1e-06)
    for piece in range(scale.shape[0]):
        wide = jnp.broadcast_to(scale[piece : piece + 1, :], (LANES, LANES))
        scale_ref[piece * LANES : (piece + 1) * LANES, :] = wide.T
    rows = stream_ref.shape[0]
    count = sems.shape[0]
    tall = rows // count

    def copy_out(group):
        here = pl.ds(pl.multiple_of(group * tall, tall), tall)
        return pltpu.make_async_copy(buffer.at[here, :], out_hbm.at[here, :], sems.at[group])

    @pl.loop(0, count)
    def _(group):
        here = pl.ds(pl.multiple_of(group * tall, tall), tall)
        factor = scale_ref[here, :]
        for part in range(stream_ref.shape[1] // LANES):
            lanes = slice(part * LANES, (part + 1) * LANES)
            buffer[here, lanes] = stream_ref[here, lanes] * factor * gain_ref[:, lanes]
        copy_out(group).start()

    for group in range(count):
        copy_out(group).wait()


def shifted(block, axis, distance, wrap):
    count = lax.axis_size(axis)
    route = [(i, (i + distance) % count) for i in range(count) if wrap or i + distance < count]
    return lax.ppermute(block, axis, route)


def on_device(query_proj, key_proj, value_proj, short_filter, decay_rate, residue, skip_gain, norm_gain, residual, lengths):
    rows, width = query_proj.shape
    poles = decay_rate.shape[0]
    ranks = lax.axis_size("ctx")
    parts = width // LANES
    groups = width // GROUP
    near_by = pl.BlockSpec(memory_space=pltpu.VMEM)
    outside = pl.BlockSpec(memory_space=pltpu.HBM)
    limit = pltpu.CompilerParams(vmem_limit_bytes=12 * 1024 * 1024)
    shape = lambda *dims: jax.ShapeDtypeStruct(dims, F32)
    kept_near = lambda *dims: pltpu.VMEM(dims, F32)
    far_off = lambda array: pltpu.with_memory_space_constraint(array, pltpu.HBM)
    close_by = lambda array: pltpu.with_memory_space_constraint(array, pltpu.VMEM)
    query_proj, key_proj, value_proj, residual, short_filter, lengths = map(
        far_off, (query_proj, key_proj, value_proj, residual, short_filter, lengths)
    )

    rims = pl.pallas_call(
        rim_kernel,
        in_specs=[outside] * 3,
        out_specs=near_by,
        out_shape=pltpu.VMEM((3, 2, width), BF16),
        scratch_shapes=[pltpu.VMEM((3, 16, width), BF16), pltpu.SemaphoreType.DMA((3,))],
        name="rims",
    )(query_proj, key_proj, value_proj)
    rims = shifted(rims, "ctx", 1, False)
    pole_gain = residue * jnp.sqrt(-jnp.expm1(-2.0 * decay_rate))
    skip = skip_gain.reshape(1, width)

    early = FIRST_SHARE * (GROUP // LANES)
    late = parts - early
    pitch = rows + CHUNKS
    held = parts * poles // ranks
    gated_a, gated_b, end, q_a, r_a, query_rim, query_taps, info = pl.pallas_call(
        functools.partial(end_kernel, rows, poles),
        in_specs=[outside] * 5 + [near_by, outside, outside],
        out_specs=[near_by, outside, outside] + [near_by] * 5,
        out_shape=[
            kept_near(early, pitch, LANES),
            pltpu.HBM((late, pitch, LANES), F32),
            pltpu.HBM((parts, poles, LANES), F32),
            pltpu.VMEM((rows, HEAD * LANES), BF16),
            pltpu.VMEM((rows, HEAD * LANES), BF16),
            pltpu.VMEM((2, width), BF16),
            kept_near(3, width),
            kept_near(SECTIONS, LANES),
        ],
        scratch_shapes=[
            pltpu.SMEM(lengths.shape, jnp.int32),
            pltpu.VMEM((rows, width), BF16),
            pltpu.VMEM((rows, width), BF16),
            pltpu.VMEM((late, pitch, LANES), F32),
            pltpu.VMEM((parts, poles, LANES), F32),
            pltpu.VMEM((3, 3, width), F32),
            pltpu.VMEM((poles, width), F32),
            pltpu.VMEM((rows + 8, LANES), F32),
            pltpu.VMEM((rows + 8, LANES), F32),
            pltpu.VMEM((rows, LANES), F32),
            pltpu.VMEM((poles, LANES), F32),
            pltpu.SemaphoreType.DMA((2, groups)),
            pltpu.SemaphoreType.DMA((late,)),
            pltpu.SemaphoreType.DMA((groups,)),
            pltpu.SemaphoreType.DMA((5,)),
        ],
        compiler_params=limit,
        name="end_state",
    )(lengths, key_proj, value_proj, query_proj, residual, rims, short_filter, decay_rate)
    info, query_rim, query_taps = map(close_by, (info, query_rim, query_taps))

    pieces = lax.all_to_all(end.reshape(ranks, held, LANES), "ctx", 0, 0, tiled=True)

    def near_side(first, count, gated, q_part, r_part, early):
        block = (count, rows, LANES)
        states = (count, poles * CHUNKS, LANES)
        given = [info, query_rim, query_taps, decay_rate, pole_gain, skip, *map(close_by, (gated, q_part, r_part))]
        fetched = [query_proj, residual, far_off(gated_b)]
        scratch = [
            pltpu.VMEM((rows, count * LANES), BF16),
            pltpu.VMEM((rows, count * LANES), BF16),
            pltpu.VMEM((rows + 16, LANES), F32),
            pltpu.VMEM((rows + 16, LANES), F32),
            pltpu.VMEM((poles, LANES), F32),
            pltpu.SemaphoreType.DMA((3, count)),
            pltpu.SemaphoreType.DMA((3, count)),
        ]
        if early:
            out_specs = [outside] * 3 + [near_by] * 4
            out_shape = [pltpu.HBM(dims, F32) for dims in (block, block, states)] + [
                kept_near(ranks, held, LANES),
                kept_near(HEAD, pitch, LANES),
                pltpu.VMEM((rows, HEAD * LANES), BF16),
                pltpu.VMEM((rows, HEAD * LANES), BF16),
            ]
            scratch = [pltpu.VMEM(dims, F32) for dims in (block, block, states)] + scratch
            scratch += [pltpu.SemaphoreType.DMA((3,))]
        else:
            out_specs = [near_by] * 3 + [outside] * 3
            out_shape = [kept_near(READY, *dims[1:]) for dims in (block, block, states)]
            out_shape += [pltpu.HBM((count - READY, *dims[1:]), F32) for dims in (block, block, states)]
            scratch = [pltpu.VMEM(dims, F32) for dims in ((count, pitch, LANES), block, block, states)] + scratch
        return pl.pallas_call(
            functools.partial(near_kernel, rows, poles, first, early),
            in_specs=[near_by] * len(given) + [outside] * len(fetched),
            out_specs=out_specs,
            out_shape=out_shape,
            scratch_shapes=scratch,
            compiler_params=limit,
            cost_estimate=pl.CostEstimate(flops=4000000, bytes_accessed=8000000, transcendentals=0),
            name="near",
        )(*given, *fetched)

    near_a, query_a, local_a, factors, gated_head, q_b, r_b = near_side(0, early, gated_a, q_a, r_a, True)
    near_b = near_side(early, late, gated_head, q_b, r_b, False)
    scanned = pl.pallas_call(
        scan_kernel,
        in_specs=[near_by, near_by],
        out_specs=near_by,
        out_shape=pltpu.HBM((ranks, held, LANES), F32),
        compiler_params=limit,
        name="rank_scan",
    )(close_by(factors), pieces)
    incoming = lax.all_to_all(scanned, "ctx", 0, 0, tiled=True).reshape(parts, poles, LANES)

    stream, kept, power = pl.pallas_call(
        functools.partial(stream_kernel, rows, poles),
        in_specs=[near_by] * 4 + [outside] * 3 + [near_by] * 3 + [outside] * 3,
        out_specs=[outside, near_by, near_by],
        out_shape=[pltpu.HBM((rows, width), F32), kept_near(rows, width), kept_near(rows // LANES, LANES)],
        scratch_shapes=[
            pltpu.VMEM((early, rows, LANES), F32),
            pltpu.VMEM((early, rows, LANES), F32),
            pltpu.VMEM((early, poles * CHUNKS, LANES), F32),
            pltpu.VMEM((late - READY, rows, LANES), F32),
            pltpu.VMEM((late - READY, rows, LANES), F32),
            pltpu.VMEM((late - READY, poles * CHUNKS, LANES), F32),
            pltpu.VMEM((rows + 8, LANES), F32),
            pltpu.VMEM((rows, LANES), F32),
            pltpu.VMEM((poles, LANES), F32),
            pltpu.SemaphoreType.DMA((groups,)),
            pltpu.SemaphoreType.DMA((3, early // (GROUP // LANES))),
            pltpu.SemaphoreType.DMA((3,)),
        ],
        compiler_params=limit,
        name="stream",
    )(
        info,
        decay_rate,
        pole_gain,
        incoming,
        *map(far_off, (near_a, query_a, local_a)),
        *map(close_by, near_b[:3]),
        *map(far_off, near_b[3:]),
    )
    shares = lax.axis_size("ch")
    powers = jnp.stack([power] + [shifted(power, "ch", i, True) for i in range(1, shares)])
    normed = pl.pallas_call(
        functools.partial(norm_kernel, float(width * shares)),
        in_specs=[near_by, near_by, near_by],
        out_specs=outside,
        out_shape=shape(rows, width),
        scratch_shapes=[
            pltpu.VMEM((rows, LANES), F32),
            pltpu.VMEM((rows, width), F32),
            pltpu.SemaphoreType.DMA((8,)),
        ],
        compiler_params=limit,
        name="norm",
    )(powers, norm_gain.reshape(1, width), close_by(kept))
    return (stream, normed)


def solution(mesh):
    placed = (
        P("ctx", "ch"),
        P("ctx", "ch"),
        P("ctx", "ch"),
        P(None, None, "ch"),
        P(None, "ch"),
        P(None, "ch"),
        P("ch"),
        P("ch"),
        P("ctx", "ch"),
        P(),
    )
    return jax.shard_map(
        on_device,
        mesh=mesh,
        in_specs=placed,
        out_specs=(P("ctx", "ch"), P("ctx", "ch")),
        check_vma=False,
    )
```

time: 73.3 us -> 67.4 us (0.920)
  Pallas kernels: 32.2 us -> 23.9 us
  waiting for transfers between devices: 11.1 us -> 14.4 us
  starting transfers between devices: 28.7 us -> 27.5 us
    pallas_call x4, Pallas kernels: 24.5 us -> 17.3 us  [the longest x2 10.1 us: near_side(): pl.pallas_call(functools.partial(near_kernel, rows, poles, first, early),...]
    all_to_all x1, waiting for transfers between devices: 3.01 us -> 5.26 us  [on_device(): lax.all_to_all(scanned, 'ctx', 0, 0, tiled=True)]
    all_to_all x1, starting transfers between devices: 6.31 us -> 5.1 us  [on_device(): lax.all_to_all(scanned, 'ctx', 0, 0, tiled=True)]
    all_to_all x1, waiting for transfers between devices: 4.03 us -> 5.24 us  [on_device(): lax.all_to_all(end.reshape(ranks, held, LANES), 'ctx', 0, 0, tiled=True)]
  transfers between devices with their start and end apart: 6 -> 6, of which waited for: 5 -> 5; matrix products, arithmetic and copies ran while one was open for 0% -> 0% of each run, Pallas kernels for 19% -> 15%
where the time goes in v2:
time: 67.4 us; the launch traced here: 66.6 us
  starting transfers between devices  27.5 us (41%)
  Pallas kernels  23.9 us (35%)
  waiting for transfers between devices  14.4 us (21%)
  between operations  0.75 us (1%)
    all_to_all x1, starting transfers between devices, on_device(): lax.all_to_all(end.reshape(ranks, held, LANES), 'ctx', 0, 0, tiled=True)  13.5 us
    pallas_call x2, Pallas kernels, near_side(): pl.pallas_call(functools.partial(near_kernel, rows, poles, first, early),...  10.1 us
    ppermute x4, starting transfers between devices, shifted(): return lax.ppermute(block, axis, route)  8.92 us
    pallas_call x1, Pallas kernels, on_device(): pl.pallas_call(functools.partial(end_kernel, rows, poles), in_specs=[outs...  6.38 us
    all_to_all x1, waiting for transfers between devices, on_device(): lax.all_to_all(scanned, 'ctx', 0, 0, tiled=True)  5.26 us
    all_to_all x1, waiting for transfers between devices, on_device(): lax.all_to_all(end.reshape(ranks, held, LANES), 'ctx', 0, 0, tiled=True)  5.24 us
    all_to_all x1, starting transfers between devices, on_device(): lax.all_to_all(scanned, 'ctx', 0, 0, tiled=True)  5.1 us
    pallas_call x1, Pallas kernels, on_device(): pl.pallas_call(functools.partial(stream_kernel, rows, poles), in_specs=[n...  4.13 us
  transfers between devices with their start and end apart: 6, of which 5 were waited for; matrix products, arithmetic and copies ran while one was open for 0% of the time, Pallas kernels for 15%

profile of v2, /device:TPU:1, one launch (start us, length us, event | category | flops | bytes accessed | tf_op | source)
XLA Modules:
  0.0 66.6 jit_solution(13899146505023036786)
XLA Ops:
  0.6 0.0 copy-start
  0.6 1.0 %rims.1 = bf16[3,2,2048]{2,1,0:T(2,128)(2,1)S(1)} custom-call(bf16[256,2048]{1,0:T(8,128)(2,1)} %q_hbm.7, bf16[256,2048]{1,0:T(8,128)(2,1)} %k_hbm.3, bf16[256,2048]{1,0:T(8,128)(2,1)} %v_hbm.3), custom_call_target="tpu_custom_call" | custom-call | tf_op jit(solution)/shard_map/rims/pallas_call | solution.py:560
  1.6 0.0 copy-start.3
  1.6 0.0 copy-start.1
  1.6 5.1 %collective-permute-start = (bf16[3,2,2048]{2,1,0:T(2,128)(2,1)S(1)}, bf16[3,2,2048]{2,1,0:T(2,128)(2,1)S(1)}, u32[]{:S(2)}, u32[]{:S(2)}) collective-permute-start(bf16[3,2,2048]{2,1,0:T(2,128)(2,1)S(1)} %rims.1), channel_id=1, source_target_pairs={{0,4},{4,8},{8,12},{12,16},{16,20},{20,24},{24,28},{28,32},{32,36}... | collective-permute-start | bytes 73736 | tf_op jit(solution)/shard_map/ppermute | solution.py:540
  6.7 0.9 %collective-permute-done.rim_ref = bf16[3,2,2048]{2,1,0:T(2,128)(2,1)S(1)} collective-permute-done((bf16[3,2,2048]{2,1,0:T(2,128)(2,1)S(1)}, bf16[3,2,2048]{2,1,0:T(2,128)(2,1)S(1)}, u32[]{:S(2)}, u32[]{:S(2)}) %collective-permute-start) | collective-permute-done | bytes 24608 | tf_op jit(solution)/shard_map/ppermute | solution.py:540
  7.6 0.0 copy-done
  7.6 6.4 %end_state.1 = (f32[8,264,128]{2,1,0:T(8,128)S(1)}, f32[8,264,128]{2,1,0:T(8,128)}, f32[16,16,128]{2,1,0:T(8,128)}, bf16[256,256]{1,0:T(8,128)(2,1)S(1)}, bf16[2...) custom-call(s32[4]{0:T(128)} %lengths_hbm.1, ...), custom_call_target="tpu_custom_call" | custom-call | tf_op jit(solution)/shard_map/end_state/pallas_call | solution.py:576
  14.0 13.5 %all-to-all-start = ((f32[64,4,128]{2,1,0:T(4,128)}), f32[64,4,128]{2,1,0:T(4,128)S(1)}, u32[]{:S(2)}, u32[]{:S(2)}) async-start(f32[64,4,128]{2,1,0:T(4,128)} %bitcast.13), calls=%async_computation | async-start | bytes 262144 | tf_op jit(solution)/shard_map/all_to_all | solution.py:612
  27.5 0.0 copy-done.3
  27.5 0.1 sqrt_multiply_fusion.gain_ref
  27.6 0.0 copy-done.1
  27.6 5.0 %near.2 = (f32[8,256,128]{2,1,0:T(8,128)}, f32[8,256,128]{2,1,0:T(8,128)}, f32[8,128,128]{2,1,0:T(8,128)}, f32[64,4,128]{2,1,0:T(4,128)S(1)}, f32[2,264,128]{2,1...) custom-call(f32[88,128]{1,0:T(8,128)S(1)} %get-tuple-element.26.info_ref, ...), custom_call_target="tpu_custom_call" | custom-call | flops 4000000 | bytes 8000000 | tf_op jit(solution)/shard_map/near/pallas_call | solution.py:643
  32.7 5.2 %all-to-all-done.pieces_ref = f32[64,4,128]{2,1,0:T(4,128)S(1)} async-done(((f32[64,4,128]{2,1,0:T(4,128)}), f32[64,4,128]{2,1,0:T(4,128)S(1)}, u32[]{:S(2)}, u32[]{:S(2)}) %all-to-all-start) | async-done | bytes 131104 | tf_op jit(solution)/shard_map/all_to_all | solution.py:612
  37.9 0.8 %rank_scan.1 = f32[64,4,128]{2,1,0:T(4,128)} custom-call(f32[64,4,128]{2,1,0:T(4,128)S(1)} %get-tuple-element.33.factor_ref, f32[64,4,128]{2,1,0:T(4,128)S(1)} %all-to-all-done.pieces_ref), custom_call_target="tpu_custom_call" | custom-call | tf_op jit(solution)/shard_map/rank_scan/pallas_call | solution.py:656
  38.7 5.1 %all-to-all-start.1 = ((f32[64,4,128]{2,1,0:T(4,128)}), f32[64,4,128]{2,1,0:T(4,128)S(1)}, u32[]{:S(2)}, u32[]{:S(2)}) async-start(f32[64,4,128]{2,1,0:T(4,128)} %rank_scan.1), calls=%async_computation.1 | async-start | bytes 262144 | tf_op jit(solution)/shard_map/all_to_all | solution.py:664
  43.8 5.1 %near.3 = (f32[6,256,128]{2,1,0:T(8,128)S(1)}, f32[6,256,128]{2,1,0:T(8,128)S(1)}, f32[6,128,128]{2,1,0:T(8,128)S(1)}, f32[2,256,128]{2,1,0:T(8,128)}, f32[2,256,128]{2,1,0:T(8,128)}, /*index=5*/f32[2,128,128]{2,1,0:T(8,128)}) custom-call(f32[88,128]{1,0:T(8,128)S(1)} %get-tuple-element.26.info_ref, bf16[2,2048]{1,0:T(2,128)(2,1)S(1)} %get-tuple-element.27.rim_ref, ...), custom_call_target="tpu_custom_call" | custom-call | flops 4000000 | bytes 8000000 | tf_op jit(solution)/shard_map/near/pallas_call | solution.py:643
  48.9 5.3 %all-to-all-done.1 = f32[64,4,128]{2,1,0:T(4,128)S(1)} async-done(((f32[64,4,128]{2,1,0:T(4,128)}), f32[64,4,128]{2,1,0:T(4,128)S(1)}, u32[]{:S(2)}, u32[]{:S(2)}) %all-to-all-start.1) | async-done | bytes 131104 | tf_op jit(solution)/shard_map/all_to_all | solution.py:664
  54.2 0.0 copy-start.2
  54.2 4.1 %stream.1 = (f32[256,2048]{1,0:T(8,128)}, f32[256,2048]{1,0:T(8,128)S(1)}, f32[2,128]{1,0:T(2,128)S(1)}) custom-call(f32[88,128]{1,0:T(8,128)S(1)} %get-tuple-element.26.info_ref, f32[16,2048]{1,0:T(8,128)S(1)} %copy-done, f32[16,2048]{1,0:T(8,128)S(1)} %sqrt_multiply_fusion.gain_ref, f32[16,16,128]{2,1,0:T(8,128)S(1)} %bitcast.8, ...), custom_call_target="tpu_custom_call" | custom-call | tf_op jit(solution)/shard_map/stream/pallas_call | solution.py:666
  58.3 2.8 %collective-permute-start.3 = (f32[2,128]{1,0:T(2,128)S(1)}, f32[2,128]{1,0:T(2,128)S(1)}, u32[]{:S(2)}, u32[]{:S(2)}) collective-permute-start(f32[2,128]{1,0:T(2,128)S(1)} %get-tuple-element.48), channel_id=1, source_target_pairs={{0,3},{1,0},{2,1},{3,2},{4,7},{5,4},{6,5},{7,6},{8,11},{9,8},{10,9... | collective-permute-start | bytes 3080 | tf_op jit(solution)/shard_map/ppermute | solution.py:540
  61.1 0.3 collective-permute-start.2
  61.5 0.7 %collective-permute-start.1 = (f32[2,128]{1,0:T(2,128)S(1)}, f32[2,128]{1,0:T(2,128)S(1)}, u32[]{:S(2)}, u32[]{:S(2)}) collective-permute-start(f32[2,128]{1,0:T(2,128)S(1)} %get-tuple-element.48), channel_id=1, source_target_pairs={{0,1},{1,2},{2,3},{3,0},{4,5},{5,6},{6,7},{7,4},{8,9},{9,10},{10,1... | collective-permute-start | bytes 3080 | tf_op jit(solution)/shard_map/ppermute | solution.py:540
  62.1 0.0 collective-permute-done.3
  62.1 2.9 %collective-permute-done.2 = f32[2,128]{1,0:T(2,128)S(1)} collective-permute-done((f32[2,128]{1,0:T(2,128)S(1)}, f32[2,128]{1,0:T(2,128)S(1)}, u32[]{:S(2)}, u32[]{:S(2)}) %collective-permute-start.2) | collective-permute-done | bytes 1056 | tf_op jit(solution)/shard_map/ppermute | solution.py:540
  65.0 0.1 collective-permute-done.1
  65.1 0.0 copy-done.2
  65.1 1.5 %norm.1 = f32[256,2048]{1,0:T(8,128)} custom-call(f32[4,2,128]{2,1,0:T(2,128)S(1)} %pad_maximum_fusion.power_ref, f32[1,2048]{1,0:T(1,128)S(1)} %bitcast.11, f32[256,2048]{1,0:T(8,128)S(1)} %get-tuple-element.49.stream_ref), custom_call_target="tpu_custom_call" | custom-call | tf_op jit(solution)/shard_map/norm/pallas_call | solution.py:698
  (1 shorter events, 0.0 us)
Async XLA Ops:
  0.6 7.0 %copy-start = (f32[16,2048]{1,0:T(8,128)S(1)}, f32[16,2048]{1,0:T(8,128)}, u32[]{:S(2)}) copy-start(f32[16,2048]{1,0:T(8,128)} %rate_ref.5) | copy-start | bytes 393220
  1.6 25.9 %copy-start.3 = (f32[16,2048]{1,0:T(8,128)S(1)}, f32[16,2048]{1,0:T(8,128)}, u32[]{:S(2)}) copy-start(f32[16,2048]{1,0:T(8,128)} %param.15) | copy-start | bytes 393220
  1.6 26.0 %copy-start.1 = (f32[2048]{0:T(1024)S(1)}, f32[2048]{0:T(1024)}, u32[]{:S(2)}) copy-start(f32[2048]{0:T(1024)} %param.16) | copy-start | bytes 24580
  1.6 6.0 %collective-permute-start = (bf16[3,2,2048]{2,1,0:T(2,128)(2,1)S(1)}, bf16[3,2,2048]{2,1,0:T(2,128)(2,1)S(1)}, u32[]{:S(2)}, u32[]{:S(2)}) collective-permute-start(bf16[3,2,2048]{2,1,0:T(2,128)(2,1)S(1)} %rims.1), channel_id=1, source_target_pairs={{0,4},{4,8},{8,12},{12,16},{16,20},{20,24},{24,28},{28,32},{32,36}... | collective-permute-start | bytes 73736 | tf_op jit(solution)/shard_map/ppermute | solution.py:540
  14.0 23.9 %all-to-all-start = ((f32[64,4,128]{2,1,0:T(4,128)}), f32[64,4,128]{2,1,0:T(4,128)S(1)}, u32[]{:S(2)}, u32[]{:S(2)}) async-start(f32[64,4,128]{2,1,0:T(4,128)} %bitcast.13), calls=%async_computation | async-start | bytes 262144 | tf_op jit(solution)/shard_map/all_to_all | solution.py:612
  38.7 15.5 %all-to-all-start.1 = ((f32[64,4,128]{2,1,0:T(4,128)}), f32[64,4,128]{2,1,0:T(4,128)S(1)}, u32[]{:S(2)}, u32[]{:S(2)}) async-start(f32[64,4,128]{2,1,0:T(4,128)} %rank_scan.1), calls=%async_computation.1 | async-start | bytes 262144 | tf_op jit(solution)/shard_map/all_to_all | solution.py:664
  54.2 10.9 %copy-start.2 = (f32[2048]{0:T(1024)S(1)}, f32[2048]{0:T(1024)}, u32[]{:S(2)}) copy-start(f32[2048]{0:T(1024)} %param.17) | copy-start | bytes 24580
  58.3 3.9 %collective-permute-start.3 = (f32[2,128]{1,0:T(2,128)S(1)}, f32[2,128]{1,0:T(2,128)S(1)}, u32[]{:S(2)}, u32[]{:S(2)}) collective-permute-start(f32[2,128]{1,0:T(2,128)S(1)} %get-tuple-element.48), channel_id=1, source_target_pairs={{0,3},{1,0},{2,1},{3,2},{4,7},{5,4},{6,5},{7,6},{8,11},{9,8},{10,9... | collective-permute-start | bytes 3080 | tf_op jit(solution)/shard_map/ppermute | solution.py:540
  61.1 3.9 %collective-permute-start.2 = (f32[2,128]{1,0:T(2,128)S(1)}, f32[2,128]{1,0:T(2,128)S(1)}, u32[]{:S(2)}, u32[]{:S(2)}) collective-permute-start(f32[2,128]{1,0:T(2,128)S(1)} %get-tuple-element.48), channel_id=1, source_target_pairs={{0,2},{1,3},{2,0},{3,1},{4,6},{5,7},{6,4},{7,5},{8,10},{9,11},{10,... | collective-permute-start | bytes 3080 | tf_op jit(solution)/shard_map/ppermute | solution.py:540
  61.5 3.6 %collective-permute-start.1 = (f32[2,128]{1,0:T(2,128)S(1)}, f32[2,128]{1,0:T(2,128)S(1)}, u32[]{:S(2)}, u32[]{:S(2)}) collective-permute-start(f32[2,128]{1,0:T(2,128)S(1)} %get-tuple-element.48), channel_id=1, source_target_pairs={{0,1},{1,2},{2,3},{3,0},{4,5},{5,6},{6,7},{7,4},{8,9},{9,10},{10,1... | collective-permute-start | bytes 3080 | tf_op jit(solution)/shard_map/ppermute | solution.py:540

commit v3 on v2

--- a/solution.py
+++ b/solution.py
@@ -12,6 +12,7 @@
 GROUP = 256
 FIRST_SHARE = 4
 HEAD = 2
+NEXT = 4
 READY = 6
 STEPS = 16
 F32 = jnp.float32
@@ -66,14 +67,6 @@
     for piece in range(CHUNKS):
         low = offset + piece * (span + 1)
         target[low : low + span, :] = source[piece * span : (piece + 1) * span, lanes].astype(F32)
-
-
-def column_copies(sources, targets, sems, group):
-    lanes = pl.ds(pl.multiple_of(group * GROUP, GROUP), GROUP)
-    return [
-        pltpu.make_async_copy(source.at[:, lanes], target.at[:, lanes], sems.at[i, group])
-        for i, (source, target) in enumerate(zip(sources, targets))
-    ]
 
 
 def rim_kernel(q_hbm, k_hbm, v_hbm, out_ref, buffer, sems):
@@ -132,37 +125,45 @@
     return row + lax.div(row, span)
 
 
-def end_kernel(rows, poles, lengths_hbm, k_hbm, v_hbm, q_hbm, res_hbm, rim_ref, taps_hbm, rate_hbm, gated_a, gated_hbm, end_hbm, q_next, r_next, rim_next, taps_next, info_ref, lengths_ref, k_ref, v_ref, gated_b, end_ref, taps_ref, rate_ref, kx, vx, gx, decay_ref, sems, out_sems, end_sems, small_sems):
+def fetch_kernel(rows, lengths_hbm, k_hbm, v_hbm, q_hbm, res_hbm, taps_hbm, k_ref, v_ref, q_next, r_next, taps_ref, info_ref, lengths_ref, sems):
+    columns = pl.ds(0, q_next.shape[1])
+    pairs = (
+        (lengths_hbm, lengths_ref),
+        (k_hbm, k_ref),
+        (v_hbm, v_ref),
+        (q_hbm.at[:, columns], q_next),
+        (res_hbm.at[:, columns], r_next),
+        (taps_hbm, taps_ref),
+    )
+    copies = [pltpu.make_async_copy(source, target, sems.at[i]) for i, (source, target) in enumerate(pairs)]
+    for copy in copies:
+        copy.start()
+    copies[0].wait()
+    describe(starts_of(lengths_ref), lax.axis_index("ctx") * rows, rows, info_ref)
+    for copy in copies[1:]:
+        copy.wait()
+
+
+def end_kernel(rows, poles, info_ref, k_ref, v_ref, rim_ref, taps_ref, rate_ref, gated_a, gated_hbm, end_hbm, rim_next, taps_next, gated_b, end_ref, kx, vx, gx, decay_ref, mends, out_sems, end_sems):
     span = rows // CHUNKS
-    base = lax.axis_index("ctx") * rows
     phase = lax.broadcasted_iota(jnp.int32, (CHUNKS, LANES), 0)
-    small = [
-        pltpu.make_async_copy(source, target, small_sems.at[i])
-        for i, (source, target) in enumerate(((lengths_hbm, lengths_ref), (taps_hbm, taps_ref), (rate_hbm, rate_ref)))
-    ]
-    columns = pl.ds(0, q_next.shape[1])
-    ahead_of_time = [
-        pltpu.make_async_copy(source.at[:, columns], target, small_sems.at[len(small) + i])
-        for i, (source, target) in enumerate(((q_hbm, q_next), (res_hbm, r_next)))
-    ]
     groups = k_ref.shape[1] // GROUP
-    for copy in small:
-        copy.start()
-    for group in range(groups):
-        for copy in column_copies((k_hbm, v_hbm), (k_ref, v_ref), sems, group):
-            copy.start()
-    for copy in ahead_of_time:
-        copy.start()
     rim_next[...] = rim_ref[0]
-    for copy in small:
-        copy.wait()
     taps_next[...] = taps_ref[0]
-    starts = starts_of(lengths_ref)
-    touched = any_in(starts, base - 1, base + rows)
     last = jnp.int32(0)
-    for start in starts:
-        last = jnp.where((start >= base) & (start < base + rows), start - base, last)
-    describe(starts, base, rows, info_ref)
+    mended = jnp.int32(0)
+    for i in range(3):
+        low = INSIDE.start + i * CHUNKS
+        inside = jnp.max(info_ref[low : low + 1, :]).astype(jnp.int32)
+        here_now = (inside >= 0) & (inside < rows)
+        last = jnp.where(here_now, inside, last)
+        for row, reach, wanted in (
+            (inside, 0, here_now),
+            (inside + 1, 1, (inside >= -1) & (inside < rows - 1)),
+        ):
+            mends[0, mended] = jnp.where(wanted, row, 0)
+            mends[1, mended] = reach
+            mended = mended + wanted.astype(jnp.int32)
     inner = GROUP // LANES
 
     def store(here):
@@ -173,9 +174,6 @@
         return pltpu.make_async_copy(end_ref.at[here], end_hbm.at[here], end_sems.at[group])
 
     def one_group(group, first, gated_ref):
-        for copy in column_copies((k_hbm, v_hbm), (k_ref, v_ref), sems, group):
-            copy.wait()
-
         @pl.loop(group * inner, (group + 1) * inner)
         def _(part):
             lanes = lanes_at(part)
@@ -199,29 +197,19 @@
                 to = low + low // span
                 gated_ref[here, to : to + CHUNKS, :] = gated
 
-            @pl.when(touched)
+            @pl.when(mended > 0)
             def _():
-                for start in starts:
-                    inside = start - base
-
-                    def mend(row, reach):
-                        shorts = []
-                        for three, source in zip(lines, (kx, vx)):
-                            short = three[0] * source[pl.ds(row + 8, 1), :]
-                            if reach:
-                                short = short + three[1] * source[pl.ds(row + 7, 1), :]
-                            shorts.append(short)
-                        gated = shorts[0] * shorts[1]
-                        gx[pl.ds(row, 1), :] = gated
-                        gated_ref[here, pl.ds(pitched(row, span), 1), :] = gated
-
-                    @pl.when((inside >= 0) & (inside < rows))
-                    def _():
-                        mend(inside, False)
-
-                    @pl.when((inside >= -1) & (inside < rows - 1))
-                    def _():
-                        mend(inside + 1, True)
+                @pl.loop(0, mended)
+                def _(i):
+                    row = mends[0, i]
+                    reach = mends[1, i].astype(F32)
+                    shorts = []
+                    for three, source in zip(lines, (kx, vx)):
+                        now = three[0] * source[pl.ds(row + 8, 1), :]
+                        shorts.append(now + three[1] * source[pl.ds(row + 7, 1), :] * reach)
+                    gated = shorts[0] * shorts[1]
+                    gx[pl.ds(row, 1), :] = gated
+                    gated_ref[here, pl.ds(pitched(row, span), 1), :] = gated
 
                 for block in range(rows // CHUNKS):
                     low = block * CHUNKS
@@ -244,10 +232,8 @@
         send(group).start()
 
     middle = gated_a.shape[0] // inner
+    pl.loop(middle, groups)(lambda group: one_group(group, middle, gated_b))
     pl.loop(0, middle)(lambda group: one_group(group, 0, gated_a))
-    pl.loop(middle, groups)(lambda group: one_group(group, middle, gated_b))
-    for copy in ahead_of_time:
-        copy.wait()
     for here in range(gated_b.shape[0]):
         store(here).wait()
     for group in range(groups):
@@ -272,11 +258,20 @@
         out_ref[rank] = kept
 
 
-def scan_kernel(factor_ref, pieces_ref, out_ref):
+def scan_kernel(factor_ref, pieces_ref, out_hbm, out_ref, sems):
     running = jnp.zeros(pieces_ref.shape[1:], F32)
-    for rank in range(pieces_ref.shape[0]):
+    ranks = pieces_ref.shape[0]
+    block = ranks // sems.shape[0]
+    copies = []
+    for rank in range(ranks):
         out_ref[rank] = running
         running = factor_ref[rank] * running + pieces_ref[rank]
+        if rank % block == block - 1:
+            here = pl.ds(rank - block + 1, block)
+            copies.append(pltpu.make_async_copy(out_ref.at[here], out_hbm.at[here], sems.at[rank // block]))
+            copies[-1].start()
+    for copy in copies:
+        copy.wait()
 
 
 def near_kernel(rows, poles, first, early, info_ref, rim_ref, taps_ref, rate_ref, gain_ref, skip_ref, gated_in, q_in, r_in, q_hbm, res_hbm, gated_hbm, *others):
@@ -290,18 +285,23 @@
         gated_ref, near_ref, query_ref, local_ref, q_ref, r_ref, qx, rx, decay_ref, own_sems, far_sems = others
         count = near_ref.shape[0]
 
-    def fetch(here):
-        pairs = [(q_hbm.at[:, lanes_at(first + here)], q_ref.at[:, lanes_at(here)])]
-        pairs.append((res_hbm.at[:, lanes_at(first + here)], r_ref.at[:, lanes_at(here)]))
+    cuts = ((HEAD, NEXT), (NEXT, count))
+
+    def fetch(cut):
+        low, high = cuts[cut]
+        from_columns = pl.ds((first + low) * LANES, (high - low) * LANES)
+        columns = pl.ds(low * LANES, (high - low) * LANES)
+        pairs = [(source.at[:, from_columns], target.at[:, columns]) for source, target in ((q_hbm, q_ref), (res_hbm, r_ref))]
         if not early:
-            pairs.append((gated_hbm.at[here], gated_ref.at[here]))
+            blocks = pl.ds(low, high - low)
+            pairs.append((gated_hbm.at[blocks], gated_ref.at[blocks]))
         return [
-            pltpu.make_async_copy(source, target, own_sems.at[i, here])
+            pltpu.make_async_copy(source, target, own_sems.at[i, cut])
             for i, (source, target) in enumerate(pairs)
         ]
 
-    for here in range(HEAD, count):
-        for copy in fetch(here):
+    for cut in range(len(cuts)):
+        for copy in fetch(cut):
             copy.start()
     for i, (source, target) in enumerate(((q_in, q_ref), (r_in, r_ref))):
         target[:, : HEAD * LANES] = source[...]
@@ -342,10 +342,12 @@
         far = info_ref[FAR, :]
         joined = info_ref[JOINED, :]
 
-        @pl.when(here >= HEAD)
-        def _():
-            for copy in fetch(here):
-                copy.wait()
+        for cut, (low, _) in enumerate(cuts):
+
+            @pl.when(here == low)
+            def _():
+                for copy in fetch(cut):
+                    copy.wait()
 
         qx[5:7, :] = rim_ref[:, lanes].astype(F32)
         lay_out(q_ref, own, qx, span, 8)
@@ -499,16 +501,20 @@
             def _(part):
                 one_part(part + first, near_ref, query_ref, local_ref, part)
 
-            copy_out(group + first // inner).start()
+            if near_ref is not near_b:
+                copy_out(group + first // inner).start()
 
     for piece in range(rows // LANES):
         turned = px[piece * LANES : (piece + 1) * LANES, :].T
         power_ref[piece : piece + 1, :] = jnp.sum(turned, axis=0, keepdims=True)
-    for group in range(groups):
+    for group in range((early + READY) // inner):
         copy_out(group).wait()
 
 
-def norm_kernel(width, power_ref, gain_ref, stream_ref, out_hbm, scale_ref, buffer, sems):
+def norm_kernel(width, left, power_ref, gain_ref, stream_ref, stream_in, out_hbm, stream_out, scale_ref, buffer, sems, left_sem):
+    columns = pl.ds(left, stream_ref.shape[1] - left)
+    rest = pltpu.make_async_copy(stream_ref.at[:, columns], stream_out.at[:, columns], left_sem.at[0])
+    rest.start()
     scale = lax.rsqrt(jnp.sum(power_ref[...], axis=0) / width + 1e-06)
     for piece in range(scale.shape[0]):
         wide = jnp.broadcast_to(scale[piece : piece + 1, :], (LANES, LANES))
@@ -532,6 +538,7 @@
 
     for group in range(count):
         copy_out(group).wait()
+    rest.wait()
 
 
 def shifted(block, axis, distance, wrap):
@@ -573,41 +580,50 @@
     late = parts - early
     pitch = rows + CHUNKS
     held = parts * poles // ranks
-    gated_a, gated_b, end, q_a, r_a, query_rim, query_taps, info = pl.pallas_call(
+    k_here, v_here, q_a, r_a, taps_here, info = pl.pallas_call(
+        functools.partial(fetch_kernel, rows),
+        in_specs=[outside] * 6,
+        out_specs=[near_by] * 6,
+        out_shape=[
+            pltpu.VMEM((rows, width), BF16),
+            pltpu.VMEM((rows, width), BF16),
+            pltpu.VMEM((rows, HEAD * LANES), BF16),
+            pltpu.VMEM((rows, HEAD * LANES), BF16),
+            kept_near(3, 3, width),
+            kept_near(SECTIONS, LANES),
+        ],
+        scratch_shapes=[pltpu.SMEM(lengths.shape, jnp.int32), pltpu.SemaphoreType.DMA((6,))],
+        compiler_params=limit,
+        cost_estimate=pl.CostEstimate(flops=1000000, bytes_accessed=5000000, transcendentals=0),
+        name="fetch",
+    )(lengths, key_proj, value_proj, query_proj, residual, short_filter)
+    info, k_here, v_here, taps_here = map(close_by, (info, k_here, v_here, taps_here))
+    gated_a, gated_b, end, query_rim, query_taps = pl.pallas_call(
         functools.partial(end_kernel, rows, poles),
-        in_specs=[outside] * 5 + [near_by, outside, outside],
-        out_specs=[near_by, outside, outside] + [near_by] * 5,
+        in_specs=[near_by] * 6,
+        out_specs=[near_by, outside, outside, near_by, near_by],
         out_shape=[
             kept_near(early, pitch, LANES),
             pltpu.HBM((late, pitch, LANES), F32),
             pltpu.HBM((parts, poles, LANES), F32),
-            pltpu.VMEM((rows, HEAD * LANES), BF16),
-            pltpu.VMEM((rows, HEAD * LANES), BF16),
             pltpu.VMEM((2, width), BF16),
             kept_near(3, width),
-            kept_near(SECTIONS, LANES),
         ],
         scratch_shapes=[
-            pltpu.SMEM(lengths.shape, jnp.int32),
-            pltpu.VMEM((rows, width), BF16),
-            pltpu.VMEM((rows, width), BF16),
             pltpu.VMEM((late, pitch, LANES), F32),
             pltpu.VMEM((parts, poles, LANES), F32),
-            pltpu.VMEM((3, 3, width), F32),
-            pltpu.VMEM((poles, width), F32),
             pltpu.VMEM((rows + 8, LANES), F32),
             pltpu.VMEM((rows + 8, LANES), F32),
             pltpu.VMEM((rows, LANES), F32),
             pltpu.VMEM((poles, LANES), F32),
-            pltpu.SemaphoreType.DMA((2, groups)),
+            pltpu.SMEM((2, 8), jnp.int32),
             pltpu.SemaphoreType.DMA((late,)),
             pltpu.SemaphoreType.DMA((groups,)),
-            pltpu.SemaphoreType.DMA((5,)),
         ],
         compiler_params=limit,
         name="end_state",
-    )(lengths, key_proj, value_proj, query_proj, residual, rims, short_filter, decay_rate)
-    info, query_rim, query_taps = map(close_by, (info, query_rim, query_taps))
+    )(info, k_here, v_here, rims, taps_here, decay_rate)
+    query_rim, query_taps = map(close_by, (query_rim, query_taps))
 
     pieces = lax.all_to_all(end.reshape(ranks, held, LANES), "ctx", 0, 0, tiled=True)
 
@@ -622,7 +638,7 @@
             pltpu.VMEM((rows + 16, LANES), F32),
             pltpu.VMEM((rows + 16, LANES), F32),
             pltpu.VMEM((poles, LANES), F32),
-            pltpu.SemaphoreType.DMA((3, count)),
+            pltpu.SemaphoreType.DMA((3, 2)),
             pltpu.SemaphoreType.DMA((3, count)),
         ]
         if early:
@@ -656,8 +672,9 @@
     scanned = pl.pallas_call(
         scan_kernel,
         in_specs=[near_by, near_by],
-        out_specs=near_by,
+        out_specs=outside,
         out_shape=pltpu.HBM((ranks, held, LANES), F32),
+        scratch_shapes=[pltpu.VMEM((ranks, held, LANES), F32), pltpu.SemaphoreType.DMA((2,))],
         compiler_params=limit,
         name="rank_scan",
     )(close_by(factors), pieces)
@@ -694,20 +711,23 @@
         *map(far_off, near_b[3:]),
     )
     shares = lax.axis_size("ch")
-    powers = jnp.stack([power] + [shifted(power, "ch", i, True) for i in range(1, shares)])
-    normed = pl.pallas_call(
-        functools.partial(norm_kernel, float(width * shares)),
-        in_specs=[near_by, near_by, near_by],
-        out_specs=outside,
-        out_shape=shape(rows, width),
+    near_first = sorted(range(1, shares), key=lambda hop: min(hop, shares - hop))
+    powers = jnp.stack([power] + [shifted(power, "ch", hop, True) for hop in near_first])
+    normed, stream = pl.pallas_call(
+        functools.partial(norm_kernel, float(width * shares), (early + READY) * LANES),
+        in_specs=[near_by, near_by, near_by, outside],
+        out_specs=[outside, outside],
+        out_shape=[pltpu.HBM((rows, width), F32)] * 2,
+        input_output_aliases={3: 1},
         scratch_shapes=[
             pltpu.VMEM((rows, LANES), F32),
             pltpu.VMEM((rows, width), F32),
             pltpu.SemaphoreType.DMA((8,)),
+            pltpu.SemaphoreType.DMA((1,)),
         ],
         compiler_params=limit,
         name="norm",
-    )(powers, norm_gain.reshape(1, width), close_by(kept))
+    )(powers, norm_gain.reshape(1, width), close_by(kept), far_off(stream))
     return (stream, normed)
 
 

time: 67.4 us -> 66.3 us (0.984); the launches traced: 66.6 us -> 66.3 us
    ppermute x4, waiting for transfers between devices: 3.86 us -> 2.94 us  [shifted(): return lax.ppermute(block, axis, route)]
    pallas_call x3 -> x4, Pallas kernels: 8.68 us -> 9.22 us  [the longest x1 5.25 us: on_device(): pl.pallas_call(functools.partial(end_kernel, rows, poles), in_specs=[near...]
  transfers between devices with their start and end apart: 6 -> 6, of which waited for: 5 -> 4; matrix products, arithmetic and copies ran while one was open for 0% -> 0% of each run, Pallas kernels for 15% -> 17%
where the time goes in v3:
time: 66.3 us
  starting transfers between devices  28 us (42%)
  Pallas kernels  23.6 us (36%)
  waiting for transfers between devices  13.8 us (21%)
  between operations  0.78 us (1%)
    all_to_all x1, starting transfers between devices, on_device(): lax.all_to_all(end.reshape(ranks, held, LANES), 'ctx', 0, 0, tiled=True)  13.2 us
    pallas_call x2, Pallas kernels, near_side(): pl.pallas_call(functools.partial(near_kernel, rows, poles, first, early),...  9.74 us
    ppermute x4, starting transfers between devices, shifted(): return lax.ppermute(block, axis, route)  9.53 us
    all_to_all x1, waiting for transfers between devices, on_device(): lax.all_to_all(end.reshape(ranks, held, LANES), 'ctx', 0, 0, tiled=True)  5.43 us
    all_to_all x1, waiting for transfers between devices, on_device(): lax.all_to_all(scanned, 'ctx', 0, 0, tiled=True)  5.42 us
    all_to_all x1, starting transfers between devices, on_device(): lax.all_to_all(scanned, 'ctx', 0, 0, tiled=True)  5.25 us
    pallas_call x1, Pallas kernels, on_device(): pl.pallas_call(functools.partial(end_kernel, rows, poles), in_specs=[near...  5.25 us
    pallas_call x1, Pallas kernels, on_device(): pl.pallas_call(functools.partial(stream_kernel, rows, poles), in_specs=[n...  3.73 us
  transfers between devices with their start and end apart: 6, of which 4 were waited for; matrix products, arithmetic and copies ran while one was open for 0% of the time, Pallas kernels for 17%

profile of v3, /device:TPU:1, one launch (start us, length us, event | category | flops | bytes accessed | tf_op | source)
XLA Modules:
  0.0 66.3 jit_solution(11425427323490532036)
XLA Ops:
  0.6 0.9 %rims.1 = bf16[3,2,2048]{2,1,0:T(2,128)(2,1)S(1)} custom-call(bf16[256,2048]{1,0:T(8,128)(2,1)} %q_hbm.7, bf16[256,2048]{1,0:T(8,128)(2,1)} %k_hbm.3, bf16[256,2048]{1,0:T(8,128)(2,1)} %v_hbm.3), custom_call_target="tpu_custom_call" | custom-call | tf_op jit(solution)/shard_map/rims/pallas_call | solution.py:567
  1.6 0.0 copy-start
  1.6 5.1 %collective-permute-start = (bf16[3,2,2048]{2,1,0:T(2,128)(2,1)S(1)}, bf16[3,2,2048]{2,1,0:T(2,128)(2,1)S(1)}, u32[]{:S(2)}, u32[]{:S(2)}) collective-permute-start(bf16[3,2,2048]{2,1,0:T(2,128)(2,1)S(1)} %rims.1), channel_id=1, source_target_pairs={{0,4},{4,8},{8,12},{12,16},{16,20},{20,24},{24,28},{28,32},{32,36}... | collective-permute-start | bytes 73736 | tf_op jit(solution)/shard_map/ppermute | solution.py:547
  6.7 1.7 %fetch.1 = (bf16[256,2048]{1,0:T(8,128)(2,1)S(1)}, bf16[256,2048]{1,0:T(8,128)(2,1)S(1)}, bf16[256,256]{1,0:T(8,128)(2,1)S(1)}, bf16[256,256]{1,0:T(8,128)(2,1)S...) custom-call(s32[4]{0:T(128)} %lengths_hbm.1, bf16[256,2048]{1,0:T(8,128)(2,1)} %k_hbm.3, bf16[256,2048]{1,0:T(8,128)(2,1)} %v_hbm.3, ...), custom_call_target="tpu_custom_call" | custom-call | flops 1000000 | bytes 5000000 | tf_op jit(solution)/shard_map/fetch/pallas_call | solution.py:583
  8.3 0.0 copy-start.3
  8.4 0.0 copy-start.1
  8.4 0.0 collective-permute-done.rim_ref
  8.4 0.0 copy-done
  8.4 5.2 %end_state.1 = (f32[8,264,128]{2,1,0:T(8,128)S(1)}, f32[8,264,128]{2,1,0:T(8,128)}, f32[16,16,128]{2,1,0:T(8,128)}, bf16[2,2048]{1,0:T(2,128)(2,1)S(1)}, f32[3,2048]{1,0:T(4,128)S(1)}) custom-call(f32[88,128]{1,0:T(8,128)S(1)} %get-tuple-element.31.info_ref, bf16[256,2048]{1,0:T(8,128)(2,1)S(1)} %get-tuple-element.32.k_ref, ...), custom_call_target="tpu_custom_call" | custom-call | tf_op jit(solution)/shard_map/end_state/pallas_call | solution.py:601
  13.6 13.2 %all-to-all-start = ((f32[64,4,128]{2,1,0:T(4,128)}), f32[64,4,128]{2,1,0:T(4,128)S(1)}, u32[]{:S(2)}, u32[]{:S(2)}) async-start(f32[64,4,128]{2,1,0:T(4,128)} %bitcast.13), calls=%async_computation | async-start | bytes 262144 | tf_op jit(solution)/shard_map/all_to_all | solution.py:628
  26.9 0.0 copy-done.3
  26.9 0.1 sqrt_multiply_fusion.gain_ref
  27.0 0.0 copy-done.1
  27.0 4.8 %near.2 = (f32[8,256,128]{2,1,0:T(8,128)}, f32[8,256,128]{2,1,0:T(8,128)}, f32[8,128,128]{2,1,0:T(8,128)}, f32[64,4,128]{2,1,0:T(4,128)S(1)}, f32[2,264,128]{2,1...) custom-call(f32[88,128]{1,0:T(8,128)S(1)} %get-tuple-element.31.info_ref, ...), custom_call_target="tpu_custom_call" | custom-call | flops 4000000 | bytes 8000000 | tf_op jit(solution)/shard_map/near/pallas_call | solution.py:659
  31.8 5.4 %all-to-all-done.pieces_ref = f32[64,4,128]{2,1,0:T(4,128)S(1)} async-done(((f32[64,4,128]{2,1,0:T(4,128)}), f32[64,4,128]{2,1,0:T(4,128)S(1)}, u32[]{:S(2)}, u32[]{:S(2)}) %all-to-all-start) | async-done | bytes 131104 | tf_op jit(solution)/shard_map/all_to_all | solution.py:628
  37.2 0.8 %rank_scan.1 = f32[64,4,128]{2,1,0:T(4,128)} custom-call(f32[64,4,128]{2,1,0:T(4,128)S(1)} %get-tuple-element.41.factor_ref, f32[64,4,128]{2,1,0:T(4,128)S(1)} %all-to-all-done.pieces_ref), custom_call_target="tpu_custom_call" | custom-call | tf_op jit(solution)/shard_map/rank_scan/pallas_call | solution.py:672
  38.0 5.3 %all-to-all-start.1 = ((f32[64,4,128]{2,1,0:T(4,128)}), f32[64,4,128]{2,1,0:T(4,128)S(1)}, u32[]{:S(2)}, u32[]{:S(2)}) async-start(f32[64,4,128]{2,1,0:T(4,128)} %rank_scan.1), calls=%async_computation.1 | async-start | bytes 262144 | tf_op jit(solution)/shard_map/all_to_all | solution.py:681
  43.3 4.9 %near.3 = (f32[6,256,128]{2,1,0:T(8,128)S(1)}, f32[6,256,128]{2,1,0:T(8,128)S(1)}, f32[6,128,128]{2,1,0:T(8,128)S(1)}, f32[2,256,128]{2,1,0:T(8,128)}, f32[2,256,128]{2,1,0:T(8,128)}, /*index=5*/f32[2,128,128]{2,1,0:T(8,128)}) custom-call(f32[88,128]{1,0:T(8,128)S(1)} %get-tuple-element.31.info_ref, bf16[2,2048]{1,0:T(2,128)(2,1)S(1)} %get-tuple-element.35.rim_ref, ...), custom_call_target="tpu_custom_call" | custom-call | flops 4000000 | bytes 8000000 | tf_op jit(solution)/shard_map/near/pallas_call | solution.py:659
  48.2 5.4 %all-to-all-done.1 = f32[64,4,128]{2,1,0:T(4,128)S(1)} async-done(((f32[64,4,128]{2,1,0:T(4,128)}), f32[64,4,128]{2,1,0:T(4,128)S(1)}, u32[]{:S(2)}, u32[]{:S(2)}) %all-to-all-start.1) | async-done | bytes 131104 | tf_op jit(solution)/shard_map/all_to_all | solution.py:681
  53.7 0.0 copy-start.2
  53.7 3.7 %stream.1 = (f32[256,2048]{1,0:T(8,128)}, f32[256,2048]{1,0:T(8,128)S(1)}, f32[2,128]{1,0:T(2,128)S(1)}) custom-call(f32[88,128]{1,0:T(8,128)S(1)} %get-tuple-element.31.info_ref, f32[16,2048]{1,0:T(8,128)S(1)} %copy-done, f32[16,2048]{1,0:T(8,128)S(1)} %sqrt_multiply_fusion.gain_ref, f32[16,16,128]{2,1,0:T(8,128)S(1)} %bitcast.8, ...), custom_call_target="tpu_custom_call" | custom-call | tf_op jit(solution)/shard_map/stream/pallas_call | solution.py:683
  57.4 3.0 %collective-permute-start.3 = (f32[2,128]{1,0:T(2,128)S(1)}, f32[2,128]{1,0:T(2,128)S(1)}, u32[]{:S(2)}, u32[]{:S(2)}) collective-permute-start(f32[2,128]{1,0:T(2,128)S(1)} %get-tuple-element.55), channel_id=1, source_target_pairs={{0,2},{1,3},{2,0},{3,1},{4,6},{5,7},{6,4},{7,5},{8,10},{9,11},{10,... | collective-permute-start | bytes 3080 | tf_op jit(solution)/shard_map/ppermute | solution.py:547
  60.4 0.8 %collective-permute-start.2 = (f32[2,128]{1,0:T(2,128)S(1)}, f32[2,128]{1,0:T(2,128)S(1)}, u32[]{:S(2)}, u32[]{:S(2)}) collective-permute-start(f32[2,128]{1,0:T(2,128)S(1)} %get-tuple-element.55), channel_id=1, source_target_pairs={{0,3},{1,0},{2,1},{3,2},{4,7},{5,4},{6,5},{7,6},{8,11},{9,8},{10,9... | collective-permute-start | bytes 3080 | tf_op jit(solution)/shard_map/ppermute | solution.py:547
  61.2 0.7 %collective-permute-start.1 = (f32[2,128]{1,0:T(2,128)S(1)}, f32[2,128]{1,0:T(2,128)S(1)}, u32[]{:S(2)}, u32[]{:S(2)}) collective-permute-start(f32[2,128]{1,0:T(2,128)S(1)} %get-tuple-element.55), channel_id=1, source_target_pairs={{0,1},{1,2},{2,3},{3,0},{4,5},{5,6},{6,7},{7,4},{8,9},{9,10},{10,1... | collective-permute-start | bytes 3080 | tf_op jit(solution)/shard_map/ppermute | solution.py:547
  61.9 0.0 collective-permute-done.3
  61.9 0.9 %collective-permute-done.2 = f32[2,128]{1,0:T(2,128)S(1)} collective-permute-done((f32[2,128]{1,0:T(2,128)S(1)}, f32[2,128]{1,0:T(2,128)S(1)}, u32[]{:S(2)}, u32[]{:S(2)}) %collective-permute-start.2) | collective-permute-done | bytes 1056 | tf_op jit(solution)/shard_map/ppermute | solution.py:547
  62.8 2.0 %collective-permute-done.1 = f32[2,128]{1,0:T(2,128)S(1)} collective-permute-done((f32[2,128]{1,0:T(2,128)S(1)}, f32[2,128]{1,0:T(2,128)S(1)}, u32[]{:S(2)}, u32[]{:S(2)}) %collective-permute-start.1) | collective-permute-done | bytes 1056 | tf_op jit(solution)/shard_map/ppermute | solution.py:547
  64.8 0.0 copy-done.2
  64.8 1.5 %norm.1 = (f32[256,2048]{1,0:T(8,128)}, f32[256,2048]{1,0:T(8,128)}) custom-call(f32[4,2,128]{2,1,0:T(2,128)S(1)} %pad_maximum_fusion.power_ref, f32[1,2048]{1,0:T(1,128)S(1)} %bitcast.11, f32[256,2048]{1,0:T(8,128)S(1)} %get-tuple-element.56.stream_ref, f32[256,2048]{1,0:T(8,128)} %get-tuple-element.57.stream_in), custom_call_target="tpu_custom_call", output_to_operand_aliasing={{1}: (3, {})} | custom-call | tf_op jit(solution)/shard_map/norm/pallas_call | solution.py:716
  (1 shorter events, 0.0 us)
Async XLA Ops:
  1.6 6.8 %copy-start = (f32[16,2048]{1,0:T(8,128)S(1)}, f32[16,2048]{1,0:T(8,128)}, u32[]{:S(2)}) copy-start(f32[16,2048]{1,0:T(8,128)} %rate_ref.7) | copy-start | bytes 393220
  1.6 6.8 %collective-permute-start = (bf16[3,2,2048]{2,1,0:T(2,128)(2,1)S(1)}, bf16[3,2,2048]{2,1,0:T(2,128)(2,1)S(1)}, u32[]{:S(2)}, u32[]{:S(2)}) collective-permute-start(bf16[3,2,2048]{2,1,0:T(2,128)(2,1)S(1)} %rims.1), channel_id=1, source_target_pairs={{0,4},{4,8},{8,12},{12,16},{16,20},{20,24},{24,28},{28,32},{32,36}... | collective-permute-start | bytes 73736 | tf_op jit(solution)/shard_map/ppermute | solution.py:547
  8.3 18.5 %copy-start.3 = (f32[16,2048]{1,0:T(8,128)S(1)}, f32[16,2048]{1,0:T(8,128)}, u32[]{:S(2)}) copy-start(f32[16,2048]{1,0:T(8,128)} %param.15) | copy-start | bytes 393220
  8.4 18.6 %copy-start.1 = (f32[2048]{0:T(1024)S(1)}, f32[2048]{0:T(1024)}, u32[]{:S(2)}) copy-start(f32[2048]{0:T(1024)} %param.16) | copy-start | bytes 24580
  13.6 23.6 %all-to-all-start = ((f32[64,4,128]{2,1,0:T(4,128)}), f32[64,4,128]{2,1,0:T(4,128)S(1)}, u32[]{:S(2)}, u32[]{:S(2)}) async-start(f32[64,4,128]{2,1,0:T(4,128)} %bitcast.13), calls=%async_computation | async-start | bytes 262144 | tf_op jit(solution)/shard_map/all_to_all | solution.py:628
  38.0 15.6 %all-to-all-start.1 = ((f32[64,4,128]{2,1,0:T(4,128)}), f32[64,4,128]{2,1,0:T(4,128)S(1)}, u32[]{:S(2)}, u32[]{:S(2)}) async-start(f32[64,4,128]{2,1,0:T(4,128)} %rank_scan.1), calls=%async_computation.1 | async-start | bytes 262144 | tf_op jit(solution)/shard_map/all_to_all | solution.py:681
  53.7 11.2 %copy-start.2 = (f32[2048]{0:T(1024)S(1)}, f32[2048]{0:T(1024)}, u32[]{:S(2)}) copy-start(f32[2048]{0:T(1024)} %param.17) | copy-start | bytes 24580
  57.4 4.5 %collective-permute-start.3 = (f32[2,128]{1,0:T(2,128)S(1)}, f32[2,128]{1,0:T(2,128)S(1)}, u32[]{:S(2)}, u32[]{:S(2)}) collective-permute-start(f32[2,128]{1,0:T(2,128)S(1)} %get-tuple-element.55), channel_id=1, source_target_pairs={{0,2},{1,3},{2,0},{3,1},{4,6},{5,7},{6,4},{7,5},{8,10},{9,11},{10,... | collective-permute-start | bytes 3080 | tf_op jit(solution)/shard_map/ppermute | solution.py:547
  60.4 2.4 %collective-permute-start.2 = (f32[2,128]{1,0:T(2,128)S(1)}, f32[2,128]{1,0:T(2,128)S(1)}, u32[]{:S(2)}, u32[]{:S(2)}) collective-permute-start(f32[2,128]{1,0:T(2,128)S(1)} %get-tuple-element.55), channel_id=1, source_target_pairs={{0,3},{1,0},{2,1},{3,2},{4,7},{5,4},{6,5},{7,6},{8,11},{9,8},{10,9... | collective-permute-start | bytes 3080 | tf_op jit(solution)/shard_map/ppermute | solution.py:547
  61.2 3.6 %collective-permute-start.1 = (f32[2,128]{1,0:T(2,128)S(1)}, f32[2,128]{1,0:T(2,128)S(1)}, u32[]{:S(2)}, u32[]{:S(2)}) collective-permute-start(f32[2,128]{1,0:T(2,128)S(1)} %get-tuple-element.55), channel_id=1, source_target_pairs={{0,1},{1,2},{2,3},{3,0},{4,5},{5,6},{6,7},{7,4},{8,9},{9,10},{10,1... | collective-permute-start | bytes 3080 | tf_op jit(solution)/shard_map/ppermute | solution.py:547

commit v4 on v3

--- a/solution.py
+++ b/solution.py
@@ -23,7 +23,7 @@
     first = lengths_ref[0]
     second = first + lengths_ref[1]
     third = second + lengths_ref[2]
-    return (first, second, third)
+    return (jnp.int32(0), first, second, third)
 
 
 def spread(row):
@@ -90,8 +90,9 @@
     return carry
 
 
-FAR, JOINED, REACHED, AHEAD, FLAGS, BEGUN, INSIDE = (slice(i * CHUNKS, (i + 1) * CHUNKS) for i in (0, 1, 2, 3, 4, 5, 8))
-SECTIONS = 11 * CHUNKS
+SEGMENTS = 4
+FAR, JOINED, REACHED, AHEAD, FLAGS, BEGUN, INSIDE = (slice(i * CHUNKS, (i + 1) * CHUNKS) for i in (0, 1, 2, 3, 4, 5, 5 + SEGMENTS))
+SECTIONS = (5 + 2 * SEGMENTS) * CHUNKS
 
 
 def describe(starts, base, rows, info_ref):
@@ -152,7 +153,7 @@
     taps_next[...] = taps_ref[0]
     last = jnp.int32(0)
     mended = jnp.int32(0)
-    for i in range(3):
+    for i in range(SEGMENTS):
         low = INSIDE.start + i * CHUNKS
         inside = jnp.max(info_ref[low : low + 1, :]).astype(jnp.int32)
         here_now = (inside >= 0) & (inside < rows)
@@ -250,7 +251,7 @@
         theirs = rate_ref[share * held : (share + 1) * held, lanes]
         rate = jnp.where(lax.rem(mine, shares) == share, theirs, rate)
     whole = jnp.exp(-float(rows) * rate)
-    begun = [info_ref[BEGUN.start + i * CHUNKS : BEGUN.start + i * CHUNKS + held, :] for i in range(3)]
+    begun = [info_ref[BEGUN.start + i * CHUNKS : BEGUN.start + i * CHUNKS + held, :] for i in range(1, SEGMENTS)]
     for rank in range(ranks):
         kept = whole
         for begin in begun:
@@ -368,7 +369,7 @@
                 place = block * STEPS + step
                 if masked:
                     keep = jnp.ones((CHUNKS, LANES), F32)
-                    for i in range(3):
+                    for i in range(SEGMENTS):
                         low = INSIDE.start + i * CHUNKS
                         keep = jnp.where(info_ref[low : low + CHUNKS, :] == float(place), 0.0, keep)
                     carry = [held * keep for held in carry]
@@ -541,10 +542,9 @@
     rest.wait()
 
 
-def shifted(block, axis, distance, wrap):
+def shifted(block, axis, distance):
     count = lax.axis_size(axis)
-    route = [(i, (i + distance) % count) for i in range(count) if wrap or i + distance < count]
-    return lax.ppermute(block, axis, route)
+    return lax.ppermute(block, axis, [(i, (i + distance) % count) for i in range(count)])
 
 
 def on_device(query_proj, key_proj, value_proj, short_filter, decay_rate, residue, skip_gain, norm_gain, residual, lengths):
@@ -572,7 +572,7 @@
         scratch_shapes=[pltpu.VMEM((3, 16, width), BF16), pltpu.SemaphoreType.DMA((3,))],
         name="rims",
     )(query_proj, key_proj, value_proj)
-    rims = shifted(rims, "ctx", 1, False)
+    rims = shifted(rims, "ctx", 1)
     pole_gain = residue * jnp.sqrt(-jnp.expm1(-2.0 * decay_rate))
     skip = skip_gain.reshape(1, width)
 
@@ -712,7 +712,7 @@
     )
     shares = lax.axis_size("ch")
     near_first = sorted(range(1, shares), key=lambda hop: min(hop, shares - hop))
-    powers = jnp.stack([power] + [shifted(power, "ch", hop, True) for hop in near_first])
+    powers = jnp.stack([power] + [shifted(power, "ch", hop) for hop in near_first])
     normed, stream = pl.pallas_call(
         functools.partial(norm_kernel, float(width * shares), (early + READY) * LANES),
         in_specs=[near_by, near_by, near_by, outside],

time: 66.3 us -> 63.8 us (0.962)
  starting transfers between devices: 28 us -> 25.2 us
    ppermute x4, starting transfers between devices: 9.53 us -> 7.57 us  [shifted(): lax.ppermute(block, axis, [(i, (i + distance) % count) for i in range(cou...]
  transfers between devices with their start and end apart: 6 -> 6, of which waited for: 4 -> 4; matrix products, arithmetic and copies ran while one was open for 0% -> 0% of each run, Pallas kernels for 17% -> 18%
where the time goes in v4:
time: 63.8 us; the launch traced here: 63.5 us
  starting transfers between devices  25.2 us (39%)
  Pallas kernels  23.7 us (37%)
  waiting for transfers between devices  13.8 us (22%)
  between operations  0.77 us (1%)
    all_to_all x1, starting transfers between devices, on_device(): lax.all_to_all(end.reshape(ranks, held, LANES), 'ctx', 0, 0, tiled=True)  12.7 us
    pallas_call x2, Pallas kernels, near_side(): pl.pallas_call(functools.partial(near_kernel, rows, poles, first, early),...  9.78 us
    ppermute x4, starting transfers between devices, shifted(): lax.ppermute(block, axis, [(i, (i + distance) % count) for i in range(cou...  7.57 us
    all_to_all x1, waiting for transfers between devices, on_device(): lax.all_to_all(end.reshape(ranks, held, LANES), 'ctx', 0, 0, tiled=True)  5.41 us
    all_to_all x1, waiting for transfers between devices, on_device(): lax.all_to_all(scanned, 'ctx', 0, 0, tiled=True)  5.4 us
    pallas_call x1, Pallas kernels, on_device(): pl.pallas_call(functools.partial(end_kernel, rows, poles), in_specs=[near...  5.25 us
    all_to_all x1, starting transfers between devices, on_device(): lax.all_to_all(scanned, 'ctx', 0, 0, tiled=True)  4.93 us
    pallas_call x1, Pallas kernels, on_device(): pl.pallas_call(functools.partial(stream_kernel, rows, poles), in_specs=[n...  3.74 us
  transfers between devices with their start and end apart: 6, of which 4 were waited for; matrix products, arithmetic and copies ran while one was open for 0% of the time, Pallas kernels for 18%

profile of v4, /device:TPU:1, one launch (start us, length us, event | category | flops | bytes accessed | tf_op | source)
XLA Modules:
  0.0 63.5 jit_solution(2694264643678661821)
XLA Ops:
  0.6 0.9 %rims.1 = bf16[3,2,2048]{2,1,0:T(2,128)(2,1)S(1)} custom-call(bf16[256,2048]{1,0:T(8,128)(2,1)} %q_hbm.7, bf16[256,2048]{1,0:T(8,128)(2,1)} %k_hbm.3, bf16[256,2048]{1,0:T(8,128)(2,1)} %v_hbm.3), custom_call_target="tpu_custom_call" | custom-call | tf_op jit(solution)/shard_map/rims/pallas_call | solution.py:567
  1.6 0.0 copy-start
  1.6 3.1 %collective-permute-start = (bf16[3,2,2048]{2,1,0:T(2,128)(2,1)S(1)}, bf16[3,2,2048]{2,1,0:T(2,128)(2,1)S(1)}, u32[]{:S(2)}, u32[]{:S(2)}) collective-permute-start(bf16[3,2,2048]{2,1,0:T(2,128)(2,1)S(1)} %rims.1), channel_id=1, source_target_pairs={{0,4},{4,8},{8,12},{12,16},{16,20},{20,24},{24,28},{28,32},{32,36}... | collective-permute-start | bytes 73736 | tf_op jit(solution)/shard_map/ppermute | solution.py:547
  4.7 1.7 %fetch.1 = (bf16[256,2048]{1,0:T(8,128)(2,1)S(1)}, bf16[256,2048]{1,0:T(8,128)(2,1)S(1)}, bf16[256,256]{1,0:T(8,128)(2,1)S(1)}, bf16[256,256]{1,0:T(8,128)(2,1)S...) custom-call(s32[4]{0:T(128)} %lengths_hbm.1, bf16[256,2048]{1,0:T(8,128)(2,1)} %k_hbm.3, bf16[256,2048]{1,0:T(8,128)(2,1)} %v_hbm.3, ...), custom_call_target="tpu_custom_call" | custom-call | flops 1000000 | bytes 5000000 | tf_op jit(solution)/shard_map/fetch/pallas_call | solution.py:583
  6.4 0.0 copy-start.3
  6.4 0.0 copy-start.1
  6.4 0.0 collective-permute-done.rim_ref
  6.4 0.0 copy-done
  6.4 5.3 %end_state.1 = (f32[8,264,128]{2,1,0:T(8,128)S(1)}, f32[8,264,128]{2,1,0:T(8,128)}, f32[16,16,128]{2,1,0:T(8,128)}, bf16[2,2048]{1,0:T(2,128)(2,1)S(1)}, f32[3,2048]{1,0:T(4,128)S(1)}) custom-call(f32[104,128]{1,0:T(8,128)S(1)} %get-tuple-element.31.info_ref, bf16[256,2048]{1,0:T(8,128)(2,1)S(1)} %get-tuple-element.32.k_ref, ...), custom_call_target="tpu_custom_call" | custom-call | tf_op jit(solution)/shard_map/end_state/pallas_call | solution.py:601
  11.7 12.7 %all-to-all-start = ((f32[64,4,128]{2,1,0:T(4,128)}), f32[64,4,128]{2,1,0:T(4,128)S(1)}, u32[]{:S(2)}, u32[]{:S(2)}) async-start(f32[64,4,128]{2,1,0:T(4,128)} %bitcast.13), calls=%async_computation | async-start | bytes 262144 | tf_op jit(solution)/shard_map/all_to_all | solution.py:628
  24.4 0.0 copy-done.3
  24.4 0.1 sqrt_multiply_fusion.gain_ref
  24.5 0.0 copy-done.1
  24.5 4.8 %near.2 = (f32[8,256,128]{2,1,0:T(8,128)}, f32[8,256,128]{2,1,0:T(8,128)}, f32[8,128,128]{2,1,0:T(8,128)}, f32[64,4,128]{2,1,0:T(4,128)S(1)}, f32[2,264,128]{2,1...) custom-call(f32[104,128]{1,0:T(8,128)S(1)} %get-tuple-element.31.info_ref, ...), custom_call_target="tpu_custom_call" | custom-call | flops 4000000 | bytes 8000000 | tf_op jit(solution)/shard_map/near/pallas_call | solution.py:659
  29.3 5.4 %all-to-all-done.pieces_ref = f32[64,4,128]{2,1,0:T(4,128)S(1)} async-done(((f32[64,4,128]{2,1,0:T(4,128)}), f32[64,4,128]{2,1,0:T(4,128)S(1)}, u32[]{:S(2)}, u32[]{:S(2)}) %all-to-all-start) | async-done | bytes 131104 | tf_op jit(solution)/shard_map/all_to_all | solution.py:628
  34.8 0.8 %rank_scan.1 = f32[64,4,128]{2,1,0:T(4,128)} custom-call(f32[64,4,128]{2,1,0:T(4,128)S(1)} %get-tuple-element.41.factor_ref, f32[64,4,128]{2,1,0:T(4,128)S(1)} %all-to-all-done.pieces_ref), custom_call_target="tpu_custom_call" | custom-call | tf_op jit(solution)/shard_map/rank_scan/pallas_call | solution.py:672
  35.5 4.9 %all-to-all-start.1 = ((f32[64,4,128]{2,1,0:T(4,128)}), f32[64,4,128]{2,1,0:T(4,128)S(1)}, u32[]{:S(2)}, u32[]{:S(2)}) async-start(f32[64,4,128]{2,1,0:T(4,128)} %rank_scan.1), calls=%async_computation.1 | async-start | bytes 262144 | tf_op jit(solution)/shard_map/all_to_all | solution.py:681
  40.5 5.0 %near.3 = (f32[6,256,128]{2,1,0:T(8,128)S(1)}, f32[6,256,128]{2,1,0:T(8,128)S(1)}, f32[6,128,128]{2,1,0:T(8,128)S(1)}, f32[2,256,128]{2,1,0:T(8,128)}, f32[2,256,128]{2,1,0:T(8,128)}, /*index=5*/f32[2,128,128]{2,1,0:T(8,128)}) custom-call(f32[104,128]{1,0:T(8,128)S(1)} %get-tuple-element.31.info_ref, bf16[2,2048]{1,0:T(2,128)(2,1)S(1)} %get-tuple-element.35.rim_ref, ...), custom_call_target="tpu_custom_call" | custom-call | flops 4000000 | bytes 8000000 | tf_op jit(solution)/shard_map/near/pallas_call | solution.py:659
  45.4 5.4 %all-to-all-done.1 = f32[64,4,128]{2,1,0:T(4,128)S(1)} async-done(((f32[64,4,128]{2,1,0:T(4,128)}), f32[64,4,128]{2,1,0:T(4,128)S(1)}, u32[]{:S(2)}, u32[]{:S(2)}) %all-to-all-start.1) | async-done | bytes 131104 | tf_op jit(solution)/shard_map/all_to_all | solution.py:681
  50.8 0.0 copy-start.2
  50.8 3.7 %stream.1 = (f32[256,2048]{1,0:T(8,128)}, f32[256,2048]{1,0:T(8,128)S(1)}, f32[2,128]{1,0:T(2,128)S(1)}) custom-call(f32[104,128]{1,0:T(8,128)S(1)} %get-tuple-element.31.info_ref, f32[16,2048]{1,0:T(8,128)S(1)} %copy-done, f32[16,2048]{1,0:T(8,128)S(1)} %sqrt_multiply_fusion.gain_ref, f32[16,16,128]{2,1,0:T(8,128)S(1)} %bitcast.8, ...), custom_call_target="tpu_custom_call" | custom-call | tf_op jit(solution)/shard_map/stream/pallas_call | solution.py:683
  54.6 3.0 %collective-permute-start.3 = (f32[2,128]{1,0:T(2,128)S(1)}, f32[2,128]{1,0:T(2,128)S(1)}, u32[]{:S(2)}, u32[]{:S(2)}) collective-permute-start(f32[2,128]{1,0:T(2,128)S(1)} %get-tuple-element.55), channel_id=1, source_target_pairs={{0,2},{1,3},{2,0},{3,1},{4,6},{5,7},{6,4},{7,5},{8,10},{9,11},{10,... | collective-permute-start | bytes 3080 | tf_op jit(solution)/shard_map/ppermute | solution.py:547
  57.6 0.8 %collective-permute-start.2 = (f32[2,128]{1,0:T(2,128)S(1)}, f32[2,128]{1,0:T(2,128)S(1)}, u32[]{:S(2)}, u32[]{:S(2)}) collective-permute-start(f32[2,128]{1,0:T(2,128)S(1)} %get-tuple-element.55), channel_id=1, source_target_pairs={{0,3},{1,0},{2,1},{3,2},{4,7},{5,4},{6,5},{7,6},{8,11},{9,8},{10,9... | collective-permute-start | bytes 3080 | tf_op jit(solution)/shard_map/ppermute | solution.py:547
  58.4 0.7 %collective-permute-start.1 = (f32[2,128]{1,0:T(2,128)S(1)}, f32[2,128]{1,0:T(2,128)S(1)}, u32[]{:S(2)}, u32[]{:S(2)}) collective-permute-start(f32[2,128]{1,0:T(2,128)S(1)} %get-tuple-element.55), channel_id=1, source_target_pairs={{0,1},{1,2},{2,3},{3,0},{4,5},{5,6},{6,7},{7,4},{8,9},{9,10},{10,1... | collective-permute-start | bytes 3080 | tf_op jit(solution)/shard_map/ppermute | solution.py:547
  59.1 0.0 collective-permute-done.3
  59.1 0.9 %collective-permute-done.2 = f32[2,128]{1,0:T(2,128)S(1)} collective-permute-done((f32[2,128]{1,0:T(2,128)S(1)}, f32[2,128]{1,0:T(2,128)S(1)}, u32[]{:S(2)}, u32[]{:S(2)}) %collective-permute-start.2) | collective-permute-done | bytes 1056 | tf_op jit(solution)/shard_map/ppermute | solution.py:547
  60.0 2.0 %collective-permute-done.1 = f32[2,128]{1,0:T(2,128)S(1)} collective-permute-done((f32[2,128]{1,0:T(2,128)S(1)}, f32[2,128]{1,0:T(2,128)S(1)}, u32[]{:S(2)}, u32[]{:S(2)}) %collective-permute-start.1) | collective-permute-done | bytes 1056 | tf_op jit(solution)/shard_map/ppermute | solution.py:547
  62.0 0.0 copy-done.2
  62.0 1.5 %norm.1 = (f32[256,2048]{1,0:T(8,128)}, f32[256,2048]{1,0:T(8,128)}) custom-call(f32[4,2,128]{2,1,0:T(2,128)S(1)} %pad_maximum_fusion.power_ref, f32[1,2048]{1,0:T(1,128)S(1)} %bitcast.11, f32[256,2048]{1,0:T(8,128)S(1)} %get-tuple-element.56.stream_ref, f32[256,2048]{1,0:T(8,128)} %get-tuple-element.57.stream_in), custom_call_target="tpu_custom_call", output_to_operand_aliasing={{1}: (3, {})} | custom-call | tf_op jit(solution)/shard_map/norm/pallas_call | solution.py:716
  (1 shorter events, 0.0 us)
Async XLA Ops:
  1.6 4.8 %copy-start = (f32[16,2048]{1,0:T(8,128)S(1)}, f32[16,2048]{1,0:T(8,128)}, u32[]{:S(2)}) copy-start(f32[16,2048]{1,0:T(8,128)} %rate_ref.7) | copy-start | bytes 393220
  1.6 4.8 %collective-permute-start = (bf16[3,2,2048]{2,1,0:T(2,128)(2,1)S(1)}, bf16[3,2,2048]{2,1,0:T(2,128)(2,1)S(1)}, u32[]{:S(2)}, u32[]{:S(2)}) collective-permute-start(bf16[3,2,2048]{2,1,0:T(2,128)(2,1)S(1)} %rims.1), channel_id=1, source_target_pairs={{0,4},{4,8},{8,12},{12,16},{16,20},{20,24},{24,28},{28,32},{32,36}... | collective-permute-start | bytes 73736 | tf_op jit(solution)/shard_map/ppermute | solution.py:547
  6.4 18.0 %copy-start.3 = (f32[16,2048]{1,0:T(8,128)S(1)}, f32[16,2048]{1,0:T(8,128)}, u32[]{:S(2)}) copy-start(f32[16,2048]{1,0:T(8,128)} %param.15) | copy-start | bytes 393220
  6.4 18.1 %copy-start.1 = (f32[2048]{0:T(1024)S(1)}, f32[2048]{0:T(1024)}, u32[]{:S(2)}) copy-start(f32[2048]{0:T(1024)} %param.16) | copy-start | bytes 24580
  11.7 23.1 %all-to-all-start = ((f32[64,4,128]{2,1,0:T(4,128)}), f32[64,4,128]{2,1,0:T(4,128)S(1)}, u32[]{:S(2)}, u32[]{:S(2)}) async-start(f32[64,4,128]{2,1,0:T(4,128)} %bitcast.13), calls=%async_computation | async-start | bytes 262144 | tf_op jit(solution)/shard_map/all_to_all | solution.py:628
  35.5 15.3 %all-to-all-start.1 = ((f32[64,4,128]{2,1,0:T(4,128)}), f32[64,4,128]{2,1,0:T(4,128)S(1)}, u32[]{:S(2)}, u32[]{:S(2)}) async-start(f32[64,4,128]{2,1,0:T(4,128)} %rank_scan.1), calls=%async_computation.1 | async-start | bytes 262144 | tf_op jit(solution)/shard_map/all_to_all | solution.py:681
  50.8 11.2 %copy-start.2 = (f32[2048]{0:T(1024)S(1)}, f32[2048]{0:T(1024)}, u32[]{:S(2)}) copy-start(f32[2048]{0:T(1024)} %param.17) | copy-start | bytes 24580
  54.6 4.5 %collective-permute-start.3 = (f32[2,128]{1,0:T(2,128)S(1)}, f32[2,128]{1,0:T(2,128)S(1)}, u32[]{:S(2)}, u32[]{:S(2)}) collective-permute-start(f32[2,128]{1,0:T(2,128)S(1)} %get-tuple-element.55), channel_id=1, source_target_pairs={{0,2},{1,3},{2,0},{3,1},{4,6},{5,7},{6,4},{7,5},{8,10},{9,11},{10,... | collective-permute-start | bytes 3080 | tf_op jit(solution)/shard_map/ppermute | solution.py:547
  57.6 2.4 %collective-permute-start.2 = (f32[2,128]{1,0:T(2,128)S(1)}, f32[2,128]{1,0:T(2,128)S(1)}, u32[]{:S(2)}, u32[]{:S(2)}) collective-permute-start(f32[2,128]{1,0:T(2,128)S(1)} %get-tuple-element.55), channel_id=1, source_target_pairs={{0,3},{1,0},{2,1},{3,2},{4,7},{5,4},{6,5},{7,6},{8,11},{9,8},{10,9... | collective-permute-start | bytes 3080 | tf_op jit(solution)/shard_map/ppermute | solution.py:547
  58.4 3.6 %collective-permute-start.1 = (f32[2,128]{1,0:T(2,128)S(1)}, f32[2,128]{1,0:T(2,128)S(1)}, u32[]{:S(2)}, u32[]{:S(2)}) collective-permute-start(f32[2,128]{1,0:T(2,128)S(1)} %get-tuple-element.55), channel_id=1, source_target_pairs={{0,1},{1,2},{2,3},{3,0},{4,5},{5,6},{6,7},{7,4},{8,9},{9,10},{10,1... | collective-permute-start | bytes 3080 | tf_op jit(solution)/shard_map/ppermute | solution.py:547

commit v5 on v4

--- a/solution.py
+++ b/solution.py
@@ -145,12 +145,10 @@
         copy.wait()
 
 
-def end_kernel(rows, poles, info_ref, k_ref, v_ref, rim_ref, taps_ref, rate_ref, gated_a, gated_hbm, end_hbm, rim_next, taps_next, gated_b, end_ref, kx, vx, gx, decay_ref, mends, out_sems, end_sems):
+def end_kernel(rows, poles, info_ref, k_ref, v_ref, taps_ref, rate_ref, gated_a, gated_hbm, end_ref, gated_b, kx, vx, gx, decay_ref, mends, out_sems):
     span = rows // CHUNKS
     phase = lax.broadcasted_iota(jnp.int32, (CHUNKS, LANES), 0)
     groups = k_ref.shape[1] // GROUP
-    rim_next[...] = rim_ref[0]
-    taps_next[...] = taps_ref[0]
     last = jnp.int32(0)
     mended = jnp.int32(0)
     for i in range(SEGMENTS):
@@ -170,17 +168,13 @@
     def store(here):
         return pltpu.make_async_copy(gated_b.at[here], gated_hbm.at[here], out_sems.at[here])
 
-    def send(group):
-        here = pl.ds(group * inner, inner)
-        return pltpu.make_async_copy(end_ref.at[here], end_hbm.at[here], end_sems.at[group])
-
     def one_group(group, first, gated_ref):
         @pl.loop(group * inner, (group + 1) * inner)
         def _(part):
             lanes = lanes_at(part)
             here = part - first * inner
             for i, source, target in ((1, k_ref, kx), (2, v_ref, vx)):
-                target[6:8, :] = rim_ref[i, :, lanes].astype(F32)
+                target[6:8, :] = jnp.zeros((2, LANES), F32)
                 target[8:, :] = source[:, lanes].astype(F32)
             decay_ref[...] = jnp.exp(-float(CHUNKS) * rate_ref[:, lanes])
             lines = [[taps_ref[i, j : j + 1, lanes] for j in range(3)] for i in (1, 2)]
@@ -230,14 +224,59 @@
             if first:
                 store(here).start()
 
-        send(group).start()
-
     middle = gated_a.shape[0] // inner
     pl.loop(middle, groups)(lambda group: one_group(group, middle, gated_b))
     pl.loop(0, middle)(lambda group: one_group(group, 0, gated_a))
     for here in range(gated_b.shape[0]):
         store(here).wait()
-    for group in range(groups):
+
+
+def edge_kernel(rows, poles, info_ref, k_ref, v_ref, rim_ref, taps_ref, rate_ref, partial_ref, end_hbm, edge_ref, rim_next, taps_next, end_ref, sems):
+    rim_next[...] = rim_ref[0]
+    taps_next[...] = taps_ref[0]
+    clear = [jnp.ones((1, LANES), F32) for _ in range(4)]
+    for i in range(SEGMENTS):
+        low = INSIDE.start + i * CHUNKS
+        inside = info_ref[low : low + 1, :]
+        for j, (first, last) in enumerate(((0, 0), (-1, -1), (1, 1), (1, rows - 1))):
+            clear[j] = jnp.where((inside >= float(first)) & (inside <= float(last)), 0.0, clear[j])
+    at_zero, at_before, at_one, after = clear
+    inner = GROUP // LANES
+
+    def send(group):
+        here = pl.ds(group * inner, inner)
+        return pltpu.make_async_copy(end_ref.at[here], end_hbm.at[here], sems.at[group])
+
+    @pl.loop(0, sems.shape[0])
+    def _(group):
+        @pl.loop(group * inner, (group + 1) * inner)
+        def _(part):
+            lanes = lanes_at(part)
+            own = [[], []]
+            full = [[], []]
+            for i, source in ((1, k_ref), (2, v_ref)):
+                taps = [taps_ref[i, j : j + 1, lanes] for j in range(3)]
+                top = source[:16, lanes].astype(F32)
+                rim = rim_ref[i, :, lanes].astype(F32)
+                zero, one, back, far = top[0:1], top[1:2], rim[1:2], rim[0:1]
+                own[0].append(taps[0] * zero)
+                own[1].append(taps[0] * one + at_one * (taps[1] * zero))
+                full[0].append(own[0][-1] + at_zero * (taps[1] * back + at_before * (taps[2] * far)))
+                full[1].append(own[1][-1] + (at_one * at_zero) * (taps[2] * back))
+            made = [full[row][0] * full[row][1] for row in range(2)]
+            change = [after * (made[row] - own[row][0] * own[row][1]) for row in range(2)]
+            for row in range(2):
+                edge_ref[part, row : row + 1, :] = made[row]
+            rate = rate_ref[:, lanes]
+            end_ref[part] = (
+                partial_ref[part]
+                + jnp.exp(-float(rows - 1) * rate) * change[0]
+                + jnp.exp(-float(rows - 2) * rate) * change[1]
+            )
+
+        send(group).start()
+
+    for group in range(sems.shape[0]):
         send(group).wait()
 
 
@@ -275,7 +314,7 @@
         copy.wait()
 
 
-def near_kernel(rows, poles, first, early, info_ref, rim_ref, taps_ref, rate_ref, gain_ref, skip_ref, gated_in, q_in, r_in, q_hbm, res_hbm, gated_hbm, *others):
+def near_kernel(rows, poles, first, early, info_ref, rim_ref, taps_ref, rate_ref, gain_ref, skip_ref, edge_ref, gated_in, q_in, r_in, q_hbm, res_hbm, gated_hbm, *others):
     if early:
         outs, (factor_ref, gated_next, q_next, r_next, *others) = others[:3], others[3:]
         near_ref, query_ref, local_ref, q_ref, r_ref, qx, rx, decay_ref, own_sems, far_sems, next_sems = others
@@ -376,6 +415,9 @@
                 query = qx[pl.ds(8 + place, CHUNKS, stride=span + 1), :]
                 query_short = taps[0] * query + taps[1] * carry[0] + taps[2] * carry[1]
                 gated = gated_ref[here, pl.ds(place, CHUNKS, stride=span + 1), :]
+                if place < 2:
+                    edge = spread(edge_ref[here + first, place : place + 1, :])
+                    gated = jnp.where(chunk == 0, edge, gated)
                 states = [decay[m] * carry[2 + m] + gated for m in range(poles)]
                 total = skip * gated
                 for m in range(poles):
@@ -598,31 +640,43 @@
         name="fetch",
     )(lengths, key_proj, value_proj, query_proj, residual, short_filter)
     info, k_here, v_here, taps_here = map(close_by, (info, k_here, v_here, taps_here))
-    gated_a, gated_b, end, query_rim, query_taps = pl.pallas_call(
+    gated_a, gated_b, partial = pl.pallas_call(
         functools.partial(end_kernel, rows, poles),
-        in_specs=[near_by] * 6,
-        out_specs=[near_by, outside, outside, near_by, near_by],
+        in_specs=[near_by] * 5,
+        out_specs=[near_by, outside, near_by],
         out_shape=[
             kept_near(early, pitch, LANES),
             pltpu.HBM((late, pitch, LANES), F32),
-            pltpu.HBM((parts, poles, LANES), F32),
-            pltpu.VMEM((2, width), BF16),
-            kept_near(3, width),
+            kept_near(parts, poles, LANES),
         ],
         scratch_shapes=[
             pltpu.VMEM((late, pitch, LANES), F32),
-            pltpu.VMEM((parts, poles, LANES), F32),
             pltpu.VMEM((rows + 8, LANES), F32),
             pltpu.VMEM((rows + 8, LANES), F32),
             pltpu.VMEM((rows, LANES), F32),
             pltpu.VMEM((poles, LANES), F32),
             pltpu.SMEM((2, 8), jnp.int32),
             pltpu.SemaphoreType.DMA((late,)),
-            pltpu.SemaphoreType.DMA((groups,)),
         ],
         compiler_params=limit,
+        cost_estimate=pl.CostEstimate(flops=4000000, bytes_accessed=8000000, transcendentals=0),
         name="end_state",
-    )(info, k_here, v_here, rims, taps_here, decay_rate)
+    )(info, k_here, v_here, taps_here, decay_rate)
+    end, edges, query_rim, query_taps = pl.pallas_call(
+        functools.partial(edge_kernel, rows, poles),
+        in_specs=[near_by] * 7,
+        out_specs=[outside, near_by, near_by, near_by],
+        out_shape=[
+            pltpu.HBM((parts, poles, LANES), F32),
+            kept_near(parts, CHUNKS, LANES),
+            pltpu.VMEM((2, width), BF16),
+            kept_near(3, width),
+        ],
+        scratch_shapes=[pltpu.VMEM((parts, poles, LANES), F32), pltpu.SemaphoreType.DMA((groups,))],
+        compiler_params=limit,
+        name="edges",
+    )(info, k_here, v_here, rims, taps_here, decay_rate, close_by(partial))
+    edges = close_by(edges)
     query_rim, query_taps = map(close_by, (query_rim, query_taps))
 
     pieces = lax.all_to_all(end.reshape(ranks, held, LANES), "ctx", 0, 0, tiled=True)
@@ -630,7 +684,7 @@
     def near_side(first, count, gated, q_part, r_part, early):
         block = (count, rows, LANES)
         states = (count, poles * CHUNKS, LANES)
-        given = [info, query_rim, query_taps, decay_rate, pole_gain, skip, *map(close_by, (gated, q_part, r_part))]
+        given = [info, query_rim, query_taps, decay_rate, pole_gain, skip, edges, *map(close_by, (gated, q_part, r_part))]
         fetched = [query_proj, residual, far_off(gated_b)]
         scratch = [
             pltpu.VMEM((rows, count * LANES), BF16),

time: 63.8 us -> 62.2 us (0.975)
  starting transfers between devices: 25.2 us -> 23.2 us
    all_to_all x1, starting transfers between devices: 12.7 us -> 10.7 us  [on_device(): lax.all_to_all(end.reshape(ranks, held, LANES), 'ctx', 0, 0, tiled=True)]
    pallas_call x0 -> x1, Pallas kernels: none -> 1.08 us  [on_device(): pl.pallas_call(functools.partial(edge_kernel, rows, poles), in_specs=[nea...]
    pallas_call x1, Pallas kernels: 5.25 us -> 4.56 us  [on_device(): pl.pallas_call(functools.partial(end_kernel, rows, poles), in_specs=[near...]
  transfers between devices with their start and end apart: 6 -> 6, of which waited for: 4 -> 4; matrix products, arithmetic and copies ran while one was open for 0% -> 0% of each run, Pallas kernels for 18% -> 26%
where the time goes in v5:
time: 62.2 us; the launch traced here: 61.9 us
  Pallas kernels  24.1 us (39%)
  starting transfers between devices  23.2 us (37%)
  waiting for transfers between devices  13.7 us (22%)
  between operations  0.78 us (1%)
    all_to_all x1, starting transfers between devices, on_device(): lax.all_to_all(end.reshape(ranks, held, LANES), 'ctx', 0, 0, tiled=True)  10.7 us
    pallas_call x2, Pallas kernels, near_side(): pl.pallas_call(functools.partial(near_kernel, rows, poles, first, early),...  9.8 us
    ppermute x4, starting transfers between devices, shifted(): lax.ppermute(block, axis, [(i, (i + distance) % count) for i in range(cou...  7.57 us
    all_to_all x1, waiting for transfers between devices, on_device(): lax.all_to_all(end.reshape(ranks, held, LANES), 'ctx', 0, 0, tiled=True)  5.42 us
    all_to_all x1, waiting for transfers between devices, on_device(): lax.all_to_all(scanned, 'ctx', 0, 0, tiled=True)  5.38 us
    all_to_all x1, starting transfers between devices, on_device(): lax.all_to_all(scanned, 'ctx', 0, 0, tiled=True)  4.93 us
    pallas_call x1, Pallas kernels, on_device(): pl.pallas_call(functools.partial(end_kernel, rows, poles), in_specs=[near...  4.56 us
    pallas_call x1, Pallas kernels, on_device(): pl.pallas_call(functools.partial(stream_kernel, rows, poles), in_specs=[n...  3.74 us
  transfers between devices with their start and end apart: 6, of which 4 were waited for; matrix products, arithmetic and copies ran while one was open for 0% of the time, Pallas kernels for 26%

profile of v5, /device:TPU:1, one launch (start us, length us, event | category | flops | bytes accessed | tf_op | source)
XLA Modules:
  0.0 61.9 jit_solution(6865290662614348489)
XLA Ops:
  0.6 0.9 %rims.1 = bf16[3,2,2048]{2,1,0:T(2,128)(2,1)S(1)} custom-call(bf16[256,2048]{1,0:T(8,128)(2,1)} %q_hbm.7, bf16[256,2048]{1,0:T(8,128)(2,1)} %k_hbm.3, bf16[256,2048]{1,0:T(8,128)(2,1)} %v_hbm.3), custom_call_target="tpu_custom_call" | custom-call | tf_op jit(solution)/shard_map/rims/pallas_call | solution.py:609
  1.6 0.0 copy-start
  1.6 3.1 %collective-permute-start = (bf16[3,2,2048]{2,1,0:T(2,128)(2,1)S(1)}, bf16[3,2,2048]{2,1,0:T(2,128)(2,1)S(1)}, u32[]{:S(2)}, u32[]{:S(2)}) collective-permute-start(bf16[3,2,2048]{2,1,0:T(2,128)(2,1)S(1)} %rims.1), channel_id=1, source_target_pairs={{0,4},{4,8},{8,12},{12,16},{16,20},{20,24},{24,28},{28,32},{32,36}... | collective-permute-start | bytes 73736 | tf_op jit(solution)/shard_map/ppermute | solution.py:589
  4.7 1.7 %fetch.1 = (bf16[256,2048]{1,0:T(8,128)(2,1)S(1)}, bf16[256,2048]{1,0:T(8,128)(2,1)S(1)}, bf16[256,256]{1,0:T(8,128)(2,1)S(1)}, bf16[256,256]{1,0:T(8,128)(2,1)S...) custom-call(s32[4]{0:T(128)} %lengths_hbm.1, bf16[256,2048]{1,0:T(8,128)(2,1)} %k_hbm.3, bf16[256,2048]{1,0:T(8,128)(2,1)} %v_hbm.3, ...), custom_call_target="tpu_custom_call" | custom-call | flops 1000000 | bytes 5000000 | tf_op jit(solution)/shard_map/fetch/pallas_call | solution.py:625
  6.4 0.0 copy-done
  6.4 0.0 copy-start.3
  6.4 4.6 %end_state.1 = (f32[8,264,128]{2,1,0:T(8,128)S(1)}, f32[8,264,128]{2,1,0:T(8,128)}, f32[16,16,128]{2,1,0:T(8,128)S(1)}) custom-call(f32[104,128]{1,0:T(8,128)S(1)} %get-tuple-element.33.info_ref, bf16[256,2048]{1,0:T(8,128)(2,1)S(1)} %get-tuple-element.34.k_ref, bf16[256,2048]{1,0:T(8,128)(2,1)S(1)} %get-tuple-element.35.v_ref, ...), custom_call_target="tpu_custom_call" | custom-call | flops 4000000 | bytes 8000000 | tf_op jit(solution)/shard_map/end_state/pallas_call | solution.py:643
  11.0 0.0 copy-start.1
  11.0 0.0 collective-permute-done.rim_ref
  11.0 1.1 %edges.1 = (f32[16,16,128]{2,1,0:T(8,128)}, f32[16,8,128]{2,1,0:T(8,128)S(1)}, bf16[2,2048]{1,0:T(2,128)(2,1)S(1)}, f32[3,2048]{1,0:T(4,128)S(1)}) custom-call(f32[104,128]{1,0:T(8,128)S(1)} %get-tuple-element.33.info_ref, bf16[256,2048]{1,0:T(8,128)(2,1)S(1)} %get-tuple-element.34.k_ref, bf16[256,2048]{1,0:T(8,128)(2,1)S(1)} %get-tuple-element.35.v_ref, ...), custom_call_target="tpu_custom_call" | custom-call | tf_op jit(solution)/shard_map/edges/pallas_call | solution.py:665
  12.1 10.7 %all-to-all-start = ((f32[64,4,128]{2,1,0:T(4,128)}), f32[64,4,128]{2,1,0:T(4,128)S(1)}, u32[]{:S(2)}, u32[]{:S(2)}) async-start(f32[64,4,128]{2,1,0:T(4,128)} %bitcast.13), calls=%async_computation | async-start | bytes 262144 | tf_op jit(solution)/shard_map/all_to_all | solution.py:682
  22.8 0.0 copy-done.3
  22.8 0.1 sqrt_multiply_fusion.gain_ref
  22.9 0.0 copy-done.1
  22.9 4.8 %near.2 = (f32[8,256,128]{2,1,0:T(8,128)}, f32[8,256,128]{2,1,0:T(8,128)}, f32[8,128,128]{2,1,0:T(8,128)}, f32[64,4,128]{2,1,0:T(4,128)S(1)}, f32[2,264,128]{2,1...) custom-call(f32[104,128]{1,0:T(8,128)S(1)} %get-tuple-element.33.info_ref, ...), custom_call_target="tpu_custom_call" | custom-call | flops 4000000 | bytes 8000000 | tf_op jit(solution)/shard_map/near/pallas_call | solution.py:713
  27.7 5.4 %all-to-all-done.pieces_ref = f32[64,4,128]{2,1,0:T(4,128)S(1)} async-done(((f32[64,4,128]{2,1,0:T(4,128)}), f32[64,4,128]{2,1,0:T(4,128)S(1)}, u32[]{:S(2)}, u32[]{:S(2)}) %all-to-all-start) | async-done | bytes 131104 | tf_op jit(solution)/shard_map/all_to_all | solution.py:682
  33.1 0.8 %rank_scan.1 = f32[64,4,128]{2,1,0:T(4,128)} custom-call(f32[64,4,128]{2,1,0:T(4,128)S(1)} %get-tuple-element.45.factor_ref, f32[64,4,128]{2,1,0:T(4,128)S(1)} %all-to-all-done.pieces_ref), custom_call_target="tpu_custom_call" | custom-call | tf_op jit(solution)/shard_map/rank_scan/pallas_call | solution.py:726
  33.9 4.9 %all-to-all-start.1 = ((f32[64,4,128]{2,1,0:T(4,128)}), f32[64,4,128]{2,1,0:T(4,128)S(1)}, u32[]{:S(2)}, u32[]{:S(2)}) async-start(f32[64,4,128]{2,1,0:T(4,128)} %rank_scan.1), calls=%async_computation.1 | async-start | bytes 262144 | tf_op jit(solution)/shard_map/all_to_all | solution.py:735
  38.9 5.0 %near.3 = (f32[6,256,128]{2,1,0:T(8,128)S(1)}, f32[6,256,128]{2,1,0:T(8,128)S(1)}, f32[6,128,128]{2,1,0:T(8,128)S(1)}, f32[2,256,128]{2,1,0:T(8,128)}, f32[2,256,128]{2,1,0:T(8,128)}, /*index=5*/f32[2,128,128]{2,1,0:T(8,128)}) custom-call(f32[104,128]{1,0:T(8,128)S(1)} %get-tuple-element.33.info_ref, bf16[2,2048]{1,0:T(2,128)(2,1)S(1)} %get-tuple-element.38.rim_ref, ...), custom_call_target="tpu_custom_call" | custom-call | flops 4000000 | bytes 8000000 | tf_op jit(solution)/shard_map/near/pallas_call | solution.py:713
  43.9 5.4 %all-to-all-done.1 = f32[64,4,128]{2,1,0:T(4,128)S(1)} async-done(((f32[64,4,128]{2,1,0:T(4,128)}), f32[64,4,128]{2,1,0:T(4,128)S(1)}, u32[]{:S(2)}, u32[]{:S(2)}) %all-to-all-start.1) | async-done | bytes 131104 | tf_op jit(solution)/shard_map/all_to_all | solution.py:735
  49.2 0.0 copy-start.2
  49.2 3.7 %stream.1 = (f32[256,2048]{1,0:T(8,128)}, f32[256,2048]{1,0:T(8,128)S(1)}, f32[2,128]{1,0:T(2,128)S(1)}) custom-call(f32[104,128]{1,0:T(8,128)S(1)} %get-tuple-element.33.info_ref, f32[16,2048]{1,0:T(8,128)S(1)} %copy-done, f32[16,2048]{1,0:T(8,128)S(1)} %sqrt_multiply_fusion.gain_ref, f32[16,16,128]{2,1,0:T(8,128)S(1)} %bitcast.8, ...), custom_call_target="tpu_custom_call" | custom-call | tf_op jit(solution)/shard_map/stream/pallas_call | solution.py:737
  53.0 3.0 %collective-permute-start.3 = (f32[2,128]{1,0:T(2,128)S(1)}, f32[2,128]{1,0:T(2,128)S(1)}, u32[]{:S(2)}, u32[]{:S(2)}) collective-permute-start(f32[2,128]{1,0:T(2,128)S(1)} %get-tuple-element.59), channel_id=1, source_target_pairs={{0,2},{1,3},{2,0},{3,1},{4,6},{5,7},{6,4},{7,5},{8,10},{9,11},{10,... | collective-permute-start | bytes 3080 | tf_op jit(solution)/shard_map/ppermute | solution.py:589
  56.0 0.8 %collective-permute-start.2 = (f32[2,128]{1,0:T(2,128)S(1)}, f32[2,128]{1,0:T(2,128)S(1)}, u32[]{:S(2)}, u32[]{:S(2)}) collective-permute-start(f32[2,128]{1,0:T(2,128)S(1)} %get-tuple-element.59), channel_id=1, source_target_pairs={{0,3},{1,0},{2,1},{3,2},{4,7},{5,4},{6,5},{7,6},{8,11},{9,8},{10,9... | collective-permute-start | bytes 3080 | tf_op jit(solution)/shard_map/ppermute | solution.py:589
  56.8 0.7 %collective-permute-start.1 = (f32[2,128]{1,0:T(2,128)S(1)}, f32[2,128]{1,0:T(2,128)S(1)}, u32[]{:S(2)}, u32[]{:S(2)}) collective-permute-start(f32[2,128]{1,0:T(2,128)S(1)} %get-tuple-element.59), channel_id=1, source_target_pairs={{0,1},{1,2},{2,3},{3,0},{4,5},{5,6},{6,7},{7,4},{8,9},{9,10},{10,1... | collective-permute-start | bytes 3080 | tf_op jit(solution)/shard_map/ppermute | solution.py:589
  57.4 0.0 collective-permute-done.3
  57.5 0.9 %collective-permute-done.2 = f32[2,128]{1,0:T(2,128)S(1)} collective-permute-done((f32[2,128]{1,0:T(2,128)S(1)}, f32[2,128]{1,0:T(2,128)S(1)}, u32[]{:S(2)}, u32[]{:S(2)}) %collective-permute-start.2) | collective-permute-done | bytes 1056 | tf_op jit(solution)/shard_map/ppermute | solution.py:589
  58.4 2.0 %collective-permute-done.1 = f32[2,128]{1,0:T(2,128)S(1)} collective-permute-done((f32[2,128]{1,0:T(2,128)S(1)}, f32[2,128]{1,0:T(2,128)S(1)}, u32[]{:S(2)}, u32[]{:S(2)}) %collective-permute-start.1) | collective-permute-done | bytes 1056 | tf_op jit(solution)/shard_map/ppermute | solution.py:589
  60.4 0.0 copy-done.2
  60.4 1.5 %norm.1 = (f32[256,2048]{1,0:T(8,128)}, f32[256,2048]{1,0:T(8,128)}) custom-call(f32[4,2,128]{2,1,0:T(2,128)S(1)} %pad_maximum_fusion.power_ref, f32[1,2048]{1,0:T(1,128)S(1)} %bitcast.11, f32[256,2048]{1,0:T(8,128)S(1)} %get-tuple-element.60.stream_ref, f32[256,2048]{1,0:T(8,128)} %get-tuple-element.61.stream_in), custom_call_target="tpu_custom_call", output_to_operand_aliasing={{1}: (3, {})} | custom-call | tf_op jit(solution)/shard_map/norm/pallas_call | solution.py:770
  (1 shorter events, 0.0 us)
Async XLA Ops:
  1.6 4.8 %copy-start = (f32[16,2048]{1,0:T(8,128)S(1)}, f32[16,2048]{1,0:T(8,128)}, u32[]{:S(2)}) copy-start(f32[16,2048]{1,0:T(8,128)} %rate_ref.9) | copy-start | bytes 393220
  1.6 9.4 %collective-permute-start = (bf16[3,2,2048]{2,1,0:T(2,128)(2,1)S(1)}, bf16[3,2,2048]{2,1,0:T(2,128)(2,1)S(1)}, u32[]{:S(2)}, u32[]{:S(2)}) collective-permute-start(bf16[3,2,2048]{2,1,0:T(2,128)(2,1)S(1)} %rims.1), channel_id=1, source_target_pairs={{0,4},{4,8},{8,12},{12,16},{16,20},{20,24},{24,28},{28,32},{32,36}... | collective-permute-start | bytes 73736 | tf_op jit(solution)/shard_map/ppermute | solution.py:589
  6.4 16.4 %copy-start.3 = (f32[16,2048]{1,0:T(8,128)S(1)}, f32[16,2048]{1,0:T(8,128)}, u32[]{:S(2)}) copy-start(f32[16,2048]{1,0:T(8,128)} %param.15) | copy-start | bytes 393220
  11.0 11.9 %copy-start.1 = (f32[2048]{0:T(1024)S(1)}, f32[2048]{0:T(1024)}, u32[]{:S(2)}) copy-start(f32[2048]{0:T(1024)} %param.16) | copy-start | bytes 24580
  12.1 21.1 %all-to-all-start = ((f32[64,4,128]{2,1,0:T(4,128)}), f32[64,4,128]{2,1,0:T(4,128)S(1)}, u32[]{:S(2)}, u32[]{:S(2)}) async-start(f32[64,4,128]{2,1,0:T(4,128)} %bitcast.13), calls=%async_computation | async-start | bytes 262144 | tf_op jit(solution)/shard_map/all_to_all | solution.py:682
  33.9 15.3 %all-to-all-start.1 = ((f32[64,4,128]{2,1,0:T(4,128)}), f32[64,4,128]{2,1,0:T(4,128)S(1)}, u32[]{:S(2)}, u32[]{:S(2)}) async-start(f32[64,4,128]{2,1,0:T(4,128)} %rank_scan.1), calls=%async_computation.1 | async-start | bytes 262144 | tf_op jit(solution)/shard_map/all_to_all | solution.py:735
  49.2 11.2 %copy-start.2 = (f32[2048]{0:T(1024)S(1)}, f32[2048]{0:T(1024)}, u32[]{:S(2)}) copy-start(f32[2048]{0:T(1024)} %param.17) | copy-start | bytes 24580
  53.0 4.5 %collective-permute-start.3 = (f32[2,128]{1,0:T(2,128)S(1)}, f32[2,128]{1,0:T(2,128)S(1)}, u32[]{:S(2)}, u32[]{:S(2)}) collective-permute-start(f32[2,128]{1,0:T(2,128)S(1)} %get-tuple-element.59), channel_id=1, source_target_pairs={{0,2},{1,3},{2,0},{3,1},{4,6},{5,7},{6,4},{7,5},{8,10},{9,11},{10,... | collective-permute-start | bytes 3080 | tf_op jit(solution)/shard_map/ppermute | solution.py:589
  56.0 2.4 %collective-permute-start.2 = (f32[2,128]{1,0:T(2,128)S(1)}, f32[2,128]{1,0:T(2,128)S(1)}, u32[]{:S(2)}, u32[]{:S(2)}) collective-permute-start(f32[2,128]{1,0:T(2,128)S(1)} %get-tuple-element.59), channel_id=1, source_target_pairs={{0,3},{1,0},{2,1},{3,2},{4,7},{5,4},{6,5},{7,6},{8,11},{9,8},{10,9... | collective-permute-start | bytes 3080 | tf_op jit(solution)/shard_map/ppermute | solution.py:589
  56.8 3.6 %collective-permute-start.1 = (f32[2,128]{1,0:T(2,128)S(1)}, f32[2,128]{1,0:T(2,128)S(1)}, u32[]{:S(2)}, u32[]{:S(2)}) collective-permute-start(f32[2,128]{1,0:T(2,128)S(1)} %get-tuple-element.59), channel_id=1, source_target_pairs={{0,1},{1,2},{2,3},{3,0},{4,5},{5,6},{6,7},{7,4},{8,9},{9,10},{10,1... | collective-permute-start | bytes 3080 | tf_op jit(solution)/shard_map/ppermute | solution.py:589

commit v6 on v5

--- a/solution.py
+++ b/solution.py
@@ -247,11 +247,9 @@
         here = pl.ds(group * inner, inner)
         return pltpu.make_async_copy(end_ref.at[here], end_hbm.at[here], sems.at[group])
 
-    @pl.loop(0, sems.shape[0])
-    def _(group):
-        @pl.loop(group * inner, (group + 1) * inner)
-        def _(part):
-            lanes = lanes_at(part)
+    for group in range(sems.shape[0]):
+        for part in range(group * inner, (group + 1) * inner):
+            lanes = slice(part * LANES, (part + 1) * LANES)
             own = [[], []]
             full = [[], []]
             for i, source in ((1, k_ref), (2, v_ref)):

time: 62.2 us -> 62 us (level)
  no operation moved by 1% of the time
where the time goes in v6:
time: 62 us; the launch traced here: 61.7 us
  Pallas kernels  23.8 us (38%)
  starting transfers between devices  23.2 us (37%)
  waiting for transfers between devices  13.7 us (22%)
  between operations  0.78 us (1%)
    all_to_all x1, starting transfers between devices, on_device(): lax.all_to_all(end.reshape(ranks, held, LANES), 'ctx', 0, 0, tiled=True)  10.7 us
    pallas_call x2, Pallas kernels, near_side(): pl.pallas_call(functools.partial(near_kernel, rows, poles, first, early),...  9.8 us
    ppermute x4, starting transfers between devices, shifted(): lax.ppermute(block, axis, [(i, (i + distance) % count) for i in range(cou...  7.57 us
    all_to_all x1, waiting for transfers between devices, on_device(): lax.all_to_all(end.reshape(ranks, held, LANES), 'ctx', 0, 0, tiled=True)  5.42 us
    all_to_all x1, waiting for transfers between devices, on_device(): lax.all_to_all(scanned, 'ctx', 0, 0, tiled=True)  5.38 us
    all_to_all x1, starting transfers between devices, on_device(): lax.all_to_all(scanned, 'ctx', 0, 0, tiled=True)  4.93 us
    pallas_call x1, Pallas kernels, on_device(): pl.pallas_call(functools.partial(end_kernel, rows, poles), in_specs=[near...  4.56 us
    pallas_call x1, Pallas kernels, on_device(): pl.pallas_call(functools.partial(stream_kernel, rows, poles), in_specs=[n...  3.74 us
  transfers between devices with their start and end apart: 6, of which 4 were waited for; matrix products, arithmetic and copies ran while one was open for 0% of the time, Pallas kernels for 26%

profile of v6, /device:TPU:1, one launch (start us, length us, event | category | flops | bytes accessed | tf_op | source)
XLA Modules:
  0.0 61.7 jit_solution(12930561782618285930)
XLA Ops:
  0.6 0.9 %rims.1 = bf16[3,2,2048]{2,1,0:T(2,128)(2,1)S(1)} custom-call(bf16[256,2048]{1,0:T(8,128)(2,1)} %q_hbm.7, bf16[256,2048]{1,0:T(8,128)(2,1)} %k_hbm.3, bf16[256,2048]{1,0:T(8,128)(2,1)} %v_hbm.3), custom_call_target="tpu_custom_call" | custom-call | tf_op jit(solution)/shard_map/rims/pallas_call | solution.py:607
  1.6 0.0 copy-start
  1.6 3.1 %collective-permute-start = (bf16[3,2,2048]{2,1,0:T(2,128)(2,1)S(1)}, bf16[3,2,2048]{2,1,0:T(2,128)(2,1)S(1)}, u32[]{:S(2)}, u32[]{:S(2)}) collective-permute-start(bf16[3,2,2048]{2,1,0:T(2,128)(2,1)S(1)} %rims.1), channel_id=1, source_target_pairs={{0,4},{4,8},{8,12},{12,16},{16,20},{20,24},{24,28},{28,32},{32,36}... | collective-permute-start | bytes 73736 | tf_op jit(solution)/shard_map/ppermute | solution.py:587
  4.7 1.7 %fetch.1 = (bf16[256,2048]{1,0:T(8,128)(2,1)S(1)}, bf16[256,2048]{1,0:T(8,128)(2,1)S(1)}, bf16[256,256]{1,0:T(8,128)(2,1)S(1)}, bf16[256,256]{1,0:T(8,128)(2,1)S...) custom-call(s32[4]{0:T(128)} %lengths_hbm.1, bf16[256,2048]{1,0:T(8,128)(2,1)} %k_hbm.3, bf16[256,2048]{1,0:T(8,128)(2,1)} %v_hbm.3, ...), custom_call_target="tpu_custom_call" | custom-call | flops 1000000 | bytes 5000000 | tf_op jit(solution)/shard_map/fetch/pallas_call | solution.py:623
  6.4 0.0 copy-done
  6.4 0.0 copy-start.3
  6.4 4.6 %end_state.1 = (f32[8,264,128]{2,1,0:T(8,128)S(1)}, f32[8,264,128]{2,1,0:T(8,128)}, f32[16,16,128]{2,1,0:T(8,128)S(1)}) custom-call(f32[104,128]{1,0:T(8,128)S(1)} %get-tuple-element.33.info_ref, bf16[256,2048]{1,0:T(8,128)(2,1)S(1)} %get-tuple-element.34.k_ref, bf16[256,2048]{1,0:T(8,128)(2,1)S(1)} %get-tuple-element.35.v_ref, ...), custom_call_target="tpu_custom_call" | custom-call | flops 4000000 | bytes 8000000 | tf_op jit(solution)/shard_map/end_state/pallas_call | solution.py:641
  11.0 0.0 copy-start.1
  11.0 0.0 collective-permute-done.rim_ref
  11.0 0.8 %edges.1 = (f32[16,16,128]{2,1,0:T(8,128)}, f32[16,8,128]{2,1,0:T(8,128)S(1)}, bf16[2,2048]{1,0:T(2,128)(2,1)S(1)}, f32[3,2048]{1,0:T(4,128)S(1)}) custom-call(f32[104,128]{1,0:T(8,128)S(1)} %get-tuple-element.33.info_ref, bf16[256,2048]{1,0:T(8,128)(2,1)S(1)} %get-tuple-element.34.k_ref, bf16[256,2048]{1,0:T(8,128)(2,1)S(1)} %get-tuple-element.35.v_ref, ...), custom_call_target="tpu_custom_call" | custom-call | tf_op jit(solution)/shard_map/edges/pallas_call | solution.py:663
  11.8 10.7 %all-to-all-start = ((f32[64,4,128]{2,1,0:T(4,128)}), f32[64,4,128]{2,1,0:T(4,128)S(1)}, u32[]{:S(2)}, u32[]{:S(2)}) async-start(f32[64,4,128]{2,1,0:T(4,128)} %bitcast.13), calls=%async_computation | async-start | bytes 262144 | tf_op jit(solution)/shard_map/all_to_all | solution.py:680
  22.5 0.0 copy-done.3
  22.5 0.1 sqrt_multiply_fusion.gain_ref
  22.6 0.0 copy-done.1
  22.7 4.8 %near.2 = (f32[8,256,128]{2,1,0:T(8,128)}, f32[8,256,128]{2,1,0:T(8,128)}, f32[8,128,128]{2,1,0:T(8,128)}, f32[64,4,128]{2,1,0:T(4,128)S(1)}, f32[2,264,128]{2,1...) custom-call(f32[104,128]{1,0:T(8,128)S(1)} %get-tuple-element.33.info_ref, ...), custom_call_target="tpu_custom_call" | custom-call | flops 4000000 | bytes 8000000 | tf_op jit(solution)/shard_map/near/pallas_call | solution.py:711
  27.5 5.4 %all-to-all-done.pieces_ref = f32[64,4,128]{2,1,0:T(4,128)S(1)} async-done(((f32[64,4,128]{2,1,0:T(4,128)}), f32[64,4,128]{2,1,0:T(4,128)S(1)}, u32[]{:S(2)}, u32[]{:S(2)}) %all-to-all-start) | async-done | bytes 131104 | tf_op jit(solution)/shard_map/all_to_all | solution.py:680
  32.9 0.8 %rank_scan.1 = f32[64,4,128]{2,1,0:T(4,128)} custom-call(f32[64,4,128]{2,1,0:T(4,128)S(1)} %get-tuple-element.45.factor_ref, f32[64,4,128]{2,1,0:T(4,128)S(1)} %all-to-all-done.pieces_ref), custom_call_target="tpu_custom_call" | custom-call | tf_op jit(solution)/shard_map/rank_scan/pallas_call | solution.py:724
  33.7 4.9 %all-to-all-start.1 = ((f32[64,4,128]{2,1,0:T(4,128)}), f32[64,4,128]{2,1,0:T(4,128)S(1)}, u32[]{:S(2)}, u32[]{:S(2)}) async-start(f32[64,4,128]{2,1,0:T(4,128)} %rank_scan.1), calls=%async_computation.1 | async-start | bytes 262144 | tf_op jit(solution)/shard_map/all_to_all | solution.py:733
  38.6 5.0 %near.3 = (f32[6,256,128]{2,1,0:T(8,128)S(1)}, f32[6,256,128]{2,1,0:T(8,128)S(1)}, f32[6,128,128]{2,1,0:T(8,128)S(1)}, f32[2,256,128]{2,1,0:T(8,128)}, f32[2,256,128]{2,1,0:T(8,128)}, /*index=5*/f32[2,128,128]{2,1,0:T(8,128)}) custom-call(f32[104,128]{1,0:T(8,128)S(1)} %get-tuple-element.33.info_ref, bf16[2,2048]{1,0:T(2,128)(2,1)S(1)} %get-tuple-element.38.rim_ref, ...), custom_call_target="tpu_custom_call" | custom-call | flops 4000000 | bytes 8000000 | tf_op jit(solution)/shard_map/near/pallas_call | solution.py:711
  43.6 5.4 %all-to-all-done.1 = f32[64,4,128]{2,1,0:T(4,128)S(1)} async-done(((f32[64,4,128]{2,1,0:T(4,128)}), f32[64,4,128]{2,1,0:T(4,128)S(1)}, u32[]{:S(2)}, u32[]{:S(2)}) %all-to-all-start.1) | async-done | bytes 131104 | tf_op jit(solution)/shard_map/all_to_all | solution.py:733
  49.0 0.0 copy-start.2
  49.0 3.7 %stream.1 = (f32[256,2048]{1,0:T(8,128)}, f32[256,2048]{1,0:T(8,128)S(1)}, f32[2,128]{1,0:T(2,128)S(1)}) custom-call(f32[104,128]{1,0:T(8,128)S(1)} %get-tuple-element.33.info_ref, f32[16,2048]{1,0:T(8,128)S(1)} %copy-done, f32[16,2048]{1,0:T(8,128)S(1)} %sqrt_multiply_fusion.gain_ref, f32[16,16,128]{2,1,0:T(8,128)S(1)} %bitcast.8, ...), custom_call_target="tpu_custom_call" | custom-call | tf_op jit(solution)/shard_map/stream/pallas_call | solution.py:735
  52.7 3.0 %collective-permute-start.3 = (f32[2,128]{1,0:T(2,128)S(1)}, f32[2,128]{1,0:T(2,128)S(1)}, u32[]{:S(2)}, u32[]{:S(2)}) collective-permute-start(f32[2,128]{1,0:T(2,128)S(1)} %get-tuple-element.59), channel_id=1, source_target_pairs={{0,2},{1,3},{2,0},{3,1},{4,6},{5,7},{6,4},{7,5},{8,10},{9,11},{10,... | collective-permute-start | bytes 3080 | tf_op jit(solution)/shard_map/ppermute | solution.py:587
  55.7 0.8 %collective-permute-start.2 = (f32[2,128]{1,0:T(2,128)S(1)}, f32[2,128]{1,0:T(2,128)S(1)}, u32[]{:S(2)}, u32[]{:S(2)}) collective-permute-start(f32[2,128]{1,0:T(2,128)S(1)} %get-tuple-element.59), channel_id=1, source_target_pairs={{0,3},{1,0},{2,1},{3,2},{4,7},{5,4},{6,5},{7,6},{8,11},{9,8},{10,9... | collective-permute-start | bytes 3080 | tf_op jit(solution)/shard_map/ppermute | solution.py:587
  56.5 0.7 %collective-permute-start.1 = (f32[2,128]{1,0:T(2,128)S(1)}, f32[2,128]{1,0:T(2,128)S(1)}, u32[]{:S(2)}, u32[]{:S(2)}) collective-permute-start(f32[2,128]{1,0:T(2,128)S(1)} %get-tuple-element.59), channel_id=1, source_target_pairs={{0,1},{1,2},{2,3},{3,0},{4,5},{5,6},{6,7},{7,4},{8,9},{9,10},{10,1... | collective-permute-start | bytes 3080 | tf_op jit(solution)/shard_map/ppermute | solution.py:587
  57.2 0.0 collective-permute-done.3
  57.2 0.9 %collective-permute-done.2 = f32[2,128]{1,0:T(2,128)S(1)} collective-permute-done((f32[2,128]{1,0:T(2,128)S(1)}, f32[2,128]{1,0:T(2,128)S(1)}, u32[]{:S(2)}, u32[]{:S(2)}) %collective-permute-start.2) | collective-permute-done | bytes 1056 | tf_op jit(solution)/shard_map/ppermute | solution.py:587
  58.2 2.0 %collective-permute-done.1 = f32[2,128]{1,0:T(2,128)S(1)} collective-permute-done((f32[2,128]{1,0:T(2,128)S(1)}, f32[2,128]{1,0:T(2,128)S(1)}, u32[]{:S(2)}, u32[]{:S(2)}) %collective-permute-start.1) | collective-permute-done | bytes 1056 | tf_op jit(solution)/shard_map/ppermute | solution.py:587
  60.1 0.0 copy-done.2
  60.2 1.5 %norm.1 = (f32[256,2048]{1,0:T(8,128)}, f32[256,2048]{1,0:T(8,128)}) custom-call(f32[4,2,128]{2,1,0:T(2,128)S(1)} %pad_maximum_fusion.power_ref, f32[1,2048]{1,0:T(1,128)S(1)} %bitcast.11, f32[256,2048]{1,0:T(8,128)S(1)} %get-tuple-element.60.stream_ref, f32[256,2048]{1,0:T(8,128)} %get-tuple-element.61.stream_in), custom_call_target="tpu_custom_call", output_to_operand_aliasing={{1}: (3, {})} | custom-call | tf_op jit(solution)/shard_map/norm/pallas_call | solution.py:768
  (1 shorter events, 0.0 us)
Async XLA Ops:
  1.6 4.8 %copy-start = (f32[16,2048]{1,0:T(8,128)S(1)}, f32[16,2048]{1,0:T(8,128)}, u32[]{:S(2)}) copy-start(f32[16,2048]{1,0:T(8,128)} %rate_ref.9) | copy-start | bytes 393220
  1.6 9.4 %collective-permute-start = (bf16[3,2,2048]{2,1,0:T(2,128)(2,1)S(1)}, bf16[3,2,2048]{2,1,0:T(2,128)(2,1)S(1)}, u32[]{:S(2)}, u32[]{:S(2)}) collective-permute-start(bf16[3,2,2048]{2,1,0:T(2,128)(2,1)S(1)} %rims.1), channel_id=1, source_target_pairs={{0,4},{4,8},{8,12},{12,16},{16,20},{20,24},{24,28},{28,32},{32,36}... | collective-permute-start | bytes 73736 | tf_op jit(solution)/shard_map/ppermute | solution.py:587
  6.4 16.2 %copy-start.3 = (f32[16,2048]{1,0:T(8,128)S(1)}, f32[16,2048]{1,0:T(8,128)}, u32[]{:S(2)}) copy-start(f32[16,2048]{1,0:T(8,128)} %param.15) | copy-start | bytes 393220
  11.0 11.7 %copy-start.1 = (f32[2048]{0:T(1024)S(1)}, f32[2048]{0:T(1024)}, u32[]{:S(2)}) copy-start(f32[2048]{0:T(1024)} %param.16) | copy-start | bytes 24580
  11.8 21.1 %all-to-all-start = ((f32[64,4,128]{2,1,0:T(4,128)}), f32[64,4,128]{2,1,0:T(4,128)S(1)}, u32[]{:S(2)}, u32[]{:S(2)}) async-start(f32[64,4,128]{2,1,0:T(4,128)} %bitcast.13), calls=%async_computation | async-start | bytes 262144 | tf_op jit(solution)/shard_map/all_to_all | solution.py:680
  33.7 15.3 %all-to-all-start.1 = ((f32[64,4,128]{2,1,0:T(4,128)}), f32[64,4,128]{2,1,0:T(4,128)S(1)}, u32[]{:S(2)}, u32[]{:S(2)}) async-start(f32[64,4,128]{2,1,0:T(4,128)} %rank_scan.1), calls=%async_computation.1 | async-start | bytes 262144 | tf_op jit(solution)/shard_map/all_to_all | solution.py:733
  49.0 11.2 %copy-start.2 = (f32[2048]{0:T(1024)S(1)}, f32[2048]{0:T(1024)}, u32[]{:S(2)}) copy-start(f32[2048]{0:T(1024)} %param.17) | copy-start | bytes 24580
  52.7 4.5 %collective-permute-start.3 = (f32[2,128]{1,0:T(2,128)S(1)}, f32[2,128]{1,0:T(2,128)S(1)}, u32[]{:S(2)}, u32[]{:S(2)}) collective-permute-start(f32[2,128]{1,0:T(2,128)S(1)} %get-tuple-element.59), channel_id=1, source_target_pairs={{0,2},{1,3},{2,0},{3,1},{4,6},{5,7},{6,4},{7,5},{8,10},{9,11},{10,... | collective-permute-start | bytes 3080 | tf_op jit(solution)/shard_map/ppermute | solution.py:587
  55.7 2.4 %collective-permute-start.2 = (f32[2,128]{1,0:T(2,128)S(1)}, f32[2,128]{1,0:T(2,128)S(1)}, u32[]{:S(2)}, u32[]{:S(2)}) collective-permute-start(f32[2,128]{1,0:T(2,128)S(1)} %get-tuple-element.59), channel_id=1, source_target_pairs={{0,3},{1,0},{2,1},{3,2},{4,7},{5,4},{6,5},{7,6},{8,11},{9,8},{10,9... | collective-permute-start | bytes 3080 | tf_op jit(solution)/shard_map/ppermute | solution.py:587
  56.5 3.6 %collective-permute-start.1 = (f32[2,128]{1,0:T(2,128)S(1)}, f32[2,128]{1,0:T(2,128)S(1)}, u32[]{:S(2)}, u32[]{:S(2)}) collective-permute-start(f32[2,128]{1,0:T(2,128)S(1)} %get-tuple-element.59), channel_id=1, source_target_pairs={{0,1},{1,2},{2,3},{3,0},{4,5},{5,6},{6,7},{7,4},{8,9},{9,10},{10,1... | collective-permute-start | bytes 3080 | tf_op jit(solution)/shard_map/ppermute | solution.py:587
